TPU v7x, 256 devices: a whole 4x4x8 slice. The times are simulated.
256 devices in a mesh: ulysses: 4 (over x), blk: 32 (over z, y_lo, core), tensor: 2 (over y_hi).
Axes of the slice: x: 4, y: 4 (y_hi: 2, y_lo: 2; y = y_hi * 2 + y_lo), z: 8, core: 2. Of those that a mesh axis runs over, the one named last changes fastest.
Arguments:
- head_inputs: bfloat16 [6144, 3, 32, 128], P(('ulysses', 'blk'), None, 'tensor'), may hold values from -16 to 16
- positions: int32 [3, 6144], P(None, ('ulysses', 'blk')), may hold values from 0 to 51, as said below
- code_words: int32 [4096, 1280], P('tensor'), may hold values from 0 to 65535
- group_scales: bfloat16 [32, 5120], P('tensor'), may hold values from 0.0029907227 to 0.011962891
- out_gate: float32 [5120], P('tensor'), may hold values from 0.5 to 1.5
- out_bias: float32 [5120], P('tensor'), may hold values from -1 to 1
Outputs:
- branch_update: float32 [6144, 5120], P(('ulysses', 'blk'), 'tensor')
Inputs may be any that keep to these rules, and one draw needn't show every extreme that they name: `positions`: each token's latent frame, patch row and patch column; no two tokens share a cell of the 4 x 30 x 52 grid, and tokens stand in an arbitrary order.
All inputs are finite; a program needn't handle non-finite values.
Results may differ from a plain program's by a relative error of at most 0.012.
The roundings to bfloat16 on the way count: a program that leaves them out, or rounds other values in their place, can miss the bound.
Values may be sent and summed in bfloat16 or wider, within the bound.
No kernel may reach another device: no remote copies, remote signals or barrier semaphores. Data moves between devices by JAX's collectives and lax.ppermute only.
A program may use at most 128 MiB of HBM per device.

v0:
```python
import math

import jax
import jax.numpy as jnp
from jax import lax
from jax.sharding import PartitionSpec as P

GROUP = 128


def rope_tables(positions, width):
    pair_index = jnp.arange(width, dtype=jnp.int32) // 2
    frame_pairs = (width - 4 * (width // 6)) // 2
    side_pairs = width // 6
    segment = jnp.where(
        pair_index < frame_pairs, 0, jnp.where(pair_index < frame_pairs + side_pairs, 1, 2)
    )
    offset = jnp.where(
        segment == 0, 0, jnp.where(segment == 1, frame_pairs, frame_pairs + side_pairs)
    )
    within = (pair_index - offset).astype(jnp.float32)
    extent = jnp.where(segment == 0, frame_pairs, side_pairs).astype(jnp.float32)
    frequency = jnp.power(jnp.float32(10000.0), -within / extent)
    coords = positions.astype(jnp.float32)
    chosen = (
        coords[0][:, None] * (segment == 0).astype(jnp.float32)[None, :]
        + coords[1][:, None] * (segment == 1).astype(jnp.float32)[None, :]
        + coords[2][:, None] * (segment == 2).astype(jnp.float32)[None, :]
    )
    angles = chosen * frequency[None, :]
    return (jnp.cos(angles), jnp.sin(angles))


def pair_swap(width):
    source = lax.broadcasted_iota(jnp.int32, (width, width), 0)
    target = lax.broadcasted_iota(jnp.int32, (width, width), 1)
    is_even = target % 2 == 0
    return jnp.where(
        is_even & (source == target + 1),
        -1.0,
        jnp.where(~is_even & (source == target - 1), 1.0, 0.0),
    ).astype(jnp.float32)


def rotate(inputs, cosine, sine):
    width = inputs.shape[-1]
    turned = jnp.dot(
        inputs.reshape(-1, width), pair_swap(width), precision=lax.Precision.HIGHEST
    ).reshape(inputs.shape)
    return inputs * cosine[:, None, :] + turned * sine[:, None, :]


def dequantize(code_words, group_scales, group_rows):
    levels = jnp.concatenate(
        [
            jnp.bitwise_and(jnp.right_shift(code_words, 4 * shift_count), 15)
            for shift_count in range(4)
        ],
        axis=1,
    )
    levels = (levels - 8).astype(jnp.float32)
    spread_scales = jnp.repeat(group_scales.astype(jnp.float32), group_rows, axis=0)
    return (levels * spread_scales).astype(jnp.bfloat16)


def online_update(state, queries, key_block, value_block):
    running_max, running_sum, weighted = state
    scale_factor = 1.0 / math.sqrt(queries.shape[-1])
    scores = (
        jnp.einsum("qhd,khd->hqk", queries, key_block, preferred_element_type=jnp.float32)
        * scale_factor
    )
    new_max = jnp.maximum(running_max, jnp.max(scores, axis=2))
    correction = jnp.exp(running_max - new_max)
    lifted = jnp.exp(scores - new_max[:, :, None])
    running_sum = running_sum * correction + jnp.sum(lifted, axis=2)
    weighted = weighted * correction[:, :, None] + jnp.einsum(
        "hqk,khd->hqd", lifted.astype(jnp.bfloat16), value_block, preferred_element_type=jnp.float32
    )
    return (new_max, running_sum, weighted)


def fold_keys(state, queries, key_rows, value_rows):
    total_rows = key_rows.shape[0]
    block_width = 2048
    block_count = total_rows // block_width
    key_blocks = key_rows.reshape((block_count, block_width) + key_rows.shape[1:])
    value_blocks = value_rows.reshape((block_count, block_width) + value_rows.shape[1:])

    def advance(carried, blocks):
        return (online_update(carried, queries, blocks[0], blocks[1]), None)

    state, unused = lax.scan(advance, state, (key_blocks, value_blocks))
    return state


def body(head_inputs, positions, code_words, group_scales, out_gate, out_bias):
    local_heads = head_inputs.shape[2]
    head_width = head_inputs.shape[3]
    cosine, sine = rope_tables(positions, head_width)
    queries = rotate(head_inputs[:, 0].astype(jnp.float32), cosine, sine).astype(jnp.bfloat16)
    keys_local = rotate(head_inputs[:, 1].astype(jnp.float32), cosine, sine).astype(jnp.bfloat16)
    prepared = jnp.stack([queries, keys_local, head_inputs[:, 2]], axis=1)
    grouped = lax.all_to_all(prepared, "ulysses", split_axis=2, concat_axis=0, tiled=True)
    group_queries = grouped[:, 0]
    group_keys = grouped[:, 1]
    group_values = grouped[:, 2]
    query_rows = group_queries.shape[0]
    group_heads = group_queries.shape[1]
    start_state = (
        jnp.full((group_heads, query_rows), -1e30, jnp.float32),
        jnp.zeros((group_heads, query_rows), jnp.float32),
        jnp.zeros((group_heads, query_rows, head_width), jnp.float32),
    )
    every_keys, every_values = (
        lax.all_gather(group_keys, "blk", axis=0, tiled=True),
        lax.all_gather(group_values, "blk", axis=0, tiled=True),
    )
    final_state = fold_keys(start_state, group_queries, every_keys, every_values)
    running_max, running_sum, weighted = final_state
    attended = (weighted / running_sum[:, :, None]).astype(jnp.bfloat16)
    returned = lax.all_to_all(attended, "ulysses", split_axis=1, concat_axis=0, tiled=True)
    weight_table = dequantize(code_words, group_scales, GROUP).reshape(local_heads, head_width, -1)
    partial_sum = jnp.einsum(
        "htd,hdc->tc", returned, weight_table, preferred_element_type=jnp.float32
    )
    half_width = out_gate.shape[0]
    summed = lax.psum(partial_sum, "tensor")
    own_part = lax.dynamic_slice_in_dim(
        summed, lax.axis_index("tensor") * half_width, half_width, 1
    )
    return out_gate[None, :] * (own_part + out_bias[None, :])


def solution(mesh):
    placed = (
        P(("ulysses", "blk"), None, "tensor", None),
        P(None, ("ulysses", "blk")),
        P("tensor", None),
        P("tensor", None),
        P("tensor"),
        P("tensor"),
    )
    return jax.shard_map(
        body, mesh=mesh, in_specs=placed, out_specs=P(("ulysses", "blk"), "tensor"), check_vma=False
    )
```

profile of v0, /device:TPU:6, one launch (start us, length us, event | category | flops | bytes accessed | tf_op | source)
XLA Modules:
  0.0 311.3 jit_solution(14568742590634218589)
XLA Ops:
  6.5 0.0 all-gather.5.cloned.1.call-start
  6.6 1.2 fusion.69
  7.8 0.4 convolution_bitcast_fusion.1
  8.2 0.2 copy.21
  8.4 0.4 convolution_bitcast_fusion
  8.8 0.2 copy.23
  8.9 0.7 convert_element_type.72
  9.6 0.2 fusion.52
  9.8 1.2 add_convert_fusion.1
  11.0 0.1 pad_maximum_fusion
  11.1 0.2 copy.25
  11.2 12.7 %all_to_all.36 = bf16[48,3,16,128]{3,0,1,2:T(8,128)(2,1)S(1)} all-to-all(bf16[48,3,16,128]{3,0,1,2:T(8,128)(2,1)S(1)} %copy.25), channel_id=1, replica_groups=mesh['ulysses'=4,'blk'=32,'tensor'=2] {'ulysses'}, dimensions={2} | all-to-all | bytes 1179648 | tf_op jit(solution)/shard_map/all_to_all | solution.py:104
  23.9 0.1 copy.26
  24.0 0.8 fusion.68
  24.8 0.0 all-gather.5.cloned.1.call-update
  24.8 0.0 all-gather.7.cloned.1.call-start
  24.8 0.7 all-gather.7.cloned.1.call-update
  25.6 72.3 %all-gather.5.cloned.1.call-done = bf16[6144,1,4,128]{3,0,2,1:T(8,128)(2,1)} async-done(((bf16[192,1,4,128]{3,0,2,1:T(8,128)(2,1)}), bf16[6144,1,4,128]{3,0,2,1:T(8,128)(2,1)}) %all-gather.5.cloned.1.call-update) | async-done | bytes 6291472 | tf_op jit(solution)/shard_map/all_gather | solution.py:116
  97.8 72.0 %all-gather.7.cloned.1.call-done = bf16[6144,1,4,128]{3,0,2,1:T(8,128)(2,1)} async-done(((bf16[192,1,4,128]{3,0,2,1:T(8,128)(2,1)}), bf16[6144,1,4,128]{3,0,2,1:T(8,128)(2,1)}) %all-gather.7.cloned.1.call-update) | async-done | bytes 6291472 | tf_op jit(solution)/shard_map/all_gather | solution.py:117
  169.9 42.0 %while.15 = (s32[]{:T(128)}, f32[4,192]{1,0:T(4,128)S(1)}, f32[4,192]{1,0:T(4,128)S(1)}, f32[4,192,128]{2,1,0:T(8,128)S(1)}, bf16[3,2048,4,128]{3,1,0,2:T(8,128)...) while((s32[]{:T(128)}, f32[4,192]{1,0:T(4,128)S(1)}, ...), condition=%wide.region_3.4_spmd.clone, body=%wide.region_0.3_spmd.clone.sunk | while | flops 818188032 | bytes 24101992 | solution.py:93
  169.9 5.2 %bitcast_reduce_fusion.2 = (f32[4,192]{1,0:T(4,128)S(1)}, f32[4,2048,192]{1,2,0:T(8,128)}) fusion(bf16[192,4,128]{2,0,1:T(8,128)(2,1)S(1)} %get-tuple-element.198, bf16[3,2048,4,128]{3,1,0,2:T(8,128)(2,1)} %get-tuple-element.197, s32[]{:T(128)} %get-tuple-element.184), kind=kOutput, calls=%fused_computation.1.clone.1 | convolution fusion | flops 405798144 | bytes 8588800 | tf_op jit(solution)/shard_map/while/body/eval_jaxpr/qhd,khd->hqk/dot_general | solution.py:70
  175.0 3.9 %fusion.83 = f32[4,192]{1,0:T(4,128)S(1)} fusion(f32[4,2048,192]{1,2,0:T(8,128)} %get-tuple-element.172, f32[4,192]{1,0:T(4,128)S(1)} %select_maximum_fusion.2), kind=kLoop, calls=%fused_computation.4.clone.1 | loop fusion | flops 4717824 | bytes 6297600 | tf_op jit(solution)/shard_map/while/body/eval_jaxpr/reduce_sum | solution.py:76
  179.0 4.8 %fusion.85 = f32[4,192,128]{2,1,0:T(8,128)S(1)} fusion(bf16[3,2048,4,128]{3,1,0,2:T(8,128)(2,1)} %get-tuple-element.199, s32[]{:T(128)} %get-tuple-element.184, f32[4,2048,192]{1,2,0:T(8,128)} %get-tuple-element.172, f32[4,192]{1,0:T(4,128)S(1)} %select_maximum_fusion.2, f32[4,192,128]{2,1,0:T(8,128)S(1)} %get-tuple-element.187, ...), kind=kOutput, calls=%fused_computation.13.clone.1 | convolution fusion | flops 407666688 | bytes 9181697 | tf_op jit(solution)/shard_map/while/body/eval_jaxpr/hqk,khd->hqd/dot_general | solution.py:77
  183.9 5.2 %bitcast_reduce_fusion.2 = (f32[4,192]{1,0:T(4,128)S(1)}, f32[4,2048,192]{1,2,0:T(8,128)}) fusion(bf16[192,4,128]{2,0,1:T(8,128)(2,1)S(1)} %get-tuple-element.198, bf16[3,2048,4,128]{3,1,0,2:T(8,128)(2,1)} %get-tuple-element.197, s32[]{:T(128)} %get-tuple-element.184), kind=kOutput, calls=%fused_computation.1.clone.1 | convolution fusion | flops 405798144 | bytes 8588800 | tf_op jit(solution)/shard_map/while/body/eval_jaxpr/qhd,khd->hqk/dot_general | solution.py:70
  189.0 3.9 %fusion.83 = f32[4,192]{1,0:T(4,128)S(1)} fusion(f32[4,2048,192]{1,2,0:T(8,128)} %get-tuple-element.172, f32[4,192]{1,0:T(4,128)S(1)} %select_maximum_fusion.2), kind=kLoop, calls=%fused_computation.4.clone.1 | loop fusion | flops 4717824 | bytes 6297600 | tf_op jit(solution)/shard_map/while/body/eval_jaxpr/reduce_sum | solution.py:76
  193.0 4.8 %fusion.85 = f32[4,192,128]{2,1,0:T(8,128)S(1)} fusion(bf16[3,2048,4,128]{3,1,0,2:T(8,128)(2,1)} %get-tuple-element.199, s32[]{:T(128)} %get-tuple-element.184, f32[4,2048,192]{1,2,0:T(8,128)} %get-tuple-element.172, f32[4,192]{1,0:T(4,128)S(1)} %select_maximum_fusion.2, f32[4,192,128]{2,1,0:T(8,128)S(1)} %get-tuple-element.187, ...), kind=kOutput, calls=%fused_computation.13.clone.1 | convolution fusion | flops 407666688 | bytes 9181697 | tf_op jit(solution)/shard_map/while/body/eval_jaxpr/hqk,khd->hqd/dot_general | solution.py:77
  197.9 5.2 %bitcast_reduce_fusion.2 = (f32[4,192]{1,0:T(4,128)S(1)}, f32[4,2048,192]{1,2,0:T(8,128)}) fusion(bf16[192,4,128]{2,0,1:T(8,128)(2,1)S(1)} %get-tuple-element.198, bf16[3,2048,4,128]{3,1,0,2:T(8,128)(2,1)} %get-tuple-element.197, s32[]{:T(128)} %get-tuple-element.184), kind=kOutput, calls=%fused_computation.1.clone.1 | convolution fusion | flops 405798144 | bytes 8588800 | tf_op jit(solution)/shard_map/while/body/eval_jaxpr/qhd,khd->hqk/dot_general | solution.py:70
  203.1 3.9 %fusion.83 = f32[4,192]{1,0:T(4,128)S(1)} fusion(f32[4,2048,192]{1,2,0:T(8,128)} %get-tuple-element.172, f32[4,192]{1,0:T(4,128)S(1)} %select_maximum_fusion.2), kind=kLoop, calls=%fused_computation.4.clone.1 | loop fusion | flops 4717824 | bytes 6297600 | tf_op jit(solution)/shard_map/while/body/eval_jaxpr/reduce_sum | solution.py:76
  207.0 4.8 %fusion.85 = f32[4,192,128]{2,1,0:T(8,128)S(1)} fusion(bf16[3,2048,4,128]{3,1,0,2:T(8,128)(2,1)} %get-tuple-element.199, s32[]{:T(128)} %get-tuple-element.184, f32[4,2048,192]{1,2,0:T(8,128)} %get-tuple-element.172, f32[4,192]{1,0:T(4,128)S(1)} %select_maximum_fusion.2, f32[4,192,128]{2,1,0:T(8,128)S(1)} %get-tuple-element.187, ...), kind=kOutput, calls=%fused_computation.13.clone.1 | convolution fusion | flops 407666688 | bytes 9181697 | tf_op jit(solution)/shard_map/while/body/eval_jaxpr/hqk,khd->hqd/dot_general | solution.py:77
  211.9 0.1 copy.29
  212.0 1.0 fusion.29
  213.0 4.8 %all-to-all-start.1 = ((bf16[4,192,128]{2,0,1:T(4,128)(2,1)}), bf16[4,192,128]{2,0,1:T(4,128)(2,1)S(1)}, u32[]{:S(2)}, u32[]{:S(2)}) async-start(bf16[4,192,128]{2,0,1:T(4,128)(2,1)} %fusion.29), calls=%async_computation.1 | async-start | bytes 393216 | tf_op jit(solution)/shard_map/all_to_all | solution.py:122
  217.8 0.0 copy-start
  217.8 0.0 all-reduce.2.cloned.1.call-start
  217.9 17.3 %shift-right-arithmetic_and_fusion.3 = (s32[2048,1280]{1,0:T(8,128)}, s32[2048,1280]{1,0:T(8,128)}, s32[2048,1280]{1,0:T(8,128)}, s32[2048,1280]{1,0:T(8,128)}) fusion(s32[2048,1280]{1,0:T(8,128)} %param.10), kind=kLoop, calls=%fused_computation.30 | loop fusion | flops 20971520 | bytes 52428800 | tf_op jit(solution)/shard_map/and | solution.py:56
  235.1 0.0 copy-done
  235.2 0.0 all-to-all-done.1
  235.2 0.0 copy-start.1
  235.2 0.0 copy-start.2
  235.2 15.8 %fusion.26 = f32[48,5120]{1,0:T(8,128)} fusion(bf16[16,48,128]{2,1,0:T(8,128)(2,1)S(1)} %bitcast.95, s32[16,128,1280]{2,1,0:T(8,128)} %bitcast.86, s32[16,128,1280]{2,1,0:T(8,128)} %bitcast.87, s32[16,128,1280]{2,1,0:T(8,128)} %bitcast.85, s32[16,128,1280]{2,1,0:T(8,128)} %bitcast.84, f32[16,5120]{1,0:T(8,128)S(1)} %convert_element_type.83), kind=kOutput, calls=%fused_computation.31 | convolution fusion | flops 1080033280 | bytes 43450368 | tf_op jit(solution)/shard_map/htd,hdc->tc/dot_general | solution.py:124
  251.0 0.0 all-reduce.2.cloned.1.call-update
  251.0 51.9 %all-reduce.2.cloned.1.call-done = f32[48,5120]{1,0:T(8,128)} async-done(((f32[48,5120]{1,0:T(8,128)}), f32[48,5120]{1,0:T(8,128)}) %all-reduce.2.cloned.1.call-update) | async-done | bytes 983056 | tf_op jit(solution)/shard_map/psum | solution.py:128
  302.9 0.0 copy-done.1
  302.9 0.0 copy-done.2
  302.9 1.9 add_multiply_fusion
  (21 shorter events, 0.2 us)
Async XLA Ops:
  6.5 91.3 %all-gather.5.cloned.1.call-start = ((), (), s32[]{:S(2)}) async-start(), calls=%async_computation.3 | async-start | bytes 6488064 | tf_op jit(solution)/shard_map/all_gather | solution.py:116
  24.8 145.1 %all-gather.7.cloned.1.call-start = ((), (), s32[]{:S(2)}) async-start(), calls=%async_computation.4 | async-start | bytes 6488064 | tf_op jit(solution)/shard_map/all_gather | solution.py:117
  213.0 22.1 %all-to-all-start.1 = ((bf16[4,192,128]{2,0,1:T(4,128)(2,1)}), bf16[4,192,128]{2,0,1:T(4,128)(2,1)S(1)}, u32[]{:S(2)}, u32[]{:S(2)}) async-start(bf16[4,192,128]{2,0,1:T(4,128)(2,1)} %fusion.29), calls=%async_computation.1 | async-start | bytes 393216 | tf_op jit(solution)/shard_map/all_to_all | solution.py:122
  217.8 17.3 %copy-start = (bf16[16,5120]{1,0:T(8,128)(2,1)S(1)}, bf16[16,5120]{1,0:T(8,128)(2,1)}, u32[]{:S(2)}) copy-start(bf16[16,5120]{1,0:T(8,128)(2,1)} %param.11) | copy-start | bytes 491524
  217.8 85.1 %all-reduce.2.cloned.1.call-start = ((), (), s32[]{:S(2)}) async-start(), calls=%async_computation.2 | async-start | bytes 1966080 | tf_op jit(solution)/shard_map/psum | solution.py:128
  235.2 67.7 %copy-start.1 = (f32[2560]{0:T(1024)S(1)}, f32[2560]{0:T(1024)}, u32[]{:S(2)}) copy-start(f32[2560]{0:T(1024)} %param.13) | copy-start | bytes 30724
  235.2 67.7 %copy-start.2 = (f32[2560]{0:T(1024)S(1)}, f32[2560]{0:T(1024)}, u32[]{:S(2)}) copy-start(f32[2560]{0:T(1024)} %param.12) | copy-start | bytes 30724
Sparse Core Ops, SparseCore 0:
  24.9 72.8 all-gather.4
  99.6 70.1 all-gather.6
  251.2 51.7 all-reduce.1
where the time goes:
time: 313 us; the launch traced here: 311 us
  waiting for transfers between devices  197 us (63%)
  matrix products  46.6 us (15%)
  other arithmetic  34.2 us (11%)
  between operations  13.3 us (4%)
  blocking collectives  12.7 us (4%)
  starting transfers between devices  4.85 us (2%)
    all_gather x1, waiting for transfers between devices, body(): lax.all_gather(group_keys, 'blk', axis=0, tiled=True)  72.3 us
    all_gather x1, waiting for transfers between devices, body(): lax.all_gather(group_values, 'blk', axis=0, tiled=True)  72 us
    psum x1, waiting for transfers between devices, body(): summed = lax.psum(partial_sum, 'tensor')  51.9 us
    and x1, other arithmetic, dequantize(): jnp.bitwise_and(jnp.right_shift(code_words, 4 * shift_count), 15)  17.3 us
    dot_general x1, matrix products, body(): jnp.einsum('htd,hdc->tc', returned, weight_table, preferred_element_type=...  15.8 us
    dot_general x3, matrix products, online_update(): jnp.einsum('qhd,khd->hqk', queries, key_block, preferred_element_type=jnp...  15.5 us
    dot_general x3, matrix products, online_update(): jnp.einsum('hqk,khd->hqd', lifted.astype(jnp.bfloat16), value_block, pref...  14.5 us
    all_to_all x1, blocking collectives, body(): lax.all_to_all(prepared, 'ulysses', split_axis=2, concat_axis=0, tiled=True)  12.7 us
  transfers between devices with their start and end apart: 4, of which 3 were waited for; matrix products, arithmetic and copies ran while one was open for 6% of the time, Pallas kernels for 0%

commit v1 on v0

v1 whole, which is shorter than its diff:
```python
import functools
import math

import jax
import jax.numpy as jnp
import numpy as np
from jax import lax
from jax.experimental import pallas as pl
from jax.experimental.pallas import tpu as pltpu
from jax.sharding import Mesh
from jax.sharding import PartitionSpec as P

HD = 128
LOG2E = 1.4426950408889634
F32 = jnp.float32
BF16 = jnp.bfloat16


def frequency_table(width):
    pair = np.arange(width) // 2
    frame = (width - 4 * (width // 6)) // 2
    side = width // 6
    segment = np.where(pair < frame, 0, np.where(pair < frame + side, 1, 2))
    start = np.where(segment == 0, 0, np.where(segment == 1, frame, frame + side))
    extent = np.where(segment == 0, frame, side)
    value = np.power(10000.0, -(pair - start) / extent)
    return np.stack([np.where(segment == s, value, 0.0) for s in range(3)]).astype(np.float32)


def rotate_kernel(pos_ref, freq_ref, x_ref, out_ref, wide):
    tokens, kinds, heads, width = x_ref.shape
    pos = pos_ref[...].astype(F32)
    freq = freq_ref[...]
    angles = pos[:, 0:1] * freq[0:1, :] + pos[:, 1:2] * freq[1:2, :] + pos[:, 2:3] * freq[2:3, :]
    cosine = jnp.cos(angles)
    sine = jnp.sin(angles)
    lane = lax.broadcasted_iota(jnp.int32, (tokens, width), 1)
    is_even = lane % 2 == 0
    sine_even = jnp.where(is_even, -sine, 0.0)
    sine_odd = jnp.where(is_even, 0.0, sine)
    wide[...] = x_ref[...].astype(F32).reshape(tokens * kinds * heads, width)
    for kind in range(kinds):
        for head in range(heads):
            x = wide[pl.ds(kind * heads + head, tokens, stride=kinds * heads), :]
            if kind < 2:
                right = pltpu.roll(x, 1, 1)
                left = pltpu.roll(x, width - 1, 1)
                x = x * cosine + (left * sine_even + right * sine_odd)
            out_ref[head, kind] = x.astype(BF16)


def rotate(positions, head_inputs):
    tokens, kinds, heads, width = head_inputs.shape
    return pl.pallas_call(
        rotate_kernel,
        out_shape=jax.ShapeDtypeStruct((heads, kinds, tokens, width), BF16),
        scratch_shapes=[pltpu.VMEM((tokens * kinds * heads, width), F32)],
        compiler_params=pltpu.CompilerParams(vmem_limit_bytes=16 * 1024 * 1024),
    )(positions.T, jnp.asarray(frequency_table(width)), head_inputs)


def dequantize_kernel(half_ref, words_ref, scales_ref, out_ref):
    half = half_ref[0]
    quarter = words_ref.shape[1]
    words = words_ref[...]
    for part in range(2):
        mine = half if part else 1 - half
        shifted = lax.shift_right_logical(words, jnp.full(words.shape, 8 * mine, jnp.int32))
        for low in range(2):
            scale = scales_ref[0, pl.ds(2 * mine + low, 1), :]
            if low:
                level = ((shifted & 240) - 128).astype(F32) * (scale * 0.0625)
            else:
                level = ((shifted & 15) - 8).astype(F32) * scale
            out_ref[part, :, low * quarter : (low + 1) * quarter] = level.astype(BF16)


def dequantize(half, code_words, group_scales):
    rows, quarter = code_words.shape
    groups = group_scales.shape[0]
    depth = rows // groups
    scales = group_scales.astype(F32).reshape(groups, 4, quarter)
    return pl.pallas_call(
        dequantize_kernel,
        grid=(groups,),
        in_specs=[
            pl.BlockSpec(memory_space=pltpu.SMEM),
            pl.BlockSpec((depth, quarter), lambda g: (g, 0)),
            pl.BlockSpec((1, 4, quarter), lambda g: (g, 0, 0)),
        ],
        out_specs=pl.BlockSpec((2, depth, 2 * quarter), lambda g: (0, g, 0)),
        out_shape=jax.ShapeDtypeStruct((2, rows, 2 * quarter), BF16),
        compiler_params=pltpu.CompilerParams(vmem_limit_bytes=24 * 1024 * 1024),
        cost_estimate=pl.CostEstimate(flops=rows * quarter * 30, bytes_accessed=rows * quarter * 12, transcendentals=0),
    )(half, code_words, scales)


def attend_kernel(first, last, blocks, tile, q_ref, *refs):
    kv_refs = refs[:blocks]
    refs = refs[blocks:]
    if not first:
        m_in, l_in, acc_in = refs[:3]
        refs = refs[3:]
    scale = LOG2E / math.sqrt(HD)
    groups, _, rows, width = q_ref.shape
    total = groups * rows
    queries = q_ref[:, 0].reshape(total, width)
    keys, values = [], []
    for ref in kv_refs:
        at = ref.shape[1] - 2
        keys.append(ref[:, at].reshape(total, width))
        values.append(ref[:, at + 1].reshape(total, width))

    def scores(step):
        row, block = divmod(step, blocks)
        return lax.dot_general(
            queries[row * tile : (row + 1) * tile],
            keys[block],
            (((1,), (1,)), ((), ())),
            preferred_element_type=F32,
        )

    steps = (total // tile) * blocks
    ahead = scores(0)
    for step in range(steps):
        row, block = divmod(step, blocks)
        here = slice(row * tile, (row + 1) * tile)
        s = ahead
        if step + 1 < steps:
            ahead = scores(step + 1)
        fresh = first and block == 0
        if block == 0 and not first:
            peak, total_l, acc = m_in[here, :], l_in[here, :], acc_in[here, :]
        s_peak = jnp.broadcast_to(jnp.max(s, axis=1, keepdims=True), (tile, width))
        new_peak = s_peak if fresh else jnp.maximum(peak, s_peak)
        parts, part_sum = [], None
        for lane in range(total // width):
            lifted = jnp.exp2((s[:, lane * width : (lane + 1) * width] - new_peak) * scale)
            part_sum = lifted if part_sum is None else part_sum + lifted
            parts.append(lifted.astype(BF16))
        mixed = jnp.dot(jnp.concatenate(parts, axis=1), values[block], preferred_element_type=F32)
        if fresh:
            total_l, acc = part_sum, mixed
        else:
            fade = jnp.exp2((peak - new_peak) * scale)
            total_l = total_l * fade + part_sum
            acc = acc * fade + mixed
        peak = new_peak
        if block == blocks - 1:
            if last:
                (out_ref,) = refs
                whole = jnp.sum(total_l, axis=1, keepdims=True)
                out_ref[here, :] = (acc / whole).astype(BF16)
            else:
                m_out, l_out, acc_out = refs
                m_out[here, :] = peak
                l_out[here, :] = total_l
                acc_out[here, :] = acc


def attend(queries, kv_blocks, state, last, tile=128):
    groups, _, rows, width = queries.shape
    total = groups * rows
    blocks = len(kv_blocks)
    first = state is None
    carried = jax.ShapeDtypeStruct((total, width), F32)
    out_shape = jax.ShapeDtypeStruct((total, width), BF16) if last else (carried,) * 3
    pairs = total * total * blocks
    return pl.pallas_call(
        functools.partial(attend_kernel, first, last, blocks, tile),
        out_shape=out_shape,
        compiler_params=pltpu.CompilerParams(vmem_limit_bytes=32 * 1024 * 1024),
        cost_estimate=pl.CostEstimate(
            flops=pairs * width * 4, bytes_accessed=total * width * 2 * (2 * blocks + 7), transcendentals=pairs
        ),
    )(queries, *kv_blocks, *(() if first else state))


def project_kernel(x_ref, w_ref, out_ref):
    heads = x_ref.shape[0]
    x = jnp.concatenate([x_ref[h] for h in range(heads)], axis=1)
    out_ref[...] = jnp.dot(x, w_ref[0], preferred_element_type=F32).astype(out_ref.dtype)


def project(part, returned, weights, out_type, tile=512):
    heads, tokens, width = returned.shape
    _, rows, columns = weights.shape
    return pl.pallas_call(
        project_kernel,
        grid=(columns // tile,),
        in_specs=[
            pl.BlockSpec((heads, tokens, width), lambda c: (0, 0, 0)),
            pl.BlockSpec((1, rows, tile), lambda c: (part, 0, c)),
        ],
        out_specs=pl.BlockSpec((tokens, tile), lambda c: (0, c)),
        out_shape=jax.ShapeDtypeStruct((tokens, columns), out_type),
        compiler_params=pltpu.CompilerParams(vmem_limit_bytes=24 * 1024 * 1024),
        cost_estimate=pl.CostEstimate(
            flops=2 * tokens * rows * columns, bytes_accessed=rows * columns * 2, transcendentals=0
        ),
    )(returned, weights)


HEAD_AXES = ("x", "zl", "yl")


def body(head_inputs, positions, code_words, group_scales, out_gate, out_bias):
    ring = lax.axis_size("zh")
    half = lax.axis_index("yh").astype(jnp.int32).reshape(1)
    prepared = rotate(positions, head_inputs)
    grouped = lax.all_to_all(prepared, HEAD_AXES, split_axis=0, concat_axis=0, tiled=True)
    own = grouped[:, 1:]

    def swap(a):
        return lax.ppermute(a, "c", [(0, 1), (1, 0)])

    up = lax.ppermute(own, "zh", [(i, (i + 1) % ring) for i in range(ring)])
    down = lax.ppermute(own, "zh", [(i, (i - 1) % ring) for i in range(ring)])
    beside = swap(own)
    weights = dequantize(half, code_words, group_scales)
    state = attend(grouped, [grouped, beside], None, False)
    core = lax.axis_index("c")
    onward = jnp.where(core == 0, up, down)
    hops = []
    for i in range(ring):
        hops.append((2 * i, 2 * ((i + 1) % ring)))
        hops.append((2 * i + 1, 2 * ((i - 1) % ring) + 1))
    far = lax.ppermute(onward, ("zh", "c"), hops)
    up_beside, down_beside = swap(up), swap(down)
    state = attend(grouped, [up, down], state, False)
    state = attend(grouped, [up_beside, down_beside], state, False)
    far_beside = swap(far)
    attended = attend(grouped, [far, far_beside], state, True)
    chunks = prepared.shape[0]
    returned = lax.all_to_all(
        attended.reshape(chunks, -1, HD), HEAD_AXES, split_axis=0, concat_axis=0, tiled=True
    )
    outgoing = project(0, returned, weights, BF16)
    incoming = lax.ppermute(outgoing, "yh", [(0, 1), (1, 0)])
    kept = project(1, returned, weights, F32)
    return out_gate[None, :] * (kept + incoming.astype(F32) + out_bias[None, :])


def solution(mesh):
    x, blk, yh = mesh.devices.shape
    fine = Mesh(mesh.devices.reshape(x, blk // 8, 2, 2, 2, yh), ("x", "zh", "zl", "yl", "c", "yh"))
    tokens = ("x", "zh", "zl", "yl", "c")
    placed = (
        P(tokens, None, "yh", None),
        P(None, tokens),
        P("yh", None),
        P("yh", None),
        P("yh"),
        P("yh"),
    )
    return jax.shard_map(
        body, mesh=fine, in_specs=placed, out_specs=P(tokens, "yh"), check_vma=False
    )
```

time: 313 us -> 114 us (0.36)
  waiting for transfers between devices: 197 us -> 36.1 us
  matrix products: 46.6 us -> 0 us
  other arithmetic: 34.2 us -> 0.89 us
  Pallas kernels: 0 us -> 29 us
  between operations: 13.3 us -> 0.12 us
  local copies, waits for them, and re-layouts: 2.71 us -> 14.5 us
  starting transfers between devices: 4.85 us -> 15.1 us
  blocking collectives: 12.7 us -> 16.8 us
    all_gather x2 -> x0, waiting for transfers between devices: 144 us -> none  [the longest x1 72.3 us: body(): lax.all_gather(group_keys, 'blk', axis=0, tiled=True)]
    psum x1 -> x0, waiting for transfers between devices: 51.9 us -> none  [body(): summed = lax.psum(partial_sum, 'tensor')]
    dot_general x9 -> x0, matrix products: 46.6 us -> none  [the longest x1 15.8 us: body(): jnp.einsum('htd,hdc->tc', returned, weight_table, preferred_element_type=...]
    ppermute x0 -> x8, waiting for transfers between devices: none -> 36.1 us  [the longest x1 14.3 us: body(): down = lax.ppermute(own, 'zh', [(i, (i - 1) % ring) for i in range(ring)])]
    pallas_call x0 -> x8, Pallas kernels: none -> 29 us  [the longest x1 12.6 us: dequantize(): pl.pallas_call(dequantize_kernel, grid=(groups,), in_specs=[pl.BlockSpec(...]
    and x2 -> x0, other arithmetic: 17.3 us -> none  [the longest x1 17.3 us: dequantize(): jnp.bitwise_and(jnp.right_shift(code_words, 4 * shift_count), 15)]
    unnamed x6 -> x13, local copies, waits for them, and re-layouts: 0.02 us -> 13.5 us
    reduce_sum x3 -> x0, other arithmetic: 11.8 us -> none  [online_update(): running_sum = running_sum * correction + jnp.sum(lifted, axis=2)]
  transfers between devices with their start and end apart: 4 -> 9, of which waited for: 3 -> 4; matrix products, arithmetic and copies ran while one was open for 6% -> 1% of each run, Pallas kernels for 0% -> 20%
where the time goes in v1:
time: 114 us; the launch traced here: 113 us
  waiting for transfers between devices  36.1 us (32%)
  Pallas kernels  29 us (25%)
  blocking collectives  16.8 us (15%)
  starting transfers between devices  15.1 us (13%)
  local copies, waits for them, and re-layouts  14.5 us (13%)
    all_to_all x1, blocking collectives, body(): lax.all_to_all(prepared, HEAD_AXES, split_axis=0, concat_axis=0, tiled=True)  16.8 us
    ppermute x1, waiting for transfers between devices, body(): down = lax.ppermute(own, 'zh', [(i, (i - 1) % ring) for i in range(ring)])  14.3 us
    unnamed x13, local copies, waits for them, and re-layouts  13.5 us
    ppermute x1, waiting for transfers between devices, body(): far = lax.ppermute(onward, ('zh', 'c'), hops)  13.4 us
    pallas_call x1, Pallas kernels, dequantize(): pl.pallas_call(dequantize_kernel, grid=(groups,), in_specs=[pl.BlockSpec(...  12.6 us
    pallas_call x4, Pallas kernels, attend(): pl.pallas_call(functools.partial(attend_kernel, first, last, blocks, tile...  9.43 us
    pallas_call x2, Pallas kernels, project(): pl.pallas_call(project_kernel, grid=(columns // tile,), in_specs=[pl.Bloc...  6.27 us
    all_to_all x1, starting transfers between devices, body(): lax.all_to_all(attended.reshape(chunks, -1, HD), HEAD_AXES, split_axis=0,...  5.88 us
  transfers between devices with their start and end apart: 9, of which 4 were waited for; matrix products, arithmetic and copies ran while one was open for 1% of the time, Pallas kernels for 20%

profile of v1, /device:TPU:6, one launch (start us, length us, event | category | flops | bytes accessed | tf_op | source)
XLA Modules:
  0.0 112.6 jit_solution(11878989171112072824)
XLA Ops:
  0.0 0.8 copy.8
  0.8 0.0 copy-start.2
  0.8 1.1 copy-done.2
  1.8 0.0 copy-start.3
  1.8 0.7 copy-done.3
  2.5 0.7 shard_map.73
  3.2 16.8 %all_to_all.10.q_ref.refs_0_ = bf16[16,3,48,128]{3,2,1,0:T(8,128)(2,1)S(1)} all-to-all(bf16[16,3,48,128]{3,2,1,0:T(8,128)(2,1)S(1)} %shard_map.73), channel_id=1, replica_groups=mesh['x'=4,'zh'=4,'zl'=2,'yl'=2,'c'=2,'yh'=2] {'x','zl','yl'}, dimensions={0} | all-to-all | bytes 1179648 | tf_op jit(solution)/shard_map/all_to_all | solution.py:211
  20.0 5.5 %collective-permute-start.1 = (bf16[16,2,48,128]{3,2,1,0:T(8,128)(2,1)S(1)}, bf16[16,2,48,128]{3,2,1,0:T(8,128)(2,1)S(1)}, u32[]{:S(2)}, u32[]{:S(2)}) collective-permute-start(bf16[16,2,48,128]{3,2,1,0:T(8,128)(2,1)S(1)} %slice.4), channel_id=1, source_target_pairs={{0,48},{16,0},{32,16},{48,32},{1,49},{17,1},{33,17},{49,33},{2,50}... | collective-permute-start | bytes 1179656 | tf_op jit(solution)/shard_map/ppermute | solution.py:218
  25.5 0.0 collective-permute-start
  25.5 14.3 %collective-permute-done.1.refs_1_ = bf16[16,2,48,128]{3,2,1,0:T(8,128)(2,1)S(1)} collective-permute-done((bf16[16,2,48,128]{3,2,1,0:T(8,128)(2,1)S(1)}, bf16[16,2,48,128]{3,2,1,0:T(8,128)(2,1)S(1)}, u32[]{:S(2)}, u32[]{:S(2)}) %collective-permute-start.1) | collective-permute-done | bytes 393248 | tf_op jit(solution)/shard_map/ppermute | solution.py:218
  39.8 4.9 %collective-permute-done.refs_0_ = bf16[16,2,48,128]{3,2,1,0:T(8,128)(2,1)S(1)} collective-permute-done((bf16[16,2,48,128]{3,2,1,0:T(8,128)(2,1)S(1)}, bf16[16,2,48,128]{3,2,1,0:T(8,128)(2,1)S(1)}, u32[]{:S(2)}, u32[]{:S(2)}) %collective-permute-start) | collective-permute-done | bytes 393248 | tf_op jit(solution)/shard_map/ppermute | solution.py:217
  44.7 0.1 collective-permute-start.2
  44.8 0.1 collective-permute-start.6
  44.9 0.5 collective-permute-start.5
  45.4 0.1 collective-permute-start.4
  45.5 13.4 %collective-permute-done.2.refs_0_ = bf16[16,2,48,128]{3,2,1,0:T(8,128)(2,1)S(1)} collective-permute-done((bf16[16,2,48,128]{3,2,1,0:T(8,128)(2,1)S(1)}, bf16[16,2,48,128]{3,2,1,0:T(8,128)(2,1)S(1)}, u32[]{:S(2)}, u32[]{:S(2)}) %collective-permute-start.2) | collective-permute-done | bytes 393248 | tf_op jit(solution)/shard_map/ppermute | solution.py:228
  58.8 0.0 collective-permute-start.3
  58.9 0.0 collective-permute-done.6.refs_1_
  58.9 2.2 %shard_map.74 = (f32[768,128]{1,0:T(8,128)S(1)}, f32[768,128]{1,0:T(8,128)S(1)}, f32[768,128]{1,0:T(8,128)S(1)}) custom-call(bf16[16,3,48,128]{3,2,1,0:T(8,128)(2,1)S(1)} %all_to_all.10.q_ref.refs_0_, bf16[16,3,48,128]{3,2,1,0:T(8,128)(2,1)S(1)} %all_to_all.10.q_ref.refs_0_, bf16[16,2,48,128]{3,2,1,0:T(8,128)(2,1)S(1)} %collective-permute-done.6.refs_1_), custom_call_target="tpu_custom_call" | custom-call | flops 603979776 | bytes 2162688 | tf_op jit(solution)/shard_map/pallas_call | solution.py:169
  61.1 2.2 %shard_map.75 = (f32[768,128]{1,0:T(8,128)S(1)}, f32[768,128]{1,0:T(8,128)S(1)}, f32[768,128]{1,0:T(8,128)S(1)}) custom-call(bf16[16,3,48,128]{3,2,1,0:T(8,128)(2,1)S(1)} %all_to_all.10.q_ref.refs_0_, bf16[16,2,48,128]{3,2,1,0:T(8,128)(2,1)S(1)} %collective-permute-done.refs_0_, bf16[16,2,48,128]{3,2,1,0:T(8,128)(2,1)S(1)} %collective-permute-done.1.refs_1_, ...), custom_call_target="tpu_custom_call" | custom-call | flops 603979776 | bytes 2162688 | tf_op jit(solution)/shard_map/pallas_call | solution.py:169
  63.2 0.0 collective-permute-done.5.refs_1_
  63.2 0.0 collective-permute-done.4.refs_0_
  63.3 2.2 %shard_map.76 = (f32[768,128]{1,0:T(8,128)S(1)}, f32[768,128]{1,0:T(8,128)S(1)}, f32[768,128]{1,0:T(8,128)S(1)}) custom-call(bf16[16,3,48,128]{3,2,1,0:T(8,128)(2,1)S(1)} %all_to_all.10.q_ref.refs_0_, bf16[16,2,48,128]{3,2,1,0:T(8,128)(2,1)S(1)} %collective-permute-done.4.refs_0_, bf16[16,2,48,128]{3,2,1,0:T(8,128)(2,1)S(1)} %collective-permute-done.5.refs_1_, ...), custom_call_target="tpu_custom_call" | custom-call | flops 603979776 | bytes 2162688 | tf_op jit(solution)/shard_map/pallas_call | solution.py:169
  65.4 0.0 collective-permute-done.3.refs_1_
  65.4 2.9 %shard_map.77 = bf16[768,128]{1,0:T(8,128)(2,1)} custom-call(bf16[16,3,48,128]{3,2,1,0:T(8,128)(2,1)S(1)} %all_to_all.10.q_ref.refs_0_, bf16[16,2,48,128]{3,2,1,0:T(8,128)(2,1)S(1)} %collective-permute-done.2.refs_0_, bf16[16,2,48,128]{3,2,1,0:T(8,128)(2,1)S(1)} %collective-permute-done.3.refs_1_, f32[768,128]{1,0:T(8,128)S(1)} %get-tuple-element.20.refs_2_, ...), custom_call_target="tpu_custom_call" | custom-call | flops 603979776 | bytes 2162688 | tf_op jit(solution)/shard_map/pallas_call | solution.py:169
  68.3 5.9 %all-to-all-start.1 = ((bf16[16,48,128]{2,1,0:T(8,128)(2,1)}), bf16[16,48,128]{2,1,0:T(8,128)(2,1)S(1)}, u32[]{:S(2)}, u32[]{:S(2)}) async-start(bf16[16,48,128]{2,1,0:T(8,128)(2,1)} %bitcast.1), calls=%async_computation.1 | async-start | bytes 393216 | tf_op jit(solution)/shard_map/all_to_all | solution.py:235
  74.2 1.1 reshape.18.scales_ref
  75.3 0.0 copy-start.1
  75.3 4.0 %copy-done.1 = s32[2048,1280]{1,0:T(8,128)S(1)} copy-done((s32[2048,1280]{1,0:T(8,128)S(1)}, s32[2048,1280]{1,0:T(8,128)}, u32[]{:S(2)}) %copy-start.1) | copy-done | bytes 10485784
  79.3 12.6 %shard_map.78.w_ref = bf16[2,2048,2560]{2,1,0:T(8,128)(2,1)} custom-call(s32[1]{0:T(128)} %bitcast.2.half_ref, s32[2048,1280]{1,0:T(8,128)S(1)} %copy-done.1, f32[16,4,1280]{2,1,0:T(4,128)S(1)} %reshape.18.scales_ref), custom_call_target="tpu_custom_call" | custom-call | flops 78643200 | bytes 31457280 | tf_op jit(solution)/shard_map/pallas_call | solution.py:83
  91.9 0.0 all-to-all-done.1.x_ref
  91.9 0.0 copy-start
  91.9 7.0 %copy-done = bf16[2,2048,2560]{2,1,0:T(8,128)(2,1)S(1)} copy-done((bf16[2,2048,2560]{2,1,0:T(8,128)(2,1)S(1)}, bf16[2,2048,2560]{2,1,0:T(8,128)(2,1)}, u32[]{:S(2)}) %copy-start) | copy-done | bytes 20971544
  98.9 0.0 copy-start.4
  98.9 0.0 copy-start.5
  98.9 3.1 %shard_map.80 = bf16[48,2560]{1,0:T(8,128)(2,1)S(1)} custom-call(bf16[16,48,128]{2,1,0:T(8,128)(2,1)S(1)} %all-to-all-done.1.x_ref, bf16[2,2048,2560]{2,1,0:T(8,128)(2,1)S(1)} %copy-done), custom_call_target="tpu_custom_call" | custom-call | flops 503316480 | bytes 10485760 | tf_op jit(solution)/shard_map/pallas_call | solution.py:188
  102.0 3.0 %collective-permute-start.7 = (bf16[48,2560]{1,0:T(8,128)(2,1)S(1)}, bf16[48,2560]{1,0:T(8,128)(2,1)S(1)}, u32[]{:S(2)}, u32[]{:S(2)}) collective-permute-start(bf16[48,2560]{1,0:T(8,128)(2,1)S(1)} %shard_map.80), channel_id=1, source_target_pairs={{0,1},{1,0},{2,3},{3,2},{4,5},{5,4},{6,7},{7,6},{8,9},{9,8},{10,11... | collective-permute-start | bytes 737288 | tf_op jit(solution)/shard_map/ppermute | solution.py:239
  105.0 3.1 %shard_map.79 = f32[48,2560]{1,0:T(8,128)S(1)} custom-call(bf16[16,48,128]{2,1,0:T(8,128)(2,1)S(1)} %all-to-all-done.1.x_ref, bf16[2,2048,2560]{2,1,0:T(8,128)(2,1)S(1)} %copy-done), custom_call_target="tpu_custom_call" | custom-call | flops 503316480 | bytes 10485760 | tf_op jit(solution)/shard_map/pallas_call | solution.py:188
  108.2 3.5 %collective-permute-done.7 = bf16[48,2560]{1,0:T(8,128)(2,1)S(1)} collective-permute-done((bf16[48,2560]{1,0:T(8,128)(2,1)S(1)}, bf16[48,2560]{1,0:T(8,128)(2,1)S(1)}, u32[]{:S(2)}, u32[]{:S(2)}) %collective-permute-start.7) | collective-permute-done | bytes 245792 | tf_op jit(solution)/shard_map/ppermute | solution.py:239
  111.7 0.0 copy-done.4
  111.7 0.0 copy-done.5
  111.7 0.8 add_multiply_fusion
  (2 shorter events, 0.1 us)
Async XLA Ops:
  0.8 1.1 copy-start.2
  1.8 0.7 copy-start.3
  20.0 19.8 %collective-permute-start.1 = (bf16[16,2,48,128]{3,2,1,0:T(8,128)(2,1)S(1)}, bf16[16,2,48,128]{3,2,1,0:T(8,128)(2,1)S(1)}, u32[]{:S(2)}, u32[]{:S(2)}) collective-permute-start(bf16[16,2,48,128]{3,2,1,0:T(8,128)(2,1)S(1)} %slice.4), channel_id=1, source_target_pairs={{0,48},{16,0},{32,16},{48,32},{1,49},{17,1},{33,17},{49,33},{2,50}... | collective-permute-start | bytes 1179656 | tf_op jit(solution)/shard_map/ppermute | solution.py:218
  25.5 19.1 %collective-permute-start = (bf16[16,2,48,128]{3,2,1,0:T(8,128)(2,1)S(1)}, bf16[16,2,48,128]{3,2,1,0:T(8,128)(2,1)S(1)}, u32[]{:S(2)}, u32[]{:S(2)}) collective-permute-start(bf16[16,2,48,128]{3,2,1,0:T(8,128)(2,1)S(1)} %slice.4), channel_id=1, source_target_pairs={{0,16},{16,32},{32,48},{48,0},{1,17},{17,33},{33,49},{49,1},{2,18}... | collective-permute-start | bytes 1179656 | tf_op jit(solution)/shard_map/ppermute | solution.py:217
  44.7 14.2 %collective-permute-start.2 = (bf16[16,2,48,128]{3,2,1,0:T(8,128)(2,1)S(1)}, bf16[16,2,48,128]{3,2,1,0:T(8,128)(2,1)S(1)}, u32[]{:S(2)}, u32[]{:S(2)}) collective-permute-start(bf16[16,2,48,128]{3,2,1,0:T(8,128)(2,1)S(1)} %broadcast_select_fusion), channel_id=1, source_target_pairs={{0,16},{2,50},{16,32},{18,2},{32,48},{34,18},{48,0},{50,34},{1,17}... | collective-permute-start | bytes 1179656 | tf_op jit(solution)/shard_map/ppermute | solution.py:228
  44.8 14.1 %collective-permute-start.6 = (bf16[16,2,48,128]{3,2,1,0:T(8,128)(2,1)S(1)}, bf16[16,2,48,128]{3,2,1,0:T(8,128)(2,1)S(1)}, u32[]{:S(2)}, u32[]{:S(2)}) collective-permute-start(bf16[16,2,48,128]{3,2,1,0:T(8,128)(2,1)S(1)} %slice.4), channel_id=1, source_target_pairs={{0,2},{2,0},{1,3},{3,1},{4,6},{6,4},{5,7},{7,5},{8,10},{10,8},{9,1... | collective-permute-start | bytes 1179656 | tf_op jit(solution)/shard_map/ppermute | solution.py:215
  44.9 18.4 %collective-permute-start.5 = (bf16[16,2,48,128]{3,2,1,0:T(8,128)(2,1)S(1)}, bf16[16,2,48,128]{3,2,1,0:T(8,128)(2,1)S(1)}, u32[]{:S(2)}, u32[]{:S(2)}) collective-permute-start(bf16[16,2,48,128]{3,2,1,0:T(8,128)(2,1)S(1)} %collective-permute-done.1.refs_1_), channel_id=1, source_target_pairs={{0,2},{2,0},{1,3},{3,1},{4,6},{6,4},{5,7},{7,5},{8,10},{10,8},{9,1... | collective-permute-start | bytes 1179656 | tf_op jit(solution)/shard_map/ppermute | solution.py:215
  45.4 17.9 %collective-permute-start.4 = (bf16[16,2,48,128]{3,2,1,0:T(8,128)(2,1)S(1)}, bf16[16,2,48,128]{3,2,1,0:T(8,128)(2,1)S(1)}, u32[]{:S(2)}, u32[]{:S(2)}) collective-permute-start(bf16[16,2,48,128]{3,2,1,0:T(8,128)(2,1)S(1)} %collective-permute-done.refs_0_), channel_id=1, source_target_pairs={{0,2},{2,0},{1,3},{3,1},{4,6},{6,4},{5,7},{7,5},{8,10},{10,8},{9,1... | collective-permute-start | bytes 1179656 | tf_op jit(solution)/shard_map/ppermute | solution.py:215
  58.8 6.6 %collective-permute-start.3 = (bf16[16,2,48,128]{3,2,1,0:T(8,128)(2,1)S(1)}, bf16[16,2,48,128]{3,2,1,0:T(8,128)(2,1)S(1)}, u32[]{:S(2)}, u32[]{:S(2)}) collective-permute-start(bf16[16,2,48,128]{3,2,1,0:T(8,128)(2,1)S(1)} %collective-permute-done.2.refs_0_), channel_id=1, source_target_pairs={{0,2},{2,0},{1,3},{3,1},{4,6},{6,4},{5,7},{7,5},{8,10},{10,8},{9,1... | collective-permute-start | bytes 1179656 | tf_op jit(solution)/shard_map/ppermute | solution.py:215
  68.3 23.6 %all-to-all-start.1 = ((bf16[16,48,128]{2,1,0:T(8,128)(2,1)}), bf16[16,48,128]{2,1,0:T(8,128)(2,1)S(1)}, u32[]{:S(2)}, u32[]{:S(2)}) async-start(bf16[16,48,128]{2,1,0:T(8,128)(2,1)} %bitcast.1), calls=%async_computation.1 | async-start | bytes 393216 | tf_op jit(solution)/shard_map/all_to_all | solution.py:235
  75.3 4.0 %copy-start.1 = (s32[2048,1280]{1,0:T(8,128)S(1)}, s32[2048,1280]{1,0:T(8,128)}, u32[]{:S(2)}) copy-start(s32[2048,1280]{1,0:T(8,128)} %words_ref.1) | copy-start | bytes 31457284
  91.9 7.0 %copy-start = (bf16[2,2048,2560]{2,1,0:T(8,128)(2,1)S(1)}, bf16[2,2048,2560]{2,1,0:T(8,128)(2,1)}, u32[]{:S(2)}) copy-start(bf16[2,2048,2560]{2,1,0:T(8,128)(2,1)} %shard_map.78.w_ref) | copy-start | bytes 62914564
  98.9 12.8 %copy-start.4 = (f32[2560]{0:T(1024)S(1)}, f32[2560]{0:T(1024)}, u32[]{:S(2)}) copy-start(f32[2560]{0:T(1024)} %param.12) | copy-start | bytes 30724
  98.9 12.8 %copy-start.5 = (f32[2560]{0:T(1024)S(1)}, f32[2560]{0:T(1024)}, u32[]{:S(2)}) copy-start(f32[2560]{0:T(1024)} %param.11) | copy-start | bytes 30724
  102.0 9.7 %collective-permute-start.7 = (bf16[48,2560]{1,0:T(8,128)(2,1)S(1)}, bf16[48,2560]{1,0:T(8,128)(2,1)S(1)}, u32[]{:S(2)}, u32[]{:S(2)}) collective-permute-start(bf16[48,2560]{1,0:T(8,128)(2,1)S(1)} %shard_map.80), channel_id=1, source_target_pairs={{0,1},{1,0},{2,3},{3,2},{4,5},{5,4},{6,7},{7,6},{8,9},{9,8},{10,11... | collective-permute-start | bytes 737288 | tf_op jit(solution)/shard_map/ppermute | solution.py:239

commit v2 on v1

--- a/solution.py
+++ b/solution.py
@@ -29,9 +29,13 @@
 
 def rotate_kernel(pos_ref, freq_ref, x_ref, out_ref, wide):
     tokens, kinds, heads, width = x_ref.shape
-    pos = pos_ref[...].astype(F32)
-    freq = freq_ref[...]
-    angles = pos[:, 0:1] * freq[0:1, :] + pos[:, 1:2] * freq[1:2, :] + pos[:, 2:3] * freq[2:3, :]
+    angles = lax.dot_general(
+        pos_ref[...].astype(F32),
+        freq_ref[...],
+        (((0,), (0,)), ((), ())),
+        precision=lax.Precision.HIGHEST,
+        preferred_element_type=F32,
+    )
     cosine = jnp.cos(angles)
     sine = jnp.sin(angles)
     lane = lax.broadcasted_iota(jnp.int32, (tokens, width), 1)
@@ -56,7 +60,7 @@
         out_shape=jax.ShapeDtypeStruct((heads, kinds, tokens, width), BF16),
         scratch_shapes=[pltpu.VMEM((tokens * kinds * heads, width), F32)],
         compiler_params=pltpu.CompilerParams(vmem_limit_bytes=16 * 1024 * 1024),
-    )(positions.T, jnp.asarray(frequency_table(width)), head_inputs)
+    )(positions, jnp.asarray(frequency_table(width)), head_inputs)
 
 
 def dequantize_kernel(half_ref, words_ref, scales_ref, out_ref):
@@ -169,7 +173,7 @@
     return pl.pallas_call(
         functools.partial(attend_kernel, first, last, blocks, tile),
         out_shape=out_shape,
-        compiler_params=pltpu.CompilerParams(vmem_limit_bytes=32 * 1024 * 1024),
+        compiler_params=pltpu.CompilerParams(vmem_limit_bytes=16 * 1024 * 1024),
         cost_estimate=pl.CostEstimate(
             flops=pairs * width * 4, bytes_accessed=total * width * 2 * (2 * blocks + 7), transcendentals=pairs
         ),
@@ -202,10 +206,11 @@
 
 
 HEAD_AXES = ("x", "zl", "yl")
+RING = "zh"
 
 
 def body(head_inputs, positions, code_words, group_scales, out_gate, out_bias):
-    ring = lax.axis_size("zh")
+    ring = lax.axis_size(RING)
     half = lax.axis_index("yh").astype(jnp.int32).reshape(1)
     prepared = rotate(positions, head_inputs)
     grouped = lax.all_to_all(prepared, HEAD_AXES, split_axis=0, concat_axis=0, tiled=True)
@@ -214,21 +219,22 @@
     def swap(a):
         return lax.ppermute(a, "c", [(0, 1), (1, 0)])
 
-    up = lax.ppermute(own, "zh", [(i, (i + 1) % ring) for i in range(ring)])
-    down = lax.ppermute(own, "zh", [(i, (i - 1) % ring) for i in range(ring)])
+    up = lax.ppermute(own, RING, [(i, (i + 1) % ring) for i in range(ring)])
+    down = lax.ppermute(own, RING, [(i, (i - 1) % ring) for i in range(ring)])
     beside = swap(own)
     weights = dequantize(half, code_words, group_scales)
     state = attend(grouped, [grouped, beside], None, False)
+    up, down, state, weights = lax.optimization_barrier((up, down, state, weights))
     core = lax.axis_index("c")
-    onward = jnp.where(core == 0, up, down)
     hops = []
     for i in range(ring):
         hops.append((2 * i, 2 * ((i + 1) % ring)))
         hops.append((2 * i + 1, 2 * ((i - 1) % ring) + 1))
-    far = lax.ppermute(onward, ("zh", "c"), hops)
+    far = lax.ppermute(jnp.where(core == 0, up, down), (RING, "c"), hops)
     up_beside, down_beside = swap(up), swap(down)
     state = attend(grouped, [up, down], state, False)
     state = attend(grouped, [up_beside, down_beside], state, False)
+    far, state = lax.optimization_barrier((far, state))
     far_beside = swap(far)
     attended = attend(grouped, [far, far_beside], state, True)
     chunks = prepared.shape[0]

time: 114 us -> 97.4 us (0.85)
  waiting for transfers between devices: 36.1 us -> 13 us
  blocking collectives: 16.8 us -> 28.5 us
  starting transfers between devices: 15.1 us -> 10.3 us
    ppermute x3, waiting for transfers between devices: 32.5 us -> 9.22 us  [the longest x1 8.27 us: body(): far = lax.ppermute(jnp.where(core == 0, up, down), (RING, 'c'), hops)]
    all_to_all x0 -> x1, blocking collectives: none -> 11.8 us  [body(): lax.all_to_all(attended.reshape(chunks, -1, HD), HEAD_AXES, split_axis=0,...]
    all_to_all x1 -> x0, starting transfers between devices: 5.88 us -> none  [body(): lax.all_to_all(attended.reshape(chunks, -1, HD), HEAD_AXES, split_axis=0,...]
    ppermute x4, waiting for transfers between devices: 0.01 us -> 1.73 us  [swap(): return lax.ppermute(a, 'c', [(0, 1), (1, 0)])]
    ppermute x1, waiting for transfers between devices: 3.54 us -> 2.03 us  [body(): incoming = lax.ppermute(outgoing, 'yh', [(0, 1), (1, 0)])]
    ppermute x3, starting transfers between devices: 5.56 us -> 6.71 us  [the longest x1 5.48 us: body(): down = lax.ppermute(own, RING, [(i, (i - 1) % ring) for i in range(ring)])]
    unnamed x13 -> x14, local copies, waits for them, and re-layouts: 13.5 us -> 13.4 us
  transfers between devices with their start and end apart: 9 -> 8, of which waited for: 4 -> 4; matrix products, arithmetic and copies ran while one was open for 1% -> 1% of each run, Pallas kernels for 20% -> 23%
where the time goes in v2:
time: 97.4 us; the launch traced here: 95.6 us
  blocking collectives  28.5 us (29%)
  Pallas kernels  28.3 us (29%)
  local copies, waits for them, and re-layouts  14.5 us (15%)
  waiting for transfers between devices  13 us (13%)
  starting transfers between devices  10.3 us (11%)
    all_to_all x1, blocking collectives, body(): lax.all_to_all(prepared, HEAD_AXES, split_axis=0, concat_axis=0, tiled=True)  16.8 us
    unnamed x14, local copies, waits for them, and re-layouts  13.4 us
    pallas_call x1, Pallas kernels, dequantize(): pl.pallas_call(dequantize_kernel, grid=(groups,), in_specs=[pl.BlockSpec(...  12.6 us
    all_to_all x1, blocking collectives, body(): lax.all_to_all(attended.reshape(chunks, -1, HD), HEAD_AXES, split_axis=0,...  11.8 us
    pallas_call x4, Pallas kernels, attend(): pl.pallas_call(functools.partial(attend_kernel, first, last, blocks, tile...  8.73 us
    ppermute x1, waiting for transfers between devices, body(): far = lax.ppermute(jnp.where(core == 0, up, down), (RING, 'c'), hops)  8.27 us
    pallas_call x2, Pallas kernels, project(): pl.pallas_call(project_kernel, grid=(columns // tile,), in_specs=[pl.Bloc...  6.27 us
    ppermute x1, starting transfers between devices, body(): down = lax.ppermute(own, RING, [(i, (i - 1) % ring) for i in range(ring)])  5.48 us
  transfers between devices with their start and end apart: 8, of which 4 were waited for; matrix products, arithmetic and copies ran while one was open for 1% of the time, Pallas kernels for 23%

profile of v2, /device:TPU:6, one launch (start us, length us, event | category | flops | bytes accessed | tf_op | source)
XLA Modules:
  0.0 95.6 jit_solution(10196023772092291970)
XLA Ops:
  0.0 0.0 copy-start.2
  0.0 1.1 %copy-done.2 = bf16[48,3,16,128]{3,2,1,0:T(8,128)(2,1)S(1)} copy-done((bf16[48,3,16,128]{3,2,1,0:T(8,128)(2,1)S(1)}, bf16[48,3,16,128]{3,2,1,0:T(8,128)(2,1)}, u32[]{:S(2)}) %copy-start.2) | copy-done | bytes 589848
  1.1 0.0 copy-start.3
  1.1 0.7 copy-done.3
  1.7 0.0 copy-start.4
  1.7 0.7 copy-done.4
  2.4 0.8 shard_map.73
  3.2 16.8 %all_to_all.10.q_ref.refs_0_ = bf16[16,3,48,128]{3,2,1,0:T(8,128)(2,1)S(1)} all-to-all(bf16[16,3,48,128]{3,2,1,0:T(8,128)(2,1)S(1)} %shard_map.73), channel_id=1, replica_groups=mesh['x'=4,'zh'=4,'zl'=2,'yl'=2,'c'=2,'yh'=2] {'x','zl','yl'}, dimensions={0} | all-to-all | bytes 1179648 | tf_op jit(solution)/shard_map/all_to_all | solution.py:216
  20.0 0.1 collective-permute-start.2
  20.1 5.5 %collective-permute-start.1 = (bf16[16,2,48,128]{3,2,1,0:T(8,128)(2,1)S(1)}, bf16[16,2,48,128]{3,2,1,0:T(8,128)(2,1)S(1)}, u32[]{:S(2)}, u32[]{:S(2)}) collective-permute-start(bf16[16,2,48,128]{3,2,1,0:T(8,128)(2,1)S(1)} %slice.4), channel_id=1, source_target_pairs={{0,48},{16,0},{32,16},{48,32},{1,49},{17,1},{33,17},{49,33},{2,50}... | collective-permute-start | bytes 1179656 | tf_op jit(solution)/shard_map/ppermute | solution.py:223
  25.6 0.0 collective-permute-start
  25.6 1.1 %reshape.18.scales_ref = f32[16,4,1280]{2,1,0:T(4,128)S(1)} reshape(bf16[16,5120]{1,0:T(8,128)(2,1)} %param.10) | data formatting | bytes 491520 | tf_op jit(solution)/shard_map/reshape | solution.py:86
  26.7 0.0 copy-start.1
  26.7 4.0 %copy-done.1 = s32[2048,1280]{1,0:T(8,128)S(1)} copy-done((s32[2048,1280]{1,0:T(8,128)S(1)}, s32[2048,1280]{1,0:T(8,128)}, u32[]{:S(2)}) %copy-start.1) | copy-done | bytes 10485784
  30.6 12.6 %shard_map.75.w_ref = bf16[2,2048,2560]{2,1,0:T(8,128)(2,1)} custom-call(s32[1]{0:T(128)} %bitcast.half_ref, s32[2048,1280]{1,0:T(8,128)S(1)} %copy-done.1, f32[16,4,1280]{2,1,0:T(4,128)S(1)} %reshape.18.scales_ref), custom_call_target="tpu_custom_call" | custom-call | flops 78643200 | bytes 31457280 | tf_op jit(solution)/shard_map/pallas_call | solution.py:87
  43.2 0.0 collective-permute-done.2.refs_1_
  43.2 2.2 %shard_map.74 = (f32[768,128]{1,0:T(8,128)S(1)}, f32[768,128]{1,0:T(8,128)S(1)}, f32[768,128]{1,0:T(8,128)S(1)}) custom-call(bf16[16,3,48,128]{3,2,1,0:T(8,128)(2,1)S(1)} %all_to_all.10.q_ref.refs_0_, bf16[16,3,48,128]{3,2,1,0:T(8,128)(2,1)S(1)} %all_to_all.10.q_ref.refs_0_, bf16[16,2,48,128]{3,2,1,0:T(8,128)(2,1)S(1)} %collective-permute-done.2.refs_1_), custom_call_target="tpu_custom_call" | custom-call | flops 603979776 | bytes 2162688 | tf_op jit(solution)/shard_map/pallas_call | solution.py:173
  45.5 0.0 collective-permute-done.1.refs_1_
  45.5 0.9 collective-permute-done.refs_0_
  46.4 0.0 collective-permute-start.4
  46.4 0.5 collective-permute-start.5
  47.0 1.2 %collective-permute-start.3 = (bf16[16,2,48,128]{3,2,1,0:T(8,128)(2,1)S(1)}, bf16[16,2,48,128]{3,2,1,0:T(8,128)(2,1)S(1)}, u32[]{:S(2)}, u32[]{:S(2)}) collective-permute-start(bf16[16,2,48,128]{3,2,1,0:T(8,128)(2,1)S(1)} %broadcast_select_fusion), channel_id=1, source_target_pairs={{0,16},{2,50},{16,32},{18,2},{32,48},{34,18},{48,0},{50,34},{1,17}... | collective-permute-start | bytes 1179656 | tf_op jit(solution)/shard_map/ppermute | solution.py:233
  48.2 2.1 %shard_map.76 = (f32[768,128]{1,0:T(8,128)S(1)}, f32[768,128]{1,0:T(8,128)S(1)}, f32[768,128]{1,0:T(8,128)S(1)}) custom-call(bf16[16,3,48,128]{3,2,1,0:T(8,128)(2,1)S(1)} %all_to_all.10.q_ref.refs_0_, bf16[16,2,48,128]{3,2,1,0:T(8,128)(2,1)S(1)} %collective-permute-done.refs_0_, bf16[16,2,48,128]{3,2,1,0:T(8,128)(2,1)S(1)} %collective-permute-done.1.refs_1_, ...), custom_call_target="tpu_custom_call" | custom-call | flops 603979776 | bytes 2162688 | tf_op jit(solution)/shard_map/pallas_call | solution.py:173
  50.3 0.0 collective-permute-done.4.refs_0_
  50.4 0.0 collective-permute-done.5.refs_1_
  50.4 2.1 %shard_map.77 = (f32[768,128]{1,0:T(8,128)S(1)}, f32[768,128]{1,0:T(8,128)S(1)}, f32[768,128]{1,0:T(8,128)S(1)}) custom-call(bf16[16,3,48,128]{3,2,1,0:T(8,128)(2,1)S(1)} %all_to_all.10.q_ref.refs_0_, bf16[16,2,48,128]{3,2,1,0:T(8,128)(2,1)S(1)} %collective-permute-done.4.refs_0_, bf16[16,2,48,128]{3,2,1,0:T(8,128)(2,1)S(1)} %collective-permute-done.5.refs_1_, ...), custom_call_target="tpu_custom_call" | custom-call | flops 603979776 | bytes 2162688 | tf_op jit(solution)/shard_map/pallas_call | solution.py:173
  52.5 8.3 %collective-permute-done.3.refs_0_ = bf16[16,2,48,128]{3,2,1,0:T(8,128)(2,1)S(1)} collective-permute-done((bf16[16,2,48,128]{3,2,1,0:T(8,128)(2,1)S(1)}, bf16[16,2,48,128]{3,2,1,0:T(8,128)(2,1)S(1)}, u32[]{:S(2)}, u32[]{:S(2)}) %collective-permute-start.3) | collective-permute-done | bytes 393248 | tf_op jit(solution)/shard_map/ppermute | solution.py:233
  60.8 0.0 collective-permute-start.6
  60.8 1.7 %collective-permute-done.6.refs_1_ = bf16[16,2,48,128]{3,2,1,0:T(8,128)(2,1)S(1)} collective-permute-done((bf16[16,2,48,128]{3,2,1,0:T(8,128)(2,1)S(1)}, bf16[16,2,48,128]{3,2,1,0:T(8,128)(2,1)S(1)}, u32[]{:S(2)}, u32[]{:S(2)}) %collective-permute-start.6) | collective-permute-done | bytes 393248 | tf_op jit(solution)/shard_map/ppermute | solution.py:220
  62.5 2.2 %shard_map.78 = bf16[768,128]{1,0:T(8,128)(2,1)S(1)} custom-call(bf16[16,3,48,128]{3,2,1,0:T(8,128)(2,1)S(1)} %all_to_all.10.q_ref.refs_0_, bf16[16,2,48,128]{3,2,1,0:T(8,128)(2,1)S(1)} %collective-permute-done.3.refs_0_, bf16[16,2,48,128]{3,2,1,0:T(8,128)(2,1)S(1)} %collective-permute-done.6.refs_1_, f32[768,128]{1,0:T(8,128)S(1)} %get-tuple-element.39.refs_2_, ...), custom_call_target="tpu_custom_call" | custom-call | flops 603979776 | bytes 2162688 | tf_op jit(solution)/shard_map/pallas_call | solution.py:173
  64.7 11.8 %all_to_all.11.x_ref = bf16[16,48,128]{2,1,0:T(8,128)(2,1)S(1)} all-to-all(bf16[16,48,128]{2,1,0:T(8,128)(2,1)S(1)} %bitcast.2), channel_id=1, replica_groups=mesh['x'=4,'zh'=4,'zl'=2,'yl'=2,'c'=2,'yh'=2] {'x','zl','yl'}, dimensions={0} | all-to-all | bytes 393216 | tf_op jit(solution)/shard_map/all_to_all | solution.py:241
  76.5 0.0 copy-start
  76.5 7.0 %copy-done = bf16[2,2048,2560]{2,1,0:T(8,128)(2,1)S(1)} copy-done((bf16[2,2048,2560]{2,1,0:T(8,128)(2,1)S(1)}, bf16[2,2048,2560]{2,1,0:T(8,128)(2,1)}, u32[]{:S(2)}) %copy-start) | copy-done | bytes 20971544
  83.5 0.0 copy-start.5
  83.5 0.0 copy-start.6
  83.5 3.1 %shard_map.80 = bf16[48,2560]{1,0:T(8,128)(2,1)S(1)} custom-call(bf16[16,48,128]{2,1,0:T(8,128)(2,1)S(1)} %all_to_all.11.x_ref, bf16[2,2048,2560]{2,1,0:T(8,128)(2,1)S(1)} %copy-done), custom_call_target="tpu_custom_call" | custom-call | flops 503316480 | bytes 10485760 | tf_op jit(solution)/shard_map/pallas_call | solution.py:192
  86.6 3.0 %collective-permute-start.7 = (bf16[48,2560]{1,0:T(8,128)(2,1)S(1)}, bf16[48,2560]{1,0:T(8,128)(2,1)S(1)}, u32[]{:S(2)}, u32[]{:S(2)}) collective-permute-start(bf16[48,2560]{1,0:T(8,128)(2,1)S(1)} %shard_map.80), channel_id=1, source_target_pairs={{0,1},{1,0},{2,3},{3,2},{4,5},{5,4},{6,7},{7,6},{8,9},{9,8},{10,11... | collective-permute-start | bytes 737288 | tf_op jit(solution)/shard_map/ppermute | solution.py:245
  89.6 3.1 %shard_map.79 = f32[48,2560]{1,0:T(8,128)S(1)} custom-call(bf16[16,48,128]{2,1,0:T(8,128)(2,1)S(1)} %all_to_all.11.x_ref, bf16[2,2048,2560]{2,1,0:T(8,128)(2,1)S(1)} %copy-done), custom_call_target="tpu_custom_call" | custom-call | flops 503316480 | bytes 10485760 | tf_op jit(solution)/shard_map/pallas_call | solution.py:192
  92.8 2.0 %collective-permute-done.7 = bf16[48,2560]{1,0:T(8,128)(2,1)S(1)} collective-permute-done((bf16[48,2560]{1,0:T(8,128)(2,1)S(1)}, bf16[48,2560]{1,0:T(8,128)(2,1)S(1)}, u32[]{:S(2)}, u32[]{:S(2)}) %collective-permute-start.7) | collective-permute-done | bytes 245792 | tf_op jit(solution)/shard_map/ppermute | solution.py:245
  94.8 0.0 copy-done.5
  94.8 0.0 copy-done.6
  94.8 0.8 add_multiply_fusion
  (2 shorter events, 0.1 us)
Async XLA Ops:
  0.0 1.1 %copy-start.2 = (bf16[48,3,16,128]{3,2,1,0:T(8,128)(2,1)S(1)}, bf16[48,3,16,128]{3,2,1,0:T(8,128)(2,1)}, u32[]{:S(2)}) copy-start(bf16[48,3,16,128]{3,2,1,0:T(8,128)(2,1)} %x_ref.1) | copy-start | bytes 1769476
  1.1 0.7 copy-start.3
  1.7 0.7 copy-start.4
  20.0 23.2 %collective-permute-start.2 = (bf16[16,2,48,128]{3,2,1,0:T(8,128)(2,1)S(1)}, bf16[16,2,48,128]{3,2,1,0:T(8,128)(2,1)S(1)}, u32[]{:S(2)}, u32[]{:S(2)}) collective-permute-start(bf16[16,2,48,128]{3,2,1,0:T(8,128)(2,1)S(1)} %slice.4), channel_id=1, source_target_pairs={{0,2},{2,0},{1,3},{3,1},{4,6},{6,4},{5,7},{7,5},{8,10},{10,8},{9,1... | collective-permute-start | bytes 1179656 | tf_op jit(solution)/shard_map/ppermute | solution.py:220
  20.1 25.4 %collective-permute-start.1 = (bf16[16,2,48,128]{3,2,1,0:T(8,128)(2,1)S(1)}, bf16[16,2,48,128]{3,2,1,0:T(8,128)(2,1)S(1)}, u32[]{:S(2)}, u32[]{:S(2)}) collective-permute-start(bf16[16,2,48,128]{3,2,1,0:T(8,128)(2,1)S(1)} %slice.4), channel_id=1, source_target_pairs={{0,48},{16,0},{32,16},{48,32},{1,49},{17,1},{33,17},{49,33},{2,50}... | collective-permute-start | bytes 1179656 | tf_op jit(solution)/shard_map/ppermute | solution.py:223
  25.6 20.8 %collective-permute-start = (bf16[16,2,48,128]{3,2,1,0:T(8,128)(2,1)S(1)}, bf16[16,2,48,128]{3,2,1,0:T(8,128)(2,1)S(1)}, u32[]{:S(2)}, u32[]{:S(2)}) collective-permute-start(bf16[16,2,48,128]{3,2,1,0:T(8,128)(2,1)S(1)} %slice.4), channel_id=1, source_target_pairs={{0,16},{16,32},{32,48},{48,0},{1,17},{17,33},{33,49},{49,1},{2,18}... | collective-permute-start | bytes 1179656 | tf_op jit(solution)/shard_map/ppermute | solution.py:222
  26.7 4.0 %copy-start.1 = (s32[2048,1280]{1,0:T(8,128)S(1)}, s32[2048,1280]{1,0:T(8,128)}, u32[]{:S(2)}) copy-start(s32[2048,1280]{1,0:T(8,128)} %words_ref.1) | copy-start | bytes 31457284
  46.4 3.9 %collective-permute-start.4 = (bf16[16,2,48,128]{3,2,1,0:T(8,128)(2,1)S(1)}, bf16[16,2,48,128]{3,2,1,0:T(8,128)(2,1)S(1)}, u32[]{:S(2)}, u32[]{:S(2)}) collective-permute-start(bf16[16,2,48,128]{3,2,1,0:T(8,128)(2,1)S(1)} %collective-permute-done.refs_0_), channel_id=1, source_target_pairs={{0,2},{2,0},{1,3},{3,1},{4,6},{6,4},{5,7},{7,5},{8,10},{10,8},{9,1... | collective-permute-start | bytes 1179656 | tf_op jit(solution)/shard_map/ppermute | solution.py:220
  46.4 3.9 %collective-permute-start.5 = (bf16[16,2,48,128]{3,2,1,0:T(8,128)(2,1)S(1)}, bf16[16,2,48,128]{3,2,1,0:T(8,128)(2,1)S(1)}, u32[]{:S(2)}, u32[]{:S(2)}) collective-permute-start(bf16[16,2,48,128]{3,2,1,0:T(8,128)(2,1)S(1)} %collective-permute-done.1.refs_1_), channel_id=1, source_target_pairs={{0,2},{2,0},{1,3},{3,1},{4,6},{6,4},{5,7},{7,5},{8,10},{10,8},{9,1... | collective-permute-start | bytes 1179656 | tf_op jit(solution)/shard_map/ppermute | solution.py:220
  47.0 13.8 %collective-permute-start.3 = (bf16[16,2,48,128]{3,2,1,0:T(8,128)(2,1)S(1)}, bf16[16,2,48,128]{3,2,1,0:T(8,128)(2,1)S(1)}, u32[]{:S(2)}, u32[]{:S(2)}) collective-permute-start(bf16[16,2,48,128]{3,2,1,0:T(8,128)(2,1)S(1)} %broadcast_select_fusion), channel_id=1, source_target_pairs={{0,16},{2,50},{16,32},{18,2},{32,48},{34,18},{48,0},{50,34},{1,17}... | collective-permute-start | bytes 1179656 | tf_op jit(solution)/shard_map/ppermute | solution.py:233
  60.8 1.7 %collective-permute-start.6 = (bf16[16,2,48,128]{3,2,1,0:T(8,128)(2,1)S(1)}, bf16[16,2,48,128]{3,2,1,0:T(8,128)(2,1)S(1)}, u32[]{:S(2)}, u32[]{:S(2)}) collective-permute-start(bf16[16,2,48,128]{3,2,1,0:T(8,128)(2,1)S(1)} %collective-permute-done.3.refs_0_), channel_id=1, source_target_pairs={{0,2},{2,0},{1,3},{3,1},{4,6},{6,4},{5,7},{7,5},{8,10},{10,8},{9,1... | collective-permute-start | bytes 1179656 | tf_op jit(solution)/shard_map/ppermute | solution.py:220
  76.5 7.0 %copy-start = (bf16[2,2048,2560]{2,1,0:T(8,128)(2,1)S(1)}, bf16[2,2048,2560]{2,1,0:T(8,128)(2,1)}, u32[]{:S(2)}) copy-start(bf16[2,2048,2560]{2,1,0:T(8,128)(2,1)} %shard_map.75.w_ref) | copy-start | bytes 62914564
  83.5 11.3 %copy-start.5 = (f32[2560]{0:T(1024)S(1)}, f32[2560]{0:T(1024)}, u32[]{:S(2)}) copy-start(f32[2560]{0:T(1024)} %param.12) | copy-start | bytes 30724
  83.5 11.3 %copy-start.6 = (f32[2560]{0:T(1024)S(1)}, f32[2560]{0:T(1024)}, u32[]{:S(2)}) copy-start(f32[2560]{0:T(1024)} %param.11) | copy-start | bytes 30724
  86.6 8.2 %collective-permute-start.7 = (bf16[48,2560]{1,0:T(8,128)(2,1)S(1)}, bf16[48,2560]{1,0:T(8,128)(2,1)S(1)}, u32[]{:S(2)}, u32[]{:S(2)}) collective-permute-start(bf16[48,2560]{1,0:T(8,128)(2,1)S(1)} %shard_map.80), channel_id=1, source_target_pairs={{0,1},{1,0},{2,3},{3,2},{4,5},{5,4},{6,7},{7,6},{8,9},{9,8},{10,11... | collective-permute-start | bytes 737288 | tf_op jit(solution)/shard_map/ppermute | solution.py:245

commit v3 on v2

--- a/solution.py
+++ b/solution.py
@@ -3,7 +3,6 @@
 
 import jax
 import jax.numpy as jnp
-import numpy as np
 from jax import lax
 from jax.experimental import pallas as pl
 from jax.experimental.pallas import tpu as pltpu
@@ -16,32 +15,39 @@
 BF16 = jnp.bfloat16
 
 
-def frequency_table(width):
-    pair = np.arange(width) // 2
+def angle_rates(width):
     frame = (width - 4 * (width // 6)) // 2
     side = width // 6
-    segment = np.where(pair < frame, 0, np.where(pair < frame + side, 1, 2))
-    start = np.where(segment == 0, 0, np.where(segment == 1, frame, frame + side))
-    extent = np.where(segment == 0, frame, side)
-    value = np.power(10000.0, -(pair - start) / extent)
-    return np.stack([np.where(segment == s, value, 0.0) for s in range(3)]).astype(np.float32)
-
-
-def rotate_kernel(pos_ref, freq_ref, x_ref, out_ref, wide):
+    pair = lax.broadcasted_iota(jnp.int32, (3, width), 1) // 2
+    row = lax.broadcasted_iota(jnp.int32, (3, width), 0)
+    start = jnp.where(row == 0, 0, jnp.where(row == 1, frame, frame + side))
+    extent = jnp.where(row == 0, frame, side)
+    within = pair - start
+    rate = jnp.exp(within.astype(F32) / extent.astype(F32) * (-math.log(10000.0)))
+    return jnp.where((within >= 0) & (within < extent), rate, 0.0)
+
+
+def rotate_kernel(pos_hbm, x_hbm, out_ref, pos_ref, x_ref, wide, sems):
+    pos_copy = pltpu.make_async_copy(pos_hbm, pos_ref, sems.at[0])
+    x_copy = pltpu.make_async_copy(x_hbm, x_ref, sems.at[1])
+    pos_copy.start()
+    x_copy.start()
     tokens, kinds, heads, width = x_ref.shape
+    rates = angle_rates(width)
+    is_even = lax.broadcasted_iota(jnp.int32, (tokens, width), 1) % 2 == 0
+    pos_copy.wait()
     angles = lax.dot_general(
         pos_ref[...].astype(F32),
-        freq_ref[...],
+        rates,
         (((0,), (0,)), ((), ())),
         precision=lax.Precision.HIGHEST,
         preferred_element_type=F32,
     )
     cosine = jnp.cos(angles)
     sine = jnp.sin(angles)
-    lane = lax.broadcasted_iota(jnp.int32, (tokens, width), 1)
-    is_even = lane % 2 == 0
     sine_even = jnp.where(is_even, -sine, 0.0)
     sine_odd = jnp.where(is_even, 0.0, sine)
+    x_copy.wait()
     wide[...] = x_ref[...].astype(F32).reshape(tokens * kinds * heads, width)
     for kind in range(kinds):
         for head in range(heads):
@@ -57,46 +63,92 @@
     tokens, kinds, heads, width = head_inputs.shape
     return pl.pallas_call(
         rotate_kernel,
+        in_specs=[pl.BlockSpec(memory_space=pltpu.HBM)] * 2,
+        out_specs=pl.BlockSpec(memory_space=pltpu.VMEM),
         out_shape=jax.ShapeDtypeStruct((heads, kinds, tokens, width), BF16),
-        scratch_shapes=[pltpu.VMEM((tokens * kinds * heads, width), F32)],
+        scratch_shapes=[
+            pltpu.VMEM(positions.shape, positions.dtype),
+            pltpu.VMEM(head_inputs.shape, head_inputs.dtype),
+            pltpu.VMEM((tokens * kinds * heads, width), F32),
+            pltpu.SemaphoreType.DMA((2,)),
+        ],
         compiler_params=pltpu.CompilerParams(vmem_limit_bytes=16 * 1024 * 1024),
-    )(positions, jnp.asarray(frequency_table(width)), head_inputs)
-
-
-def dequantize_kernel(half_ref, words_ref, scales_ref, out_ref):
+    )(in_hbm(positions), in_hbm(head_inputs))
+
+
+def in_hbm(array):
+    return pltpu.with_memory_space_constraint(array, pltpu.HBM)
+
+
+def dequantize_kernel(half_ref, words_ref, scales_ref, out_ref, slots, wide, sems):
+    rows, quarter = words_ref.shape
+    groups = scales_ref.shape[0]
+    depth = rows // groups
     half = half_ref[0]
-    quarter = words_ref.shape[1]
-    words = words_ref[...]
-    for part in range(2):
-        mine = half if part else 1 - half
-        shifted = lax.shift_right_logical(words, jnp.full(words.shape, 8 * mine, jnp.int32))
-        for low in range(2):
-            scale = scales_ref[0, pl.ds(2 * mine + low, 1), :]
-            if low:
-                level = ((shifted & 240) - 128).astype(F32) * (scale * 0.0625)
-            else:
-                level = ((shifted & 15) - 8).astype(F32) * scale
-            out_ref[part, :, low * quarter : (low + 1) * quarter] = level.astype(BF16)
+    ahead, chunk, across = slots.shape[0], 16, 256
+
+    def fetch(g):
+        slot = lax.rem(g, ahead)
+        start = pl.multiple_of(g * depth, depth)
+        return pltpu.make_async_copy(words_ref.at[pl.ds(start, depth)], slots.at[slot], sems.at[slot])
+
+    for g in range(ahead):
+        fetch(g).start()
+    wide[...] = scales_ref[...].astype(F32)
+
+    def step(g, carry):
+        fetch(g).wait()
+        slot = lax.rem(g, ahead)
+        start = pl.multiple_of(g * depth, depth)
+        for column in range(0, quarter, across):
+            for part in range(2):
+                mine = half if part else 1 - half
+                scales = []
+                for low in range(2):
+                    at = pl.multiple_of((2 * mine + low) * quarter + column, 128)
+                    row = wide[pl.ds(g, 1), pl.ds(at, across)] * (0.0625 if low else 1.0)
+                    scales.append(jnp.broadcast_to(row, (chunk, across)))
+                for r in range(0, depth, chunk):
+                    words = slots[slot, r : r + chunk, column : column + across]
+                    shifted = lax.shift_right_logical(words, jnp.full(words.shape, 8 * mine, jnp.int32))
+                    for low in range(2):
+                        level = ((shifted & 240) - 128) if low else ((shifted & 15) - 8)
+                        out_ref[
+                            part,
+                            pl.ds(start + r, chunk),
+                            low * quarter + column : low * quarter + column + across,
+                        ] = (level.astype(F32) * scales[low]).astype(BF16)
+
+        @pl.when(g + ahead < groups)
+        def _():
+            fetch(g + ahead).start()
+
+        return carry
+
+    lax.fori_loop(0, groups, step, 0)
 
 
 def dequantize(half, code_words, group_scales):
     rows, quarter = code_words.shape
     groups = group_scales.shape[0]
-    depth = rows // groups
-    scales = group_scales.astype(F32).reshape(groups, 4, quarter)
+    ahead = 4
     return pl.pallas_call(
         dequantize_kernel,
-        grid=(groups,),
         in_specs=[
             pl.BlockSpec(memory_space=pltpu.SMEM),
-            pl.BlockSpec((depth, quarter), lambda g: (g, 0)),
-            pl.BlockSpec((1, 4, quarter), lambda g: (g, 0, 0)),
+            pl.BlockSpec(memory_space=pltpu.HBM),
+            pl.BlockSpec(memory_space=pltpu.VMEM),
         ],
-        out_specs=pl.BlockSpec((2, depth, 2 * quarter), lambda g: (0, g, 0)),
-        out_shape=jax.ShapeDtypeStruct((2, rows, 2 * quarter), BF16),
-        compiler_params=pltpu.CompilerParams(vmem_limit_bytes=24 * 1024 * 1024),
+        out_specs=pl.BlockSpec(memory_space=pltpu.VMEM),
+        out_shape=pltpu.VMEM((2, rows, 2 * quarter), BF16),
+        scratch_shapes=[
+            pltpu.VMEM((ahead, rows // groups, quarter), jnp.int32),
+            pltpu.VMEM(group_scales.shape, F32),
+            pltpu.SemaphoreType.DMA((ahead,)),
+        ],
+        compiler_params=pltpu.CompilerParams(vmem_limit_bytes=8 * 1024 * 1024),
         cost_estimate=pl.CostEstimate(flops=rows * quarter * 30, bytes_accessed=rows * quarter * 12, transcendentals=0),
-    )(half, code_words, scales)
+    )(half, in_hbm(code_words), group_scales)
 
 
 def attend_kernel(first, last, blocks, tile, q_ref, *refs):
@@ -180,25 +232,22 @@
     )(queries, *kv_blocks, *(() if first else state))
 
 
-def project_kernel(x_ref, w_ref, out_ref):
-    heads = x_ref.shape[0]
-    x = jnp.concatenate([x_ref[h] for h in range(heads)], axis=1)
-    out_ref[...] = jnp.dot(x, w_ref[0], preferred_element_type=F32).astype(out_ref.dtype)
+def project_kernel(part, tile, x_ref, w_ref, out_ref):
+    x = jnp.concatenate([x_ref[h] for h in range(x_ref.shape[0])], axis=1)
+    for c in range(0, out_ref.shape[1], tile):
+        mixed = jnp.dot(x, w_ref[part, :, c : c + tile], preferred_element_type=F32)
+        out_ref[:, c : c + tile] = mixed.astype(out_ref.dtype)
 
 
 def project(part, returned, weights, out_type, tile=512):
     heads, tokens, width = returned.shape
     _, rows, columns = weights.shape
     return pl.pallas_call(
-        project_kernel,
-        grid=(columns // tile,),
-        in_specs=[
-            pl.BlockSpec((heads, tokens, width), lambda c: (0, 0, 0)),
-            pl.BlockSpec((1, rows, tile), lambda c: (part, 0, c)),
-        ],
-        out_specs=pl.BlockSpec((tokens, tile), lambda c: (0, c)),
+        functools.partial(project_kernel, part, tile),
+        in_specs=[pl.BlockSpec(memory_space=pltpu.VMEM)] * 2,
+        out_specs=pl.BlockSpec(memory_space=pltpu.VMEM),
         out_shape=jax.ShapeDtypeStruct((tokens, columns), out_type),
-        compiler_params=pltpu.CompilerParams(vmem_limit_bytes=24 * 1024 * 1024),
+        compiler_params=pltpu.CompilerParams(vmem_limit_bytes=8 * 1024 * 1024),
         cost_estimate=pl.CostEstimate(
             flops=2 * tokens * rows * columns, bytes_accessed=rows * columns * 2, transcendentals=0
         ),

time: 97.4 us -> 87.2 us (0.90)
  local copies, waits for them, and re-layouts: 14.5 us -> 0.95 us
  waiting for transfers between devices: 13 us -> 22.8 us
  Pallas kernels: 28.3 us -> 23.1 us
  starting transfers between devices: 10.3 us -> 9.15 us
    unnamed x14 -> x6, local copies, waits for them, and re-layouts: 13.4 us -> 0.92 us
    pallas_call x4, Pallas kernels: 19.6 us -> 14.4 us  [the longest x1 8.85 us: dequantize(): pl.pallas_call(dequantize_kernel, in_specs=[pl.BlockSpec(memory_space=plt...]
    ppermute x1, waiting for transfers between devices: 0.01 us -> 3.99 us  [body(): down = lax.ppermute(own, RING, [(i, (i - 1) % ring) for i in range(ring)])]
    ppermute x1, waiting for transfers between devices: 0.95 us -> 4.85 us  [body(): up = lax.ppermute(own, RING, [(i, (i + 1) % ring) for i in range(ring)])]
    ppermute x1, waiting for transfers between devices: 2.03 us -> 3.3 us  [body(): incoming = lax.ppermute(outgoing, 'yh', [(0, 1), (1, 0)])]
    ppermute x1, starting transfers between devices: 1.23 us -> 0.08 us  [body(): far = lax.ppermute(jnp.where(core == 0, up, down), (RING, 'c'), hops)]
    reshape x1 -> x0, local copies, waits for them, and re-layouts: 1.07 us -> none  [dequantize(): scales = group_scales.astype(F32).reshape(groups, 4, quarter)]
  transfers between devices with their start and end apart: 8 -> 8, of which waited for: 4 -> 5; matrix products, arithmetic and copies ran while one was open for 1% -> 0% of each run, Pallas kernels for 23% -> 20%
where the time goes in v3:
time: 87.2 us; the launch traced here: 85.5 us
  blocking collectives  28.5 us (33%)
  Pallas kernels  23.1 us (26%)
  waiting for transfers between devices  22.8 us (26%)
  starting transfers between devices  9.15 us (10%)
  local copies, waits for them, and re-layouts  0.95 us (1%)
  other arithmetic  0.9 us (1%)
    all_to_all x1, blocking collectives, body(): lax.all_to_all(prepared, HEAD_AXES, split_axis=0, concat_axis=0, tiled=True)  16.8 us
    all_to_all x1, blocking collectives, body(): lax.all_to_all(attended.reshape(chunks, -1, HD), HEAD_AXES, split_axis=0,...  11.7 us
    ppermute x1, waiting for transfers between devices, body(): far = lax.ppermute(jnp.where(core == 0, up, down), (RING, 'c'), hops)  8.89 us
    pallas_call x1, Pallas kernels, dequantize(): pl.pallas_call(dequantize_kernel, in_specs=[pl.BlockSpec(memory_space=plt...  8.85 us
    pallas_call x4, Pallas kernels, attend(): pl.pallas_call(functools.partial(attend_kernel, first, last, blocks, tile...  8.74 us
    ppermute x1, starting transfers between devices, body(): down = lax.ppermute(own, RING, [(i, (i - 1) % ring) for i in range(ring)])  5.48 us
    ppermute x1, waiting for transfers between devices, body(): up = lax.ppermute(own, RING, [(i, (i + 1) % ring) for i in range(ring)])  4.85 us
    ppermute x1, waiting for transfers between devices, body(): down = lax.ppermute(own, RING, [(i, (i - 1) % ring) for i in range(ring)])  3.99 us
  transfers between devices with their start and end apart: 8, of which 5 were waited for; matrix products, arithmetic and copies ran while one was open for 0% of the time, Pallas kernels for 20%

profile of v3, /device:TPU:6, one launch (start us, length us, event | category | flops | bytes accessed | tf_op | source)
XLA Modules:
  0.0 85.5 jit_solution(1424761044205404774)
XLA Ops:
  0.0 1.8 %shard_map.64 = bf16[16,3,48,128]{3,2,1,0:T(8,128)(2,1)S(1)} custom-call(s32[3,48]{1,0:T(4,128)} %pos_hbm.1, bf16[48,3,16,128]{3,2,1,0:T(8,128)(2,1)} %x_hbm.1), custom_call_target="tpu_custom_call" | custom-call | tf_op jit(solution)/shard_map/pallas_call | solution.py:64
  1.8 16.8 %all_to_all.10.q_ref.refs_0_ = bf16[16,3,48,128]{3,2,1,0:T(8,128)(2,1)S(1)} all-to-all(bf16[16,3,48,128]{3,2,1,0:T(8,128)(2,1)S(1)} %shard_map.64), channel_id=1, replica_groups=mesh['x'=4,'zh'=4,'zl'=2,'yl'=2,'c'=2,'yh'=2] {'x','zl','yl'}, dimensions={0} | all-to-all | bytes 1179648 | tf_op jit(solution)/shard_map/all_to_all | solution.py:265
  18.6 0.1 collective-permute-start.2
  18.7 5.5 %collective-permute-start.1 = (bf16[16,2,48,128]{3,2,1,0:T(8,128)(2,1)S(1)}, bf16[16,2,48,128]{3,2,1,0:T(8,128)(2,1)S(1)}, u32[]{:S(2)}, u32[]{:S(2)}) collective-permute-start(bf16[16,2,48,128]{3,2,1,0:T(8,128)(2,1)S(1)} %slice.4), channel_id=1, source_target_pairs={{0,48},{16,0},{32,16},{48,32},{1,49},{17,1},{33,17},{49,33},{2,50}... | collective-permute-start | bytes 1179656 | tf_op jit(solution)/shard_map/ppermute | solution.py:272
  24.1 0.0 collective-permute-start
  24.1 0.0 copy-start
  24.1 0.9 %copy-done = bf16[16,5120]{1,0:T(8,128)(2,1)S(1)} copy-done((bf16[16,5120]{1,0:T(8,128)(2,1)S(1)}, bf16[16,5120]{1,0:T(8,128)(2,1)}, u32[]{:S(2)}) %copy-start) | copy-done | bytes 163864
  25.1 8.9 %shard_map.66.w_ref = bf16[2,2048,2560]{2,1,0:T(8,128)(2,1)S(1)} custom-call(s32[1]{0:T(128)} %bitcast.half_ref, s32[2048,1280]{1,0:T(8,128)} %words_ref.1, bf16[16,5120]{1,0:T(8,128)(2,1)S(1)} %copy-done), custom_call_target="tpu_custom_call" | custom-call | flops 78643200 | bytes 31457280 | tf_op jit(solution)/shard_map/pallas_call | solution.py:135
  33.9 0.0 collective-permute-done.2.refs_1_
  33.9 2.2 %shard_map.65 = (f32[768,128]{1,0:T(8,128)S(1)}, f32[768,128]{1,0:T(8,128)S(1)}, f32[768,128]{1,0:T(8,128)S(1)}) custom-call(bf16[16,3,48,128]{3,2,1,0:T(8,128)(2,1)S(1)} %all_to_all.10.q_ref.refs_0_, bf16[16,3,48,128]{3,2,1,0:T(8,128)(2,1)S(1)} %all_to_all.10.q_ref.refs_0_, bf16[16,2,48,128]{3,2,1,0:T(8,128)(2,1)S(1)} %collective-permute-done.2.refs_1_), custom_call_target="tpu_custom_call" | custom-call | flops 603979776 | bytes 2162688 | tf_op jit(solution)/shard_map/pallas_call | solution.py:225
  36.1 4.0 %collective-permute-done.1.refs_1_ = bf16[16,2,48,128]{3,2,1,0:T(8,128)(2,1)S(1)} collective-permute-done((bf16[16,2,48,128]{3,2,1,0:T(8,128)(2,1)S(1)}, bf16[16,2,48,128]{3,2,1,0:T(8,128)(2,1)S(1)}, u32[]{:S(2)}, u32[]{:S(2)}) %collective-permute-start.1) | collective-permute-done | bytes 393248 | tf_op jit(solution)/shard_map/ppermute | solution.py:272
  40.1 4.9 %collective-permute-done.refs_0_ = bf16[16,2,48,128]{3,2,1,0:T(8,128)(2,1)S(1)} collective-permute-done((bf16[16,2,48,128]{3,2,1,0:T(8,128)(2,1)S(1)}, bf16[16,2,48,128]{3,2,1,0:T(8,128)(2,1)S(1)}, u32[]{:S(2)}, u32[]{:S(2)}) %collective-permute-start) | collective-permute-done | bytes 393248 | tf_op jit(solution)/shard_map/ppermute | solution.py:271
  45.0 0.0 collective-permute-start.4
  45.0 0.5 collective-permute-start.5
  45.5 0.1 collective-permute-start.3
  45.6 2.2 %shard_map.67 = (f32[768,128]{1,0:T(8,128)S(1)}, f32[768,128]{1,0:T(8,128)S(1)}, f32[768,128]{1,0:T(8,128)S(1)}) custom-call(bf16[16,3,48,128]{3,2,1,0:T(8,128)(2,1)S(1)} %all_to_all.10.q_ref.refs_0_, bf16[16,2,48,128]{3,2,1,0:T(8,128)(2,1)S(1)} %collective-permute-done.refs_0_, bf16[16,2,48,128]{3,2,1,0:T(8,128)(2,1)S(1)} %collective-permute-done.1.refs_1_, ...), custom_call_target="tpu_custom_call" | custom-call | flops 603979776 | bytes 2162688 | tf_op jit(solution)/shard_map/pallas_call | solution.py:225
  47.8 0.0 collective-permute-done.4.refs_0_
  47.8 0.0 collective-permute-done.5.refs_1_
  47.8 2.2 %shard_map.68 = (f32[768,128]{1,0:T(8,128)S(1)}, f32[768,128]{1,0:T(8,128)S(1)}, f32[768,128]{1,0:T(8,128)S(1)}) custom-call(bf16[16,3,48,128]{3,2,1,0:T(8,128)(2,1)S(1)} %all_to_all.10.q_ref.refs_0_, bf16[16,2,48,128]{3,2,1,0:T(8,128)(2,1)S(1)} %collective-permute-done.4.refs_0_, bf16[16,2,48,128]{3,2,1,0:T(8,128)(2,1)S(1)} %collective-permute-done.5.refs_1_, ...), custom_call_target="tpu_custom_call" | custom-call | flops 603979776 | bytes 2162688 | tf_op jit(solution)/shard_map/pallas_call | solution.py:225
  50.0 8.9 %collective-permute-done.3.refs_0_ = bf16[16,2,48,128]{3,2,1,0:T(8,128)(2,1)S(1)} collective-permute-done((bf16[16,2,48,128]{3,2,1,0:T(8,128)(2,1)S(1)}, bf16[16,2,48,128]{3,2,1,0:T(8,128)(2,1)S(1)}, u32[]{:S(2)}, u32[]{:S(2)}) %collective-permute-start.3) | collective-permute-done | bytes 393248 | tf_op jit(solution)/shard_map/ppermute | solution.py:282
  58.9 0.0 collective-permute-start.6
  58.9 1.7 %collective-permute-done.6.refs_1_ = bf16[16,2,48,128]{3,2,1,0:T(8,128)(2,1)S(1)} collective-permute-done((bf16[16,2,48,128]{3,2,1,0:T(8,128)(2,1)S(1)}, bf16[16,2,48,128]{3,2,1,0:T(8,128)(2,1)S(1)}, u32[]{:S(2)}, u32[]{:S(2)}) %collective-permute-start.6) | collective-permute-done | bytes 393248 | tf_op jit(solution)/shard_map/ppermute | solution.py:269
  60.6 2.2 %shard_map.69 = bf16[768,128]{1,0:T(8,128)(2,1)S(1)} custom-call(bf16[16,3,48,128]{3,2,1,0:T(8,128)(2,1)S(1)} %all_to_all.10.q_ref.refs_0_, bf16[16,2,48,128]{3,2,1,0:T(8,128)(2,1)S(1)} %collective-permute-done.3.refs_0_, bf16[16,2,48,128]{3,2,1,0:T(8,128)(2,1)S(1)} %collective-permute-done.6.refs_1_, f32[768,128]{1,0:T(8,128)S(1)} %get-tuple-element.39.refs_2_, ...), custom_call_target="tpu_custom_call" | custom-call | flops 603979776 | bytes 2162688 | tf_op jit(solution)/shard_map/pallas_call | solution.py:225
  62.8 11.7 %all_to_all.11.x_ref = bf16[16,48,128]{2,1,0:T(8,128)(2,1)S(1)} all-to-all(bf16[16,48,128]{2,1,0:T(8,128)(2,1)S(1)} %bitcast.2), channel_id=1, replica_groups=mesh['x'=4,'zh'=4,'zl'=2,'yl'=2,'c'=2,'yh'=2] {'x','zl','yl'}, dimensions={0} | all-to-all | bytes 393216 | tf_op jit(solution)/shard_map/all_to_all | solution.py:290
  74.6 0.0 copy-start.1
  74.6 0.0 copy-start.2
  74.6 1.9 %shard_map.71 = bf16[48,2560]{1,0:T(8,128)(2,1)S(1)} custom-call(bf16[16,48,128]{2,1,0:T(8,128)(2,1)S(1)} %all_to_all.11.x_ref, bf16[2,2048,2560]{2,1,0:T(8,128)(2,1)S(1)} %shard_map.66.w_ref), custom_call_target="tpu_custom_call" | custom-call | flops 503316480 | bytes 10485760 | tf_op jit(solution)/shard_map/pallas_call | solution.py:245
  76.5 3.0 %collective-permute-start.7 = (bf16[48,2560]{1,0:T(8,128)(2,1)S(1)}, bf16[48,2560]{1,0:T(8,128)(2,1)S(1)}, u32[]{:S(2)}, u32[]{:S(2)}) collective-permute-start(bf16[48,2560]{1,0:T(8,128)(2,1)S(1)} %shard_map.71), channel_id=1, source_target_pairs={{0,1},{1,0},{2,3},{3,2},{4,5},{5,4},{6,7},{7,6},{8,9},{9,8},{10,11... | collective-permute-start | bytes 737288 | tf_op jit(solution)/shard_map/ppermute | solution.py:294
  79.4 1.9 %shard_map.70 = f32[48,2560]{1,0:T(8,128)S(1)} custom-call(bf16[16,48,128]{2,1,0:T(8,128)(2,1)S(1)} %all_to_all.11.x_ref, bf16[2,2048,2560]{2,1,0:T(8,128)(2,1)S(1)} %shard_map.66.w_ref), custom_call_target="tpu_custom_call" | custom-call | flops 503316480 | bytes 10485760 | tf_op jit(solution)/shard_map/pallas_call | solution.py:245
  81.3 3.3 %collective-permute-done.7 = bf16[48,2560]{1,0:T(8,128)(2,1)S(1)} collective-permute-done((bf16[48,2560]{1,0:T(8,128)(2,1)S(1)}, bf16[48,2560]{1,0:T(8,128)(2,1)S(1)}, u32[]{:S(2)}, u32[]{:S(2)}) %collective-permute-start.7) | collective-permute-done | bytes 245792 | tf_op jit(solution)/shard_map/ppermute | solution.py:294
  84.6 0.0 copy-done.1
  84.6 0.0 copy-done.2
  84.6 0.9 %add_multiply_fusion = f32[48,2560]{1,0:T(8,128)} fusion(f32[48,2560]{1,0:T(8,128)S(1)} %shard_map.70, bf16[48,2560]{1,0:T(8,128)(2,1)S(1)} %collective-permute-done.7, f32[2560]{0:T(1024)S(1)} %copy-done.1, f32[2560]{0:T(1024)S(1)} %copy-done.2), kind=kLoop, calls=%fused_computation | loop fusion | flops 491520 | bytes 1249280 | tf_op jit(solution)/shard_map/mul | solution.py:296
  (2 shorter events, 0.1 us)
Async XLA Ops:
  18.6 15.4 %collective-permute-start.2 = (bf16[16,2,48,128]{3,2,1,0:T(8,128)(2,1)S(1)}, bf16[16,2,48,128]{3,2,1,0:T(8,128)(2,1)S(1)}, u32[]{:S(2)}, u32[]{:S(2)}) collective-permute-start(bf16[16,2,48,128]{3,2,1,0:T(8,128)(2,1)S(1)} %slice.4), channel_id=1, source_target_pairs={{0,2},{2,0},{1,3},{3,1},{4,6},{6,4},{5,7},{7,5},{8,10},{10,8},{9,1... | collective-permute-start | bytes 1179656 | tf_op jit(solution)/shard_map/ppermute | solution.py:269
  18.7 21.5 %collective-permute-start.1 = (bf16[16,2,48,128]{3,2,1,0:T(8,128)(2,1)S(1)}, bf16[16,2,48,128]{3,2,1,0:T(8,128)(2,1)S(1)}, u32[]{:S(2)}, u32[]{:S(2)}) collective-permute-start(bf16[16,2,48,128]{3,2,1,0:T(8,128)(2,1)S(1)} %slice.4), channel_id=1, source_target_pairs={{0,48},{16,0},{32,16},{48,32},{1,49},{17,1},{33,17},{49,33},{2,50}... | collective-permute-start | bytes 1179656 | tf_op jit(solution)/shard_map/ppermute | solution.py:272
  24.1 20.8 %collective-permute-start = (bf16[16,2,48,128]{3,2,1,0:T(8,128)(2,1)S(1)}, bf16[16,2,48,128]{3,2,1,0:T(8,128)(2,1)S(1)}, u32[]{:S(2)}, u32[]{:S(2)}) collective-permute-start(bf16[16,2,48,128]{3,2,1,0:T(8,128)(2,1)S(1)} %slice.4), channel_id=1, source_target_pairs={{0,16},{16,32},{32,48},{48,0},{1,17},{17,33},{33,49},{49,1},{2,18}... | collective-permute-start | bytes 1179656 | tf_op jit(solution)/shard_map/ppermute | solution.py:271
  24.1 0.9 %copy-start = (bf16[16,5120]{1,0:T(8,128)(2,1)S(1)}, bf16[16,5120]{1,0:T(8,128)(2,1)}, u32[]{:S(2)}) copy-start(bf16[16,5120]{1,0:T(8,128)(2,1)} %scales_ref.1) | copy-start | bytes 491524
  45.0 2.8 %collective-permute-start.4 = (bf16[16,2,48,128]{3,2,1,0:T(8,128)(2,1)S(1)}, bf16[16,2,48,128]{3,2,1,0:T(8,128)(2,1)S(1)}, u32[]{:S(2)}, u32[]{:S(2)}) collective-permute-start(bf16[16,2,48,128]{3,2,1,0:T(8,128)(2,1)S(1)} %collective-permute-done.refs_0_), channel_id=1, source_target_pairs={{0,2},{2,0},{1,3},{3,1},{4,6},{6,4},{5,7},{7,5},{8,10},{10,8},{9,1... | collective-permute-start | bytes 1179656 | tf_op jit(solution)/shard_map/ppermute | solution.py:269
  45.0 2.8 %collective-permute-start.5 = (bf16[16,2,48,128]{3,2,1,0:T(8,128)(2,1)S(1)}, bf16[16,2,48,128]{3,2,1,0:T(8,128)(2,1)S(1)}, u32[]{:S(2)}, u32[]{:S(2)}) collective-permute-start(bf16[16,2,48,128]{3,2,1,0:T(8,128)(2,1)S(1)} %collective-permute-done.1.refs_1_), channel_id=1, source_target_pairs={{0,2},{2,0},{1,3},{3,1},{4,6},{6,4},{5,7},{7,5},{8,10},{10,8},{9,1... | collective-permute-start | bytes 1179656 | tf_op jit(solution)/shard_map/ppermute | solution.py:269
  45.5 13.3 %collective-permute-start.3 = (bf16[16,2,48,128]{3,2,1,0:T(8,128)(2,1)S(1)}, bf16[16,2,48,128]{3,2,1,0:T(8,128)(2,1)S(1)}, u32[]{:S(2)}, u32[]{:S(2)}) collective-permute-start(bf16[16,2,48,128]{3,2,1,0:T(8,128)(2,1)S(1)} %broadcast_select_fusion), channel_id=1, source_target_pairs={{0,16},{2,50},{16,32},{18,2},{32,48},{34,18},{48,0},{50,34},{1,17}... | collective-permute-start | bytes 1179656 | tf_op jit(solution)/shard_map/ppermute | solution.py:282
  58.9 1.7 %collective-permute-start.6 = (bf16[16,2,48,128]{3,2,1,0:T(8,128)(2,1)S(1)}, bf16[16,2,48,128]{3,2,1,0:T(8,128)(2,1)S(1)}, u32[]{:S(2)}, u32[]{:S(2)}) collective-permute-start(bf16[16,2,48,128]{3,2,1,0:T(8,128)(2,1)S(1)} %collective-permute-done.3.refs_0_), channel_id=1, source_target_pairs={{0,2},{2,0},{1,3},{3,1},{4,6},{6,4},{5,7},{7,5},{8,10},{10,8},{9,1... | collective-permute-start | bytes 1179656 | tf_op jit(solution)/shard_map/ppermute | solution.py:269
  74.6 10.1 %copy-start.1 = (f32[2560]{0:T(1024)S(1)}, f32[2560]{0:T(1024)}, u32[]{:S(2)}) copy-start(f32[2560]{0:T(1024)} %param.11) | copy-start | bytes 30724
  74.6 10.1 %copy-start.2 = (f32[2560]{0:T(1024)S(1)}, f32[2560]{0:T(1024)}, u32[]{:S(2)}) copy-start(f32[2560]{0:T(1024)} %param.10) | copy-start | bytes 30724
  76.5 8.2 %collective-permute-start.7 = (bf16[48,2560]{1,0:T(8,128)(2,1)S(1)}, bf16[48,2560]{1,0:T(8,128)(2,1)S(1)}, u32[]{:S(2)}, u32[]{:S(2)}) collective-permute-start(bf16[48,2560]{1,0:T(8,128)(2,1)S(1)} %shard_map.71), channel_id=1, source_target_pairs={{0,1},{1,0},{2,3},{3,2},{4,5},{5,4},{6,7},{7,6},{8,9},{9,8},{10,11... | collective-permute-start | bytes 737288 | tf_op jit(solution)/shard_map/ppermute | solution.py:294

commit v4 on v3

--- a/solution.py
+++ b/solution.py
@@ -151,9 +151,9 @@
     )(half, in_hbm(code_words), group_scales)
 
 
-def attend_kernel(first, last, blocks, tile, q_ref, *refs):
+def attend_kernel(first, last, blocks, after, tile, q_ref, *refs):
     kv_refs = refs[:blocks]
-    refs = refs[blocks:]
+    refs = refs[blocks + after :]
     if not first:
         m_in, l_in, acc_in = refs[:3]
         refs = refs[3:]
@@ -164,8 +164,9 @@
     keys, values = [], []
     for ref in kv_refs:
         at = ref.shape[1] - 2
-        keys.append(ref[:, at].reshape(total, width))
-        values.append(ref[:, at + 1].reshape(total, width))
+        count = ref.shape[0] * rows
+        keys.append(ref[:, at].reshape(count, width))
+        values.append(ref[:, at + 1].reshape(count, width))
 
     def scores(step):
         row, block = divmod(step, blocks)
@@ -190,7 +191,7 @@
         s_peak = jnp.broadcast_to(jnp.max(s, axis=1, keepdims=True), (tile, width))
         new_peak = s_peak if fresh else jnp.maximum(peak, s_peak)
         parts, part_sum = [], None
-        for lane in range(total // width):
+        for lane in range(s.shape[1] // width):
             lifted = jnp.exp2((s[:, lane * width : (lane + 1) * width] - new_peak) * scale)
             part_sum = lifted if part_sum is None else part_sum + lifted
             parts.append(lifted.astype(BF16))
@@ -214,22 +215,22 @@
                 acc_out[here, :] = acc
 
 
-def attend(queries, kv_blocks, state, last, tile=128):
+def attend(queries, kv_blocks, state, last=False, after=(), tile=128):
     groups, _, rows, width = queries.shape
     total = groups * rows
     blocks = len(kv_blocks)
     first = state is None
     carried = jax.ShapeDtypeStruct((total, width), F32)
     out_shape = jax.ShapeDtypeStruct((total, width), BF16) if last else (carried,) * 3
-    pairs = total * total * blocks
+    pairs = total * sum(block.shape[0] * rows for block in kv_blocks)
     return pl.pallas_call(
-        functools.partial(attend_kernel, first, last, blocks, tile),
+        functools.partial(attend_kernel, first, last, blocks, len(after), tile),
         out_shape=out_shape,
         compiler_params=pltpu.CompilerParams(vmem_limit_bytes=16 * 1024 * 1024),
         cost_estimate=pl.CostEstimate(
             flops=pairs * width * 4, bytes_accessed=total * width * 2 * (2 * blocks + 7), transcendentals=pairs
         ),
-    )(queries, *kv_blocks, *(() if first else state))
+    )(queries, *kv_blocks, *after, *(() if first else state))
 
 
 def project_kernel(part, tile, x_ref, w_ref, out_ref):
@@ -268,24 +269,28 @@
     def swap(a):
         return lax.ppermute(a, "c", [(0, 1), (1, 0)])
 
-    up = lax.ppermute(own, RING, [(i, (i + 1) % ring) for i in range(ring)])
-    down = lax.ppermute(own, RING, [(i, (i - 1) % ring) for i in range(ring)])
+    def send(a, way):
+        hops = []
+        for i in range(ring):
+            hops.append((2 * i, 2 * ((i + way) % ring)))
+            hops.append((2 * i + 1, 2 * ((i - way) % ring) + 1))
+        return lax.ppermute(a, (RING, "c"), hops)
+
+    near = send(own, 1)
+    back = send(own, -1)
     beside = swap(own)
     weights = dequantize(half, code_words, group_scales)
-    state = attend(grouped, [grouped, beside], None, False)
-    up, down, state, weights = lax.optimization_barrier((up, down, state, weights))
-    core = lax.axis_index("c")
-    hops = []
-    for i in range(ring):
-        hops.append((2 * i, 2 * ((i + 1) % ring)))
-        hops.append((2 * i + 1, 2 * ((i - 1) % ring) + 1))
-    far = lax.ppermute(jnp.where(core == 0, up, down), (RING, "c"), hops)
-    up_beside, down_beside = swap(up), swap(down)
-    state = attend(grouped, [up, down], state, False)
-    state = attend(grouped, [up_beside, down_beside], state, False)
+    state = attend(grouped, [grouped, beside], None, after=(weights,))
+    near, back, state = lax.optimization_barrier((near, back, state))
+    far = send(near, 1)
+    near_beside = swap(near)
+    back_beside = swap(back)
+    state = attend(grouped, [near, back], state)
+    state = attend(grouped, [near_beside, back_beside], state)
     far, state = lax.optimization_barrier((far, state))
     far_beside = swap(far)
-    attended = attend(grouped, [far, far_beside], state, True)
+    state = attend(grouped, [far], state)
+    attended = attend(grouped, [far_beside], state, True)
     chunks = prepared.shape[0]
     returned = lax.all_to_all(
         attended.reshape(chunks, -1, HD), HEAD_AXES, split_axis=0, concat_axis=0, tiled=True

time: 87.2 us -> 82.2 us (0.943)
  the two profiles are of different devices: /device:TPU:6 before, /device:TPU:16 now
where the time goes in v4:
time: 82.2 us; the launch traced here: 82 us
  blocking collectives  29.4 us (36%)
  Pallas kernels  23.4 us (28%)
  waiting for transfers between devices  18.5 us (23%)
  starting transfers between devices  8.76 us (11%)
  local copies, waits for them, and re-layouts  0.95 us (1%)
  other arithmetic  0.85 us (1%)
    all_to_all x1, blocking collectives, body(): lax.all_to_all(prepared, HEAD_AXES, split_axis=0, concat_axis=0, tiled=True)  18.1 us
    ppermute x3, waiting for transfers between devices, send(): return lax.ppermute(a, (RING, 'c'), hops)  12.4 us
    all_to_all x1, blocking collectives, body(): lax.all_to_all(attended.reshape(chunks, -1, HD), HEAD_AXES, split_axis=0,...  11.3 us
    pallas_call x5, Pallas kernels, attend(): pl.pallas_call(functools.partial(attend_kernel, first, last, blocks, len(...  9.05 us
    pallas_call x1, Pallas kernels, dequantize(): pl.pallas_call(dequantize_kernel, in_specs=[pl.BlockSpec(memory_space=plt...  8.85 us
    ppermute x3, starting transfers between devices, send(): return lax.ppermute(a, (RING, 'c'), hops)  7.44 us
    ppermute x1, waiting for transfers between devices, body(): incoming = lax.ppermute(outgoing, 'yh', [(0, 1), (1, 0)])  5.71 us
    pallas_call x2, Pallas kernels, project(): pl.pallas_call(functools.partial(project_kernel, part, tile), in_specs=[p...  3.76 us
  transfers between devices with their start and end apart: 8, of which 5 were waited for; matrix products, arithmetic and copies ran while one was open for 0% of the time, Pallas kernels for 23%

profile of v4, /device:TPU:16, one launch (start us, length us, event | category | flops | bytes accessed | tf_op | source)
XLA Modules:
  0.0 82.0 jit_solution(197018659966691804)
XLA Ops:
  0.0 1.8 %shard_map.64 = bf16[16,3,48,128]{3,2,1,0:T(8,128)(2,1)S(1)} custom-call(s32[3,48]{1,0:T(4,128)} %pos_hbm.1, bf16[48,3,16,128]{3,2,1,0:T(8,128)(2,1)} %x_hbm.1), custom_call_target="tpu_custom_call" | custom-call | tf_op jit(solution)/shard_map/pallas_call | solution.py:64
  1.8 18.1 %all_to_all.10.q_ref.refs_0_ = bf16[16,3,48,128]{3,2,1,0:T(8,128)(2,1)S(1)} all-to-all(bf16[16,3,48,128]{3,2,1,0:T(8,128)(2,1)S(1)} %shard_map.64), channel_id=1, replica_groups=mesh['x'=4,'zh'=4,'zl'=2,'yl'=2,'c'=2,'yh'=2] {'x','zl','yl'}, dimensions={0} | all-to-all | bytes 1179648 | tf_op jit(solution)/shard_map/all_to_all | solution.py:266
  19.9 0.1 collective-permute-start.2
  20.0 5.5 %collective-permute-start.1 = (bf16[16,2,48,128]{3,2,1,0:T(8,128)(2,1)S(1)}, bf16[16,2,48,128]{3,2,1,0:T(8,128)(2,1)S(1)}, u32[]{:S(2)}, u32[]{:S(2)}) collective-permute-start(bf16[16,2,48,128]{3,2,1,0:T(8,128)(2,1)S(1)} %slice.4), channel_id=1, source_target_pairs={{0,48},{2,18},{16,0},{18,34},{32,16},{34,50},{48,32},{50,2},{1,49}... | collective-permute-start | bytes 1179656 | tf_op jit(solution)/shard_map/ppermute | solution.py:277
  25.4 0.0 collective-permute-start
  25.4 0.0 copy-start
  25.4 0.9 %copy-done = bf16[16,5120]{1,0:T(8,128)(2,1)S(1)} copy-done((bf16[16,5120]{1,0:T(8,128)(2,1)S(1)}, bf16[16,5120]{1,0:T(8,128)(2,1)}, u32[]{:S(2)}) %copy-start) | copy-done | bytes 163864
  26.4 8.9 %shard_map.65.refs_2_.w_ref = bf16[2,2048,2560]{2,1,0:T(8,128)(2,1)S(1)} custom-call(s32[1]{0:T(128)} %bitcast.half_ref, s32[2048,1280]{1,0:T(8,128)} %words_ref.1, bf16[16,5120]{1,0:T(8,128)(2,1)S(1)} %copy-done), custom_call_target="tpu_custom_call" | custom-call | flops 78643200 | bytes 31457280 | tf_op jit(solution)/shard_map/pallas_call | solution.py:135
  35.2 0.0 collective-permute-done.2.refs_1_
  35.2 2.2 %shard_map.66 = (f32[768,128]{1,0:T(8,128)S(1)}, f32[768,128]{1,0:T(8,128)S(1)}, f32[768,128]{1,0:T(8,128)S(1)}) custom-call(bf16[16,3,48,128]{3,2,1,0:T(8,128)(2,1)S(1)} %all_to_all.10.q_ref.refs_0_, bf16[16,3,48,128]{3,2,1,0:T(8,128)(2,1)S(1)} %all_to_all.10.q_ref.refs_0_, bf16[16,2,48,128]{3,2,1,0:T(8,128)(2,1)S(1)} %collective-permute-done.2.refs_1_, ...), custom_call_target="tpu_custom_call" | custom-call | flops 603979776 | bytes 2162688 | tf_op jit(solution)/shard_map/pallas_call | solution.py:226
  37.5 4.1 %collective-permute-done.1.refs_1_ = bf16[16,2,48,128]{3,2,1,0:T(8,128)(2,1)S(1)} collective-permute-done((bf16[16,2,48,128]{3,2,1,0:T(8,128)(2,1)S(1)}, bf16[16,2,48,128]{3,2,1,0:T(8,128)(2,1)S(1)}, u32[]{:S(2)}, u32[]{:S(2)}) %collective-permute-start.1) | collective-permute-done | bytes 393248 | tf_op jit(solution)/shard_map/ppermute | solution.py:277
  41.5 2.0 %collective-permute-done.refs_0_ = bf16[16,2,48,128]{3,2,1,0:T(8,128)(2,1)S(1)} collective-permute-done((bf16[16,2,48,128]{3,2,1,0:T(8,128)(2,1)S(1)}, bf16[16,2,48,128]{3,2,1,0:T(8,128)(2,1)S(1)}, u32[]{:S(2)}, u32[]{:S(2)}) %collective-permute-start) | collective-permute-done | bytes 393248 | tf_op jit(solution)/shard_map/ppermute | solution.py:277
  43.6 0.0 collective-permute-start.5
  43.6 0.5 collective-permute-start.4
  44.1 2.0 %collective-permute-start.3 = (bf16[16,2,48,128]{3,2,1,0:T(8,128)(2,1)S(1)}, bf16[16,2,48,128]{3,2,1,0:T(8,128)(2,1)S(1)}, u32[]{:S(2)}, u32[]{:S(2)}) collective-permute-start(bf16[16,2,48,128]{3,2,1,0:T(8,128)(2,1)S(1)} %collective-permute-done.refs_0_), channel_id=1, source_target_pairs={{0,16},{2,50},{16,32},{18,2},{32,48},{34,18},{48,0},{50,34},{1,17}... | collective-permute-start | bytes 1179656 | tf_op jit(solution)/shard_map/ppermute | solution.py:277
  46.0 2.1 %shard_map.67 = (f32[768,128]{1,0:T(8,128)S(1)}, f32[768,128]{1,0:T(8,128)S(1)}, f32[768,128]{1,0:T(8,128)S(1)}) custom-call(bf16[16,3,48,128]{3,2,1,0:T(8,128)(2,1)S(1)} %all_to_all.10.q_ref.refs_0_, bf16[16,2,48,128]{3,2,1,0:T(8,128)(2,1)S(1)} %collective-permute-done.refs_0_, bf16[16,2,48,128]{3,2,1,0:T(8,128)(2,1)S(1)} %collective-permute-done.1.refs_1_, ...), custom_call_target="tpu_custom_call" | custom-call | flops 603979776 | bytes 2162688 | tf_op jit(solution)/shard_map/pallas_call | solution.py:226
  48.2 0.0 collective-permute-done.5.refs_1_
  48.2 0.0 collective-permute-done.4.refs_0_
  48.2 2.2 %shard_map.68 = (f32[768,128]{1,0:T(8,128)S(1)}, f32[768,128]{1,0:T(8,128)S(1)}, f32[768,128]{1,0:T(8,128)S(1)}) custom-call(bf16[16,3,48,128]{3,2,1,0:T(8,128)(2,1)S(1)} %all_to_all.10.q_ref.refs_0_, bf16[16,2,48,128]{3,2,1,0:T(8,128)(2,1)S(1)} %collective-permute-done.4.refs_0_, bf16[16,2,48,128]{3,2,1,0:T(8,128)(2,1)S(1)} %collective-permute-done.5.refs_1_, ...), custom_call_target="tpu_custom_call" | custom-call | flops 603979776 | bytes 2162688 | tf_op jit(solution)/shard_map/pallas_call | solution.py:226
  50.4 6.3 %collective-permute-done.3.refs_0_ = bf16[16,2,48,128]{3,2,1,0:T(8,128)(2,1)S(1)} collective-permute-done((bf16[16,2,48,128]{3,2,1,0:T(8,128)(2,1)S(1)}, bf16[16,2,48,128]{3,2,1,0:T(8,128)(2,1)S(1)}, u32[]{:S(2)}, u32[]{:S(2)}) %collective-permute-start.3) | collective-permute-done | bytes 393248 | tf_op jit(solution)/shard_map/ppermute | solution.py:277
  56.6 0.0 collective-permute-start.6
  56.6 1.3 %shard_map.69 = (f32[768,128]{1,0:T(8,128)S(1)}, f32[768,128]{1,0:T(8,128)S(1)}, f32[768,128]{1,0:T(8,128)S(1)}) custom-call(bf16[16,3,48,128]{3,2,1,0:T(8,128)(2,1)S(1)} %all_to_all.10.q_ref.refs_0_, bf16[16,2,48,128]{3,2,1,0:T(8,128)(2,1)S(1)} %collective-permute-done.3.refs_0_, f32[768,128]{1,0:T(8,128)S(1)} %get-tuple-element.41.refs_1_, ...), custom_call_target="tpu_custom_call" | custom-call | flops 301989888 | bytes 1769472 | tf_op jit(solution)/shard_map/pallas_call | solution.py:226
  57.9 0.4 collective-permute-done.6.refs_0_
  58.4 1.3 %shard_map.70 = bf16[768,128]{1,0:T(8,128)(2,1)S(1)} custom-call(bf16[16,3,48,128]{3,2,1,0:T(8,128)(2,1)S(1)} %all_to_all.10.q_ref.refs_0_, bf16[16,2,48,128]{3,2,1,0:T(8,128)(2,1)S(1)} %collective-permute-done.6.refs_0_, f32[768,128]{1,0:T(8,128)S(1)} %get-tuple-element.44.refs_1_, f32[768,128]{1,0:T(8,128)S(1)} %get-tuple-element.45.refs_2_, ...), custom_call_target="tpu_custom_call" | custom-call | flops 301989888 | bytes 1769472 | tf_op jit(solution)/shard_map/pallas_call | solution.py:226
  59.6 11.3 %all_to_all.11.x_ref = bf16[16,48,128]{2,1,0:T(8,128)(2,1)S(1)} all-to-all(bf16[16,48,128]{2,1,0:T(8,128)(2,1)S(1)} %bitcast.2), channel_id=1, replica_groups=mesh['x'=4,'zh'=4,'zl'=2,'yl'=2,'c'=2,'yh'=2] {'x','zl','yl'}, dimensions={0} | all-to-all | bytes 393216 | tf_op jit(solution)/shard_map/all_to_all | solution.py:295
  70.9 0.0 copy-start.1
  70.9 0.0 copy-start.2
  70.9 1.9 %shard_map.72 = bf16[48,2560]{1,0:T(8,128)(2,1)S(1)} custom-call(bf16[16,48,128]{2,1,0:T(8,128)(2,1)S(1)} %all_to_all.11.x_ref, bf16[2,2048,2560]{2,1,0:T(8,128)(2,1)S(1)} %shard_map.65.refs_2_.w_ref), custom_call_target="tpu_custom_call" | custom-call | flops 503316480 | bytes 10485760 | tf_op jit(solution)/shard_map/pallas_call | solution.py:246
  72.8 0.7 collective-permute-start.7
  73.5 1.9 %shard_map.71 = f32[48,2560]{1,0:T(8,128)S(1)} custom-call(bf16[16,48,128]{2,1,0:T(8,128)(2,1)S(1)} %all_to_all.11.x_ref, bf16[2,2048,2560]{2,1,0:T(8,128)(2,1)S(1)} %shard_map.65.refs_2_.w_ref), custom_call_target="tpu_custom_call" | custom-call | flops 503316480 | bytes 10485760 | tf_op jit(solution)/shard_map/pallas_call | solution.py:246
  75.4 5.7 %collective-permute-done.7 = bf16[48,2560]{1,0:T(8,128)(2,1)S(1)} collective-permute-done((bf16[48,2560]{1,0:T(8,128)(2,1)S(1)}, bf16[48,2560]{1,0:T(8,128)(2,1)S(1)}, u32[]{:S(2)}, u32[]{:S(2)}) %collective-permute-start.7) | collective-permute-done | bytes 245792 | tf_op jit(solution)/shard_map/ppermute | solution.py:299
  81.1 0.0 copy-done.1
  81.1 0.0 copy-done.2
  81.1 0.8 %add_multiply_fusion = f32[48,2560]{1,0:T(8,128)} fusion(f32[48,2560]{1,0:T(8,128)S(1)} %shard_map.71, bf16[48,2560]{1,0:T(8,128)(2,1)S(1)} %collective-permute-done.7, f32[2560]{0:T(1024)S(1)} %copy-done.1, f32[2560]{0:T(1024)S(1)} %copy-done.2), kind=kLoop, calls=%fused_computation | loop fusion | flops 491520 | bytes 1249280 | tf_op jit(solution)/shard_map/mul | solution.py:301
  (1 shorter events, 0.0 us)
Async XLA Ops:
  19.9 15.4 %collective-permute-start.2 = (bf16[16,2,48,128]{3,2,1,0:T(8,128)(2,1)S(1)}, bf16[16,2,48,128]{3,2,1,0:T(8,128)(2,1)S(1)}, u32[]{:S(2)}, u32[]{:S(2)}) collective-permute-start(bf16[16,2,48,128]{3,2,1,0:T(8,128)(2,1)S(1)} %slice.4), channel_id=1, source_target_pairs={{0,2},{2,0},{1,3},{3,1},{4,6},{6,4},{5,7},{7,5},{8,10},{10,8},{9,1... | collective-permute-start | bytes 1179656 | tf_op jit(solution)/shard_map/ppermute | solution.py:270
  20.0 21.6 %collective-permute-start.1 = (bf16[16,2,48,128]{3,2,1,0:T(8,128)(2,1)S(1)}, bf16[16,2,48,128]{3,2,1,0:T(8,128)(2,1)S(1)}, u32[]{:S(2)}, u32[]{:S(2)}) collective-permute-start(bf16[16,2,48,128]{3,2,1,0:T(8,128)(2,1)S(1)} %slice.4), channel_id=1, source_target_pairs={{0,48},{2,18},{16,0},{18,34},{32,16},{34,50},{48,32},{50,2},{1,49}... | collective-permute-start | bytes 1179656 | tf_op jit(solution)/shard_map/ppermute | solution.py:277
  25.4 18.1 %collective-permute-start = (bf16[16,2,48,128]{3,2,1,0:T(8,128)(2,1)S(1)}, bf16[16,2,48,128]{3,2,1,0:T(8,128)(2,1)S(1)}, u32[]{:S(2)}, u32[]{:S(2)}) collective-permute-start(bf16[16,2,48,128]{3,2,1,0:T(8,128)(2,1)S(1)} %slice.4), channel_id=1, source_target_pairs={{0,16},{2,50},{16,32},{18,2},{32,48},{34,18},{48,0},{50,34},{1,17}... | collective-permute-start | bytes 1179656 | tf_op jit(solution)/shard_map/ppermute | solution.py:277
  25.4 0.9 %copy-start = (bf16[16,5120]{1,0:T(8,128)(2,1)S(1)}, bf16[16,5120]{1,0:T(8,128)(2,1)}, u32[]{:S(2)}) copy-start(bf16[16,5120]{1,0:T(8,128)(2,1)} %scales_ref.1) | copy-start | bytes 491524
  43.6 4.6 %collective-permute-start.5 = (bf16[16,2,48,128]{3,2,1,0:T(8,128)(2,1)S(1)}, bf16[16,2,48,128]{3,2,1,0:T(8,128)(2,1)S(1)}, u32[]{:S(2)}, u32[]{:S(2)}) collective-permute-start(bf16[16,2,48,128]{3,2,1,0:T(8,128)(2,1)S(1)} %collective-permute-done.1.refs_1_), channel_id=1, source_target_pairs={{0,2},{2,0},{1,3},{3,1},{4,6},{6,4},{5,7},{7,5},{8,10},{10,8},{9,1... | collective-permute-start | bytes 1179656 | tf_op jit(solution)/shard_map/ppermute | solution.py:270
  43.6 4.6 %collective-permute-start.4 = (bf16[16,2,48,128]{3,2,1,0:T(8,128)(2,1)S(1)}, bf16[16,2,48,128]{3,2,1,0:T(8,128)(2,1)S(1)}, u32[]{:S(2)}, u32[]{:S(2)}) collective-permute-start(bf16[16,2,48,128]{3,2,1,0:T(8,128)(2,1)S(1)} %collective-permute-done.refs_0_), channel_id=1, source_target_pairs={{0,2},{2,0},{1,3},{3,1},{4,6},{6,4},{5,7},{7,5},{8,10},{10,8},{9,1... | collective-permute-start | bytes 1179656 | tf_op jit(solution)/shard_map/ppermute | solution.py:270
  44.1 12.5 %collective-permute-start.3 = (bf16[16,2,48,128]{3,2,1,0:T(8,128)(2,1)S(1)}, bf16[16,2,48,128]{3,2,1,0:T(8,128)(2,1)S(1)}, u32[]{:S(2)}, u32[]{:S(2)}) collective-permute-start(bf16[16,2,48,128]{3,2,1,0:T(8,128)(2,1)S(1)} %collective-permute-done.refs_0_), channel_id=1, source_target_pairs={{0,16},{2,50},{16,32},{18,2},{32,48},{34,18},{48,0},{50,34},{1,17}... | collective-permute-start | bytes 1179656 | tf_op jit(solution)/shard_map/ppermute | solution.py:277
  56.6 1.7 %collective-permute-start.6 = (bf16[16,2,48,128]{3,2,1,0:T(8,128)(2,1)S(1)}, bf16[16,2,48,128]{3,2,1,0:T(8,128)(2,1)S(1)}, u32[]{:S(2)}, u32[]{:S(2)}) collective-permute-start(bf16[16,2,48,128]{3,2,1,0:T(8,128)(2,1)S(1)} %collective-permute-done.3.refs_0_), channel_id=1, source_target_pairs={{0,2},{2,0},{1,3},{3,1},{4,6},{6,4},{5,7},{7,5},{8,10},{10,8},{9,1... | collective-permute-start | bytes 1179656 | tf_op jit(solution)/shard_map/ppermute | solution.py:270
  70.9 10.2 %copy-start.1 = (f32[2560]{0:T(1024)S(1)}, f32[2560]{0:T(1024)}, u32[]{:S(2)}) copy-start(f32[2560]{0:T(1024)} %param.11) | copy-start | bytes 30724
  70.9 10.2 %copy-start.2 = (f32[2560]{0:T(1024)S(1)}, f32[2560]{0:T(1024)}, u32[]{:S(2)}) copy-start(f32[2560]{0:T(1024)} %param.10) | copy-start | bytes 30724
  72.8 8.3 %collective-permute-start.7 = (bf16[48,2560]{1,0:T(8,128)(2,1)S(1)}, bf16[48,2560]{1,0:T(8,128)(2,1)S(1)}, u32[]{:S(2)}, u32[]{:S(2)}) collective-permute-start(bf16[48,2560]{1,0:T(8,128)(2,1)S(1)} %shard_map.72), channel_id=1, source_target_pairs={{0,1},{1,0},{2,3},{3,2},{4,5},{5,4},{6,7},{7,6},{8,9},{9,8},{10,11... | collective-permute-start | bytes 737288 | tf_op jit(solution)/shard_map/ppermute | solution.py:299

commit v5 on v4

--- a/solution.py
+++ b/solution.py
@@ -80,7 +80,7 @@
     return pltpu.with_memory_space_constraint(array, pltpu.HBM)
 
 
-def dequantize_kernel(half_ref, words_ref, scales_ref, out_ref, slots, wide, sems):
+def dequantize_kernel(half_ref, words_ref, scales_ref, out_ref, slots, narrow, wide, sems):
     rows, quarter = words_ref.shape
     groups = scales_ref.shape[0]
     depth = rows // groups
@@ -92,9 +92,12 @@
         start = pl.multiple_of(g * depth, depth)
         return pltpu.make_async_copy(words_ref.at[pl.ds(start, depth)], slots.at[slot], sems.at[slot])
 
+    scales_copy = pltpu.make_async_copy(scales_ref, narrow, sems.at[ahead])
+    scales_copy.start()
     for g in range(ahead):
         fetch(g).start()
-    wide[...] = scales_ref[...].astype(F32)
+    scales_copy.wait()
+    wide[...] = narrow[...].astype(F32)
 
     def step(g, carry):
         fetch(g).wait()
@@ -107,17 +110,17 @@
                 for low in range(2):
                     at = pl.multiple_of((2 * mine + low) * quarter + column, 128)
                     row = wide[pl.ds(g, 1), pl.ds(at, across)] * (0.0625 if low else 1.0)
-                    scales.append(jnp.broadcast_to(row, (chunk, across)))
+                    scales.append(jnp.broadcast_to(row, (chunk, across)).astype(BF16))
                 for r in range(0, depth, chunk):
                     words = slots[slot, r : r + chunk, column : column + across]
                     shifted = lax.shift_right_logical(words, jnp.full(words.shape, 8 * mine, jnp.int32))
                     for low in range(2):
-                        level = ((shifted & 240) - 128) if low else ((shifted & 15) - 8)
+                        level = ((shifted & 240) if low else (shifted & 15)).astype(F32).astype(BF16)
                         out_ref[
                             part,
                             pl.ds(start + r, chunk),
                             low * quarter + column : low * quarter + column + across,
-                        ] = (level.astype(F32) * scales[low]).astype(BF16)
+                        ] = (level - (128 if low else 8)) * scales[low]
 
         @pl.when(g + ahead < groups)
         def _():
@@ -137,18 +140,19 @@
         in_specs=[
             pl.BlockSpec(memory_space=pltpu.SMEM),
             pl.BlockSpec(memory_space=pltpu.HBM),
-            pl.BlockSpec(memory_space=pltpu.VMEM),
+            pl.BlockSpec(memory_space=pltpu.HBM),
         ],
         out_specs=pl.BlockSpec(memory_space=pltpu.VMEM),
         out_shape=pltpu.VMEM((2, rows, 2 * quarter), BF16),
         scratch_shapes=[
             pltpu.VMEM((ahead, rows // groups, quarter), jnp.int32),
+            pltpu.VMEM(group_scales.shape, group_scales.dtype),
             pltpu.VMEM(group_scales.shape, F32),
-            pltpu.SemaphoreType.DMA((ahead,)),
+            pltpu.SemaphoreType.DMA((ahead + 1,)),
         ],
         compiler_params=pltpu.CompilerParams(vmem_limit_bytes=8 * 1024 * 1024),
         cost_estimate=pl.CostEstimate(flops=rows * quarter * 30, bytes_accessed=rows * quarter * 12, transcendentals=0),
-    )(half, in_hbm(code_words), group_scales)
+    )(half, in_hbm(code_words), in_hbm(group_scales))
 
 
 def attend_kernel(first, last, blocks, after, tile, q_ref, *refs):
@@ -255,8 +259,8 @@
     )(returned, weights)
 
 
-HEAD_AXES = ("x", "zl", "yl")
-RING = "zh"
+HEAD_AXES = ("zh", "zl", "yl")
+RING = "x"
 
 
 def body(head_inputs, positions, code_words, group_scales, out_gate, out_bias):
@@ -278,15 +282,12 @@
 
     near = send(own, 1)
     back = send(own, -1)
-    beside = swap(own)
     weights = dequantize(half, code_words, group_scales)
-    state = attend(grouped, [grouped, beside], None, after=(weights,))
-    near, back, state = lax.optimization_barrier((near, back, state))
+    near, back, own, weights = lax.optimization_barrier((near, back, own, weights))
     far = send(near, 1)
-    near_beside = swap(near)
-    back_beside = swap(back)
-    state = attend(grouped, [near, back], state)
-    state = attend(grouped, [near_beside, back_beside], state)
+    beside, near_beside, back_beside = swap(own), swap(near), swap(back)
+    state = attend(grouped, [own, near, back], None)
+    state = attend(grouped, [beside, near_beside, back_beside], state)
     far, state = lax.optimization_barrier((far, state))
     far_beside = swap(far)
     state = attend(grouped, [far], state)

time: 82.2 us -> 79.8 us (0.971)
  the two profiles are of different devices: /device:TPU:16 before, /device:TPU:6 now
where the time goes in v5:
time: 79.8 us; the launch traced here: 78.7 us
  blocking collectives  43.1 us (54%)
  Pallas kernels  22.2 us (28%)
  starting transfers between devices  8.31 us (10%)
  waiting for transfers between devices  4.12 us (5%)
  other arithmetic  0.86 us (1%)
    all_to_all x1, blocking collectives, body(): lax.all_to_all(prepared, HEAD_AXES, split_axis=0, concat_axis=0, tiled=True)  29 us
    all_to_all x1, blocking collectives, body(): lax.all_to_all(attended.reshape(chunks, -1, HD), HEAD_AXES, split_axis=0,...  14.1 us
    pallas_call x4, Pallas kernels, attend(): pl.pallas_call(functools.partial(attend_kernel, first, last, blocks, len(...  8.71 us
    pallas_call x1, Pallas kernels, dequantize(): pl.pallas_call(dequantize_kernel, in_specs=[pl.BlockSpec(memory_space=plt...  7.93 us
    ppermute x3, starting transfers between devices, send(): return lax.ppermute(a, (RING, 'c'), hops)  4.16 us
    pallas_call x2, Pallas kernels, project(): pl.pallas_call(functools.partial(project_kernel, part, tile), in_specs=[p...  3.76 us
    ppermute x1, waiting for transfers between devices, body(): incoming = lax.ppermute(outgoing, 'yh', [(0, 1), (1, 0)])  3.33 us
    ppermute x1, starting transfers between devices, body(): incoming = lax.ppermute(outgoing, 'yh', [(0, 1), (1, 0)])  2.98 us
  transfers between devices with their start and end apart: 8, of which 3 were waited for; matrix products, arithmetic and copies ran while one was open for 0% of the time, Pallas kernels for 22%

profile of v5, /device:TPU:6, one launch (start us, length us, event | category | flops | bytes accessed | tf_op | source)
XLA Modules:
  0.0 78.7 jit_solution(8473411108357802371)
XLA Ops:
  0.0 1.8 %shard_map.64 = bf16[16,3,48,128]{3,2,1,0:T(8,128)(2,1)S(1)} custom-call(s32[3,48]{1,0:T(4,128)} %pos_hbm.1, bf16[48,3,16,128]{3,2,1,0:T(8,128)(2,1)} %x_hbm.1), custom_call_target="tpu_custom_call" | custom-call | tf_op jit(solution)/shard_map/pallas_call | solution.py:64
  1.8 29.0 %all_to_all.10.q_ref = bf16[16,3,48,128]{3,2,1,0:T(8,128)(2,1)S(1)} all-to-all(bf16[16,3,48,128]{3,2,1,0:T(8,128)(2,1)S(1)} %shard_map.64), channel_id=1, replica_groups=mesh['x'=4,'zh'=4,'zl'=2,'yl'=2,'c'=2,'yh'=2] {'zh','zl','yl'}, dimensions={0} | all-to-all | bytes 1179648 | tf_op jit(solution)/shard_map/all_to_all | solution.py:270
  30.7 0.9 %collective-permute-start.1 = (bf16[16,2,48,128]{3,2,1,0:T(8,128)(2,1)S(1)}, bf16[16,2,48,128]{3,2,1,0:T(8,128)(2,1)S(1)}, u32[]{:S(2)}, u32[]{:S(2)}) collective-permute-start(bf16[16,2,48,128]{3,2,1,0:T(8,128)(2,1)S(1)} %slice.4.refs_0_), channel_id=1, source_target_pairs={{0,192},{2,66},{64,0},{66,130},{128,64},{130,194},{192,128},{194,2... | collective-permute-start | bytes 1179656 | tf_op jit(solution)/shard_map/ppermute | solution.py:281
  31.6 2.4 %collective-permute-start = (bf16[16,2,48,128]{3,2,1,0:T(8,128)(2,1)S(1)}, bf16[16,2,48,128]{3,2,1,0:T(8,128)(2,1)S(1)}, u32[]{:S(2)}, u32[]{:S(2)}) collective-permute-start(bf16[16,2,48,128]{3,2,1,0:T(8,128)(2,1)S(1)} %slice.4.refs_0_), channel_id=1, source_target_pairs={{0,64},{2,194},{64,128},{66,2},{128,192},{130,66},{192,0},{194,130... | collective-permute-start | bytes 1179656 | tf_op jit(solution)/shard_map/ppermute | solution.py:281
  34.1 7.9 %shard_map.65.w_ref = bf16[2,2048,2560]{2,1,0:T(8,128)(2,1)S(1)} custom-call(s32[1]{0:T(128)} %bitcast.half_ref, s32[2048,1280]{1,0:T(8,128)} %words_ref.1, bf16[16,5120]{1,0:T(8,128)(2,1)} %scales_ref.1), custom_call_target="tpu_custom_call" | custom-call | flops 78643200 | bytes 31457280 | tf_op jit(solution)/shard_map/pallas_call | solution.py:138
  42.0 0.0 collective-permute-done.1.refs_2_
  42.0 0.0 collective-permute-done.refs_1_
  42.0 0.1 collective-permute-start.3
  42.1 0.5 collective-permute-start.5
  42.6 0.1 collective-permute-start.4
  42.7 0.8 %collective-permute-start.2 = (bf16[16,2,48,128]{3,2,1,0:T(8,128)(2,1)S(1)}, bf16[16,2,48,128]{3,2,1,0:T(8,128)(2,1)S(1)}, u32[]{:S(2)}, u32[]{:S(2)}) collective-permute-start(bf16[16,2,48,128]{3,2,1,0:T(8,128)(2,1)S(1)} %collective-permute-done.refs_1_), channel_id=1, source_target_pairs={{0,64},{2,194},{64,128},{66,2},{128,192},{130,66},{192,0},{194,130... | collective-permute-start | bytes 1179656 | tf_op jit(solution)/shard_map/ppermute | solution.py:281
  43.6 3.1 %shard_map.66 = (f32[768,128]{1,0:T(8,128)S(1)}, f32[768,128]{1,0:T(8,128)S(1)}, f32[768,128]{1,0:T(8,128)S(1)}) custom-call(bf16[16,3,48,128]{3,2,1,0:T(8,128)(2,1)S(1)} %all_to_all.10.q_ref, bf16[16,2,48,128]{3,2,1,0:T(8,128)(2,1)S(1)} %slice.4.refs_0_, bf16[16,2,48,128]{3,2,1,0:T(8,128)(2,1)S(1)} %collective-permute-done.refs_1_, ...), custom_call_target="tpu_custom_call" | custom-call | flops 905969664 | bytes 2555904 | tf_op jit(solution)/shard_map/pallas_call | solution.py:230
  46.7 0.0 collective-permute-done.3.refs_0_
  46.7 0.0 collective-permute-done.5.refs_2_
  46.7 0.0 collective-permute-done.4.refs_1_
  46.7 3.1 %shard_map.67 = (f32[768,128]{1,0:T(8,128)S(1)}, f32[768,128]{1,0:T(8,128)S(1)}, f32[768,128]{1,0:T(8,128)S(1)}) custom-call(bf16[16,3,48,128]{3,2,1,0:T(8,128)(2,1)S(1)} %all_to_all.10.q_ref, bf16[16,2,48,128]{3,2,1,0:T(8,128)(2,1)S(1)} %collective-permute-done.3.refs_0_, bf16[16,2,48,128]{3,2,1,0:T(8,128)(2,1)S(1)} %collective-permute-done.4.refs_1_, ...), custom_call_target="tpu_custom_call" | custom-call | flops 905969664 | bytes 2555904 | tf_op jit(solution)/shard_map/pallas_call | solution.py:230
  49.8 0.7 collective-permute-done.2.refs_0_
  50.5 0.5 collective-permute-start.6
  51.0 1.3 %shard_map.68 = (f32[768,128]{1,0:T(8,128)S(1)}, f32[768,128]{1,0:T(8,128)S(1)}, f32[768,128]{1,0:T(8,128)S(1)}) custom-call(bf16[16,3,48,128]{3,2,1,0:T(8,128)(2,1)S(1)} %all_to_all.10.q_ref, bf16[16,2,48,128]{3,2,1,0:T(8,128)(2,1)S(1)} %collective-permute-done.2.refs_0_, f32[768,128]{1,0:T(8,128)S(1)} %get-tuple-element.32.refs_1_, ...), custom_call_target="tpu_custom_call" | custom-call | flops 301989888 | bytes 1769472 | tf_op jit(solution)/shard_map/pallas_call | solution.py:230
  52.2 0.1 collective-permute-done.6.refs_0_
  52.3 1.3 %shard_map.69 = bf16[768,128]{1,0:T(8,128)(2,1)S(1)} custom-call(bf16[16,3,48,128]{3,2,1,0:T(8,128)(2,1)S(1)} %all_to_all.10.q_ref, bf16[16,2,48,128]{3,2,1,0:T(8,128)(2,1)S(1)} %collective-permute-done.6.refs_0_, f32[768,128]{1,0:T(8,128)S(1)} %get-tuple-element.35.refs_1_, f32[768,128]{1,0:T(8,128)S(1)} %get-tuple-element.36.refs_2_, ...), custom_call_target="tpu_custom_call" | custom-call | flops 301989888 | bytes 1769472 | tf_op jit(solution)/shard_map/pallas_call | solution.py:230
  53.6 14.1 %all_to_all.11.x_ref = bf16[16,48,128]{2,1,0:T(8,128)(2,1)S(1)} all-to-all(bf16[16,48,128]{2,1,0:T(8,128)(2,1)S(1)} %bitcast.2), channel_id=1, replica_groups=mesh['x'=4,'zh'=4,'zl'=2,'yl'=2,'c'=2,'yh'=2] {'zh','zl','yl'}, dimensions={0} | all-to-all | bytes 393216 | tf_op jit(solution)/shard_map/all_to_all | solution.py:296
  67.7 0.0 copy-start
  67.7 0.0 copy-start.1
  67.7 1.9 %shard_map.71 = bf16[48,2560]{1,0:T(8,128)(2,1)S(1)} custom-call(bf16[16,48,128]{2,1,0:T(8,128)(2,1)S(1)} %all_to_all.11.x_ref, bf16[2,2048,2560]{2,1,0:T(8,128)(2,1)S(1)} %shard_map.65.w_ref), custom_call_target="tpu_custom_call" | custom-call | flops 503316480 | bytes 10485760 | tf_op jit(solution)/shard_map/pallas_call | solution.py:250
  69.6 3.0 %collective-permute-start.7 = (bf16[48,2560]{1,0:T(8,128)(2,1)S(1)}, bf16[48,2560]{1,0:T(8,128)(2,1)S(1)}, u32[]{:S(2)}, u32[]{:S(2)}) collective-permute-start(bf16[48,2560]{1,0:T(8,128)(2,1)S(1)} %shard_map.71), channel_id=1, source_target_pairs={{0,1},{1,0},{2,3},{3,2},{4,5},{5,4},{6,7},{7,6},{8,9},{9,8},{10,11... | collective-permute-start | bytes 737288 | tf_op jit(solution)/shard_map/ppermute | solution.py:300
  72.6 1.9 %shard_map.70 = f32[48,2560]{1,0:T(8,128)S(1)} custom-call(bf16[16,48,128]{2,1,0:T(8,128)(2,1)S(1)} %all_to_all.11.x_ref, bf16[2,2048,2560]{2,1,0:T(8,128)(2,1)S(1)} %shard_map.65.w_ref), custom_call_target="tpu_custom_call" | custom-call | flops 503316480 | bytes 10485760 | tf_op jit(solution)/shard_map/pallas_call | solution.py:250
  74.5 3.3 %collective-permute-done.7 = bf16[48,2560]{1,0:T(8,128)(2,1)S(1)} collective-permute-done((bf16[48,2560]{1,0:T(8,128)(2,1)S(1)}, bf16[48,2560]{1,0:T(8,128)(2,1)S(1)}, u32[]{:S(2)}, u32[]{:S(2)}) %collective-permute-start.7) | collective-permute-done | bytes 245792 | tf_op jit(solution)/shard_map/ppermute | solution.py:300
  77.8 0.0 copy-done
  77.8 0.0 copy-done.1
  77.8 0.9 %add_multiply_fusion = f32[48,2560]{1,0:T(8,128)} fusion(f32[48,2560]{1,0:T(8,128)S(1)} %shard_map.70, bf16[48,2560]{1,0:T(8,128)(2,1)S(1)} %collective-permute-done.7, f32[2560]{0:T(1024)S(1)} %copy-done, f32[2560]{0:T(1024)S(1)} %copy-done.1), kind=kLoop, calls=%fused_computation | loop fusion | flops 491520 | bytes 1249280 | tf_op jit(solution)/shard_map/mul | solution.py:302
  (1 shorter events, 0.0 us)
Async XLA Ops:
  30.7 11.3 %collective-permute-start.1 = (bf16[16,2,48,128]{3,2,1,0:T(8,128)(2,1)S(1)}, bf16[16,2,48,128]{3,2,1,0:T(8,128)(2,1)S(1)}, u32[]{:S(2)}, u32[]{:S(2)}) collective-permute-start(bf16[16,2,48,128]{3,2,1,0:T(8,128)(2,1)S(1)} %slice.4.refs_0_), channel_id=1, source_target_pairs={{0,192},{2,66},{64,0},{66,130},{128,64},{130,194},{192,128},{194,2... | collective-permute-start | bytes 1179656 | tf_op jit(solution)/shard_map/ppermute | solution.py:281
  31.6 10.4 %collective-permute-start = (bf16[16,2,48,128]{3,2,1,0:T(8,128)(2,1)S(1)}, bf16[16,2,48,128]{3,2,1,0:T(8,128)(2,1)S(1)}, u32[]{:S(2)}, u32[]{:S(2)}) collective-permute-start(bf16[16,2,48,128]{3,2,1,0:T(8,128)(2,1)S(1)} %slice.4.refs_0_), channel_id=1, source_target_pairs={{0,64},{2,194},{64,128},{66,2},{128,192},{130,66},{192,0},{194,130... | collective-permute-start | bytes 1179656 | tf_op jit(solution)/shard_map/ppermute | solution.py:281
  42.0 4.6 %collective-permute-start.3 = (bf16[16,2,48,128]{3,2,1,0:T(8,128)(2,1)S(1)}, bf16[16,2,48,128]{3,2,1,0:T(8,128)(2,1)S(1)}, u32[]{:S(2)}, u32[]{:S(2)}) collective-permute-start(bf16[16,2,48,128]{3,2,1,0:T(8,128)(2,1)S(1)} %slice.4.refs_0_), channel_id=1, source_target_pairs={{0,2},{2,0},{1,3},{3,1},{4,6},{6,4},{5,7},{7,5},{8,10},{10,8},{9,1... | collective-permute-start | bytes 1179656 | tf_op jit(solution)/shard_map/ppermute | solution.py:274
  42.1 4.6 %collective-permute-start.5 = (bf16[16,2,48,128]{3,2,1,0:T(8,128)(2,1)S(1)}, bf16[16,2,48,128]{3,2,1,0:T(8,128)(2,1)S(1)}, u32[]{:S(2)}, u32[]{:S(2)}) collective-permute-start(bf16[16,2,48,128]{3,2,1,0:T(8,128)(2,1)S(1)} %collective-permute-done.1.refs_2_), channel_id=1, source_target_pairs={{0,2},{2,0},{1,3},{3,1},{4,6},{6,4},{5,7},{7,5},{8,10},{10,8},{9,1... | collective-permute-start | bytes 1179656 | tf_op jit(solution)/shard_map/ppermute | solution.py:274
  42.6 4.1 %collective-permute-start.4 = (bf16[16,2,48,128]{3,2,1,0:T(8,128)(2,1)S(1)}, bf16[16,2,48,128]{3,2,1,0:T(8,128)(2,1)S(1)}, u32[]{:S(2)}, u32[]{:S(2)}) collective-permute-start(bf16[16,2,48,128]{3,2,1,0:T(8,128)(2,1)S(1)} %collective-permute-done.refs_1_), channel_id=1, source_target_pairs={{0,2},{2,0},{1,3},{3,1},{4,6},{6,4},{5,7},{7,5},{8,10},{10,8},{9,1... | collective-permute-start | bytes 1179656 | tf_op jit(solution)/shard_map/ppermute | solution.py:274
  42.7 7.8 %collective-permute-start.2 = (bf16[16,2,48,128]{3,2,1,0:T(8,128)(2,1)S(1)}, bf16[16,2,48,128]{3,2,1,0:T(8,128)(2,1)S(1)}, u32[]{:S(2)}, u32[]{:S(2)}) collective-permute-start(bf16[16,2,48,128]{3,2,1,0:T(8,128)(2,1)S(1)} %collective-permute-done.refs_1_), channel_id=1, source_target_pairs={{0,64},{2,194},{64,128},{66,2},{128,192},{130,66},{192,0},{194,130... | collective-permute-start | bytes 1179656 | tf_op jit(solution)/shard_map/ppermute | solution.py:281
  50.5 1.8 %collective-permute-start.6 = (bf16[16,2,48,128]{3,2,1,0:T(8,128)(2,1)S(1)}, bf16[16,2,48,128]{3,2,1,0:T(8,128)(2,1)S(1)}, u32[]{:S(2)}, u32[]{:S(2)}) collective-permute-start(bf16[16,2,48,128]{3,2,1,0:T(8,128)(2,1)S(1)} %collective-permute-done.2.refs_0_), channel_id=1, source_target_pairs={{0,2},{2,0},{1,3},{3,1},{4,6},{6,4},{5,7},{7,5},{8,10},{10,8},{9,1... | collective-permute-start | bytes 1179656 | tf_op jit(solution)/shard_map/ppermute | solution.py:274
  67.7 10.1 %copy-start = (f32[2560]{0:T(1024)S(1)}, f32[2560]{0:T(1024)}, u32[]{:S(2)}) copy-start(f32[2560]{0:T(1024)} %param.11) | copy-start | bytes 30724
  67.7 10.1 %copy-start.1 = (f32[2560]{0:T(1024)S(1)}, f32[2560]{0:T(1024)}, u32[]{:S(2)}) copy-start(f32[2560]{0:T(1024)} %param.10) | copy-start | bytes 30724
  69.6 8.2 %collective-permute-start.7 = (bf16[48,2560]{1,0:T(8,128)(2,1)S(1)}, bf16[48,2560]{1,0:T(8,128)(2,1)S(1)}, u32[]{:S(2)}, u32[]{:S(2)}) collective-permute-start(bf16[48,2560]{1,0:T(8,128)(2,1)S(1)} %shard_map.71), channel_id=1, source_target_pairs={{0,1},{1,0},{2,3},{3,2},{4,5},{5,4},{6,7},{7,6},{8,9},{9,8},{10,11... | collective-permute-start | bytes 737288 | tf_op jit(solution)/shard_map/ppermute | solution.py:300

commit v6 on v5

--- a/solution.py
+++ b/solution.py
@@ -27,7 +27,7 @@
     return jnp.where((within >= 0) & (within < extent), rate, 0.0)
 
 
-def rotate_kernel(pos_hbm, x_hbm, out_ref, pos_ref, x_ref, wide, sems):
+def rotate_kernel(pos_hbm, x_hbm, q_ref, kv_ref, pos_ref, x_ref, wide, sems):
     pos_copy = pltpu.make_async_copy(pos_hbm, pos_ref, sems.at[0])
     x_copy = pltpu.make_async_copy(x_hbm, x_ref, sems.at[1])
     pos_copy.start()
@@ -56,7 +56,10 @@
                 right = pltpu.roll(x, 1, 1)
                 left = pltpu.roll(x, width - 1, 1)
                 x = x * cosine + (left * sine_even + right * sine_odd)
-            out_ref[head, kind] = x.astype(BF16)
+            if kind:
+                kv_ref[head, kind - 1] = x.astype(BF16)
+            else:
+                q_ref[head] = x.astype(BF16)
 
 
 def rotate(positions, head_inputs):
@@ -64,8 +67,11 @@
     return pl.pallas_call(
         rotate_kernel,
         in_specs=[pl.BlockSpec(memory_space=pltpu.HBM)] * 2,
-        out_specs=pl.BlockSpec(memory_space=pltpu.VMEM),
-        out_shape=jax.ShapeDtypeStruct((heads, kinds, tokens, width), BF16),
+        out_specs=[pl.BlockSpec(memory_space=pltpu.VMEM)] * 2,
+        out_shape=[
+            jax.ShapeDtypeStruct((heads, tokens, width), BF16),
+            jax.ShapeDtypeStruct((heads, kinds - 1, tokens, width), BF16),
+        ],
         scratch_shapes=[
             pltpu.VMEM(positions.shape, positions.dtype),
             pltpu.VMEM(head_inputs.shape, head_inputs.dtype),
@@ -104,23 +110,20 @@
         slot = lax.rem(g, ahead)
         start = pl.multiple_of(g * depth, depth)
         for column in range(0, quarter, across):
-            for part in range(2):
-                mine = half if part else 1 - half
-                scales = []
+            scales = []
+            for low in range(2):
+                at = pl.multiple_of((2 * half + low) * quarter + column, 128)
+                row = wide[pl.ds(g, 1), pl.ds(at, across)] * (0.0625 if low else 1.0)
+                scales.append(jnp.broadcast_to(row, (chunk, across)).astype(BF16))
+            for r in range(0, depth, chunk):
+                words = slots[slot, r : r + chunk, column : column + across]
+                shifted = lax.shift_right_logical(words, jnp.full(words.shape, 8 * half, jnp.int32))
                 for low in range(2):
-                    at = pl.multiple_of((2 * mine + low) * quarter + column, 128)
-                    row = wide[pl.ds(g, 1), pl.ds(at, across)] * (0.0625 if low else 1.0)
-                    scales.append(jnp.broadcast_to(row, (chunk, across)).astype(BF16))
-                for r in range(0, depth, chunk):
-                    words = slots[slot, r : r + chunk, column : column + across]
-                    shifted = lax.shift_right_logical(words, jnp.full(words.shape, 8 * mine, jnp.int32))
-                    for low in range(2):
-                        level = ((shifted & 240) if low else (shifted & 15)).astype(F32).astype(BF16)
-                        out_ref[
-                            part,
-                            pl.ds(start + r, chunk),
-                            low * quarter + column : low * quarter + column + across,
-                        ] = (level - (128 if low else 8)) * scales[low]
+                    level = ((shifted & 240) if low else (shifted & 15)).astype(F32).astype(BF16)
+                    out_ref[
+                        pl.ds(start + r, chunk),
+                        low * quarter + column : low * quarter + column + across,
+                    ] = (level - (128 if low else 8)) * scales[low]
 
         @pl.when(g + ahead < groups)
         def _():
@@ -134,7 +137,7 @@
 def dequantize(half, code_words, group_scales):
     rows, quarter = code_words.shape
     groups = group_scales.shape[0]
-    ahead = 4
+    ahead = 8
     return pl.pallas_call(
         dequantize_kernel,
         in_specs=[
@@ -143,15 +146,15 @@
             pl.BlockSpec(memory_space=pltpu.HBM),
         ],
         out_specs=pl.BlockSpec(memory_space=pltpu.VMEM),
-        out_shape=pltpu.VMEM((2, rows, 2 * quarter), BF16),
+        out_shape=pltpu.VMEM((rows, 2 * quarter), BF16),
         scratch_shapes=[
             pltpu.VMEM((ahead, rows // groups, quarter), jnp.int32),
             pltpu.VMEM(group_scales.shape, group_scales.dtype),
             pltpu.VMEM(group_scales.shape, F32),
             pltpu.SemaphoreType.DMA((ahead + 1,)),
         ],
-        compiler_params=pltpu.CompilerParams(vmem_limit_bytes=8 * 1024 * 1024),
-        cost_estimate=pl.CostEstimate(flops=rows * quarter * 30, bytes_accessed=rows * quarter * 12, transcendentals=0),
+        compiler_params=pltpu.CompilerParams(vmem_limit_bytes=12 * 1024 * 1024),
+        cost_estimate=pl.CostEstimate(flops=rows * quarter * 15, bytes_accessed=rows * quarter * 8, transcendentals=0),
     )(half, in_hbm(code_words), in_hbm(group_scales))
 
 
@@ -162,15 +165,14 @@
         m_in, l_in, acc_in = refs[:3]
         refs = refs[3:]
     scale = LOG2E / math.sqrt(HD)
-    groups, _, rows, width = q_ref.shape
+    groups, rows, width = q_ref.shape
     total = groups * rows
-    queries = q_ref[:, 0].reshape(total, width)
+    queries = q_ref[...].reshape(total, width)
     keys, values = [], []
     for ref in kv_refs:
-        at = ref.shape[1] - 2
         count = ref.shape[0] * rows
-        keys.append(ref[:, at].reshape(count, width))
-        values.append(ref[:, at + 1].reshape(count, width))
+        keys.append(ref[:, 0].reshape(count, width))
+        values.append(ref[:, 1].reshape(count, width))
 
     def scores(step):
         row, block = divmod(step, blocks)
@@ -219,8 +221,8 @@
                 acc_out[here, :] = acc
 
 
-def attend(queries, kv_blocks, state, last=False, after=(), tile=128):
-    groups, _, rows, width = queries.shape
+def attend(queries, kv_blocks, state, last=False, after=(), tile=384):
+    groups, rows, width = queries.shape
     total = groups * rows
     blocks = len(kv_blocks)
     first = state is None
@@ -237,18 +239,18 @@
     )(queries, *kv_blocks, *after, *(() if first else state))
 
 
-def project_kernel(part, tile, x_ref, w_ref, out_ref):
+def project_kernel(tile, x_ref, w_ref, out_ref):
     x = jnp.concatenate([x_ref[h] for h in range(x_ref.shape[0])], axis=1)
     for c in range(0, out_ref.shape[1], tile):
-        mixed = jnp.dot(x, w_ref[part, :, c : c + tile], preferred_element_type=F32)
+        mixed = jnp.dot(x, w_ref[:, c : c + tile], preferred_element_type=F32)
         out_ref[:, c : c + tile] = mixed.astype(out_ref.dtype)
 
 
-def project(part, returned, weights, out_type, tile=512):
+def project(returned, weights, out_type, tile=512):
     heads, tokens, width = returned.shape
-    _, rows, columns = weights.shape
+    rows, columns = weights.shape
     return pl.pallas_call(
-        functools.partial(project_kernel, part, tile),
+        functools.partial(project_kernel, tile),
         in_specs=[pl.BlockSpec(memory_space=pltpu.VMEM)] * 2,
         out_specs=pl.BlockSpec(memory_space=pltpu.VMEM),
         out_shape=jax.ShapeDtypeStruct((tokens, columns), out_type),
@@ -266,9 +268,10 @@
 def body(head_inputs, positions, code_words, group_scales, out_gate, out_bias):
     ring = lax.axis_size(RING)
     half = lax.axis_index("yh").astype(jnp.int32).reshape(1)
-    prepared = rotate(positions, head_inputs)
-    grouped = lax.all_to_all(prepared, HEAD_AXES, split_axis=0, concat_axis=0, tiled=True)
-    own = grouped[:, 1:]
+    turned_queries, turned_pairs = rotate(positions, head_inputs)
+
+    def regroup(a):
+        return lax.all_to_all(a, HEAD_AXES, split_axis=0, concat_axis=0, tiled=True)
 
     def swap(a):
         return lax.ppermute(a, "c", [(0, 1), (1, 0)])
@@ -280,25 +283,27 @@
             hops.append((2 * i + 1, 2 * ((i - way) % ring) + 1))
         return lax.ppermute(a, (RING, "c"), hops)
 
+    own = regroup(turned_pairs)
+    theirs = dequantize(1 - half, code_words, group_scales)
+    own, theirs, turned_queries = lax.optimization_barrier((own, theirs, turned_queries))
     near = send(own, 1)
     back = send(own, -1)
-    weights = dequantize(half, code_words, group_scales)
-    near, back, own, weights = lax.optimization_barrier((near, back, own, weights))
+    queries = regroup(turned_queries)
+    near, back, own = lax.optimization_barrier((near, back, own))
     far = send(near, 1)
     beside, near_beside, back_beside = swap(own), swap(near), swap(back)
-    state = attend(grouped, [own, near, back], None)
-    state = attend(grouped, [beside, near_beside, back_beside], state)
+    state = attend(queries, [own, near, back], None)
+    state = attend(queries, [beside, near_beside, back_beside], state)
     far, state = lax.optimization_barrier((far, state))
     far_beside = swap(far)
-    state = attend(grouped, [far], state)
-    attended = attend(grouped, [far_beside], state, True)
-    chunks = prepared.shape[0]
-    returned = lax.all_to_all(
-        attended.reshape(chunks, -1, HD), HEAD_AXES, split_axis=0, concat_axis=0, tiled=True
-    )
-    outgoing = project(0, returned, weights, BF16)
+    state = attend(queries, [far], state)
+    attended = attend(queries, [far_beside], state, True)
+    returned = regroup(attended.reshape(queries.shape))
+    returned, half = lax.optimization_barrier((returned, half))
+    mine = dequantize(half, code_words, group_scales)
+    outgoing = project(returned, theirs, BF16)
     incoming = lax.ppermute(outgoing, "yh", [(0, 1), (1, 0)])
-    kept = project(1, returned, weights, F32)
+    kept = project(returned, mine, F32)
     return out_gate[None, :] * (kept + incoming.astype(F32) + out_bias[None, :])
 
 

time: 79.8 us -> 78.3 us (0.981); the launches traced: 78.7 us -> 78 us
  blocking collectives: 43.1 us -> 14.3 us
  starting transfers between devices: 8.31 us -> 21.5 us
  waiting for transfers between devices: 4.12 us -> 14.7 us
  local copies, waits for them, and re-layouts: 0.03 us -> 4.01 us
    all_to_all x2 -> x1, blocking collectives: 43.1 us -> 14.3 us  [regroup(): return lax.all_to_all(a, HEAD_AXES, split_axis=0, concat_axis=0, tiled=True)]
    all_to_all x0 -> x2, starting transfers between devices: none -> 13.1 us  [regroup(): return lax.all_to_all(a, HEAD_AXES, split_axis=0, concat_axis=0, tiled=True)]
    all_to_all x0 -> x2, waiting for transfers between devices: none -> 9.93 us  [regroup(): return lax.all_to_all(a, HEAD_AXES, split_axis=0, concat_axis=0, tiled=True)]
    unnamed x4 -> x8, local copies, waits for them, and re-layouts: 0.01 us -> 4.01 us
    ppermute x3, waiting for transfers between devices: 0.7 us -> 4.04 us  [send(): return lax.ppermute(a, (RING, 'c'), hops)]
    ppermute x1, waiting for transfers between devices: 3.33 us -> 0.01 us  [body(): incoming = lax.ppermute(outgoing, 'yh', [(0, 1), (1, 0)])]
    pallas_call x4, Pallas kernels: 8.71 us -> 6.68 us  [attend(): pl.pallas_call(functools.partial(attend_kernel, first, last, blocks, len(...]
    pallas_call x1 -> x2, Pallas kernels: 7.93 us -> 9.5 us  [dequantize(): pl.pallas_call(dequantize_kernel, in_specs=[pl.BlockSpec(memory_space=plt...]
  transfers between devices with their start and end apart: 8 -> 10, of which waited for: 3 -> 4; matrix products, arithmetic and copies ran while one was open for 0% -> 0% of each run, Pallas kernels for 22% -> 22%
where the time goes in v6:
time: 78.3 us; the launch traced here: 78 us
  Pallas kernels  22.4 us (29%)
  starting transfers between devices  21.5 us (27%)
  waiting for transfers between devices  14.7 us (19%)
  blocking collectives  14.3 us (18%)
  local copies, waits for them, and re-layouts  4.01 us (5%)
  other arithmetic  0.86 us (1%)
    all_to_all x1, blocking collectives, regroup(): return lax.all_to_all(a, HEAD_AXES, split_axis=0, concat_axis=0, tiled=True)  14.3 us
    all_to_all x2, starting transfers between devices, regroup(): return lax.all_to_all(a, HEAD_AXES, split_axis=0, concat_axis=0, tiled=True)  13.1 us
    all_to_all x2, waiting for transfers between devices, regroup(): return lax.all_to_all(a, HEAD_AXES, split_axis=0, concat_axis=0, tiled=True)  9.93 us
    pallas_call x2, Pallas kernels, dequantize(): pl.pallas_call(dequantize_kernel, in_specs=[pl.BlockSpec(memory_space=plt...  9.5 us
    pallas_call x4, Pallas kernels, attend(): pl.pallas_call(functools.partial(attend_kernel, first, last, blocks, len(...  6.68 us
    ppermute x3, starting transfers between devices, send(): return lax.ppermute(a, (RING, 'c'), hops)  4.66 us
    ppermute x3, waiting for transfers between devices, send(): return lax.ppermute(a, (RING, 'c'), hops)  4.04 us
    unnamed x8, local copies, waits for them, and re-layouts  4.01 us
  transfers between devices with their start and end apart: 10, of which 4 were waited for; matrix products, arithmetic and copies ran while one was open for 0% of the time, Pallas kernels for 22%

profile of v6, /device:TPU:6, one launch (start us, length us, event | category | flops | bytes accessed | tf_op | source)
XLA Modules:
  0.0 78.0 jit_solution(758578990382779883)
XLA Ops:
  0.0 2.4 %shard_map.64 = (bf16[16,48,128]{2,1,0:T(8,128)(2,1)}, bf16[16,2,48,128]{3,2,1,0:T(8,128)(2,1)}) custom-call(s32[3,48]{1,0:T(4,128)} %pos_hbm.1, bf16[48,3,16,128]{3,2,1,0:T(8,128)(2,1)} %x_hbm.1), custom_call_target="tpu_custom_call" | custom-call | tf_op jit(solution)/shard_map/pallas_call | solution.py:67
  2.4 9.6 %all-to-all-start = ((bf16[16,2,48,128]{3,2,1,0:T(8,128)(2,1)}), bf16[16,2,48,128]{3,2,1,0:T(8,128)(2,1)S(1)}, u32[]{:S(2)}, u32[]{:S(2)}) async-start(bf16[16,2,48,128]{3,2,1,0:T(8,128)(2,1)} %get-tuple-element.28), calls=%async_computation | async-start | bytes 786432 | tf_op jit(solution)/shard_map/all_to_all | solution.py:274
  12.0 4.8 %shard_map.65.w_ref = bf16[2048,2560]{1,0:T(8,128)(2,1)S(1)} custom-call(s32[1]{0:T(128)S(6)} %sub.3.half_ref, s32[2048,1280]{1,0:T(8,128)} %words_ref.3, bf16[16,5120]{1,0:T(8,128)(2,1)} %scales_ref.3), custom_call_target="tpu_custom_call" | custom-call | flops 39321600 | bytes 20971520 | tf_op jit(solution)/shard_map/pallas_call | solution.py:141
  16.8 0.0 copy-start
  16.8 4.0 %copy-done = bf16[2048,2560]{1,0:T(8,128)(2,1)} copy-done((bf16[2048,2560]{1,0:T(8,128)(2,1)}, bf16[2048,2560]{1,0:T(8,128)(2,1)S(1)}, u32[]{:S(2)}) %copy-start) | copy-done | bytes 10485784
  20.8 5.7 %all-to-all-done.refs_0_ = bf16[16,2,48,128]{3,2,1,0:T(8,128)(2,1)S(1)} async-done(((bf16[16,2,48,128]{3,2,1,0:T(8,128)(2,1)}), bf16[16,2,48,128]{3,2,1,0:T(8,128)(2,1)S(1)}, u32[]{:S(2)}, u32[]{:S(2)}) %all-to-all-start) | async-done | bytes 393248 | tf_op jit(solution)/shard_map/all_to_all | solution.py:274
  26.5 0.8 %collective-permute-start.1 = (bf16[16,2,48,128]{3,2,1,0:T(8,128)(2,1)S(1)}, bf16[16,2,48,128]{3,2,1,0:T(8,128)(2,1)S(1)}, u32[]{:S(2)}, u32[]{:S(2)}) collective-permute-start(bf16[16,2,48,128]{3,2,1,0:T(8,128)(2,1)S(1)} %all-to-all-done.refs_0_), channel_id=1, source_target_pairs={{0,192},{2,66},{64,0},{66,130},{128,64},{130,194},{192,128},{194,2... | collective-permute-start | bytes 1179656 | tf_op jit(solution)/shard_map/ppermute | solution.py:284
  27.4 2.4 %collective-permute-start = (bf16[16,2,48,128]{3,2,1,0:T(8,128)(2,1)S(1)}, bf16[16,2,48,128]{3,2,1,0:T(8,128)(2,1)S(1)}, u32[]{:S(2)}, u32[]{:S(2)}) collective-permute-start(bf16[16,2,48,128]{3,2,1,0:T(8,128)(2,1)S(1)} %all-to-all-done.refs_0_), channel_id=1, source_target_pairs={{0,64},{2,194},{64,128},{66,2},{128,192},{130,66},{192,0},{194,130... | collective-permute-start | bytes 1179656 | tf_op jit(solution)/shard_map/ppermute | solution.py:284
  29.8 3.5 %all-to-all-start.1 = ((bf16[16,48,128]{2,1,0:T(8,128)(2,1)}), bf16[16,48,128]{2,1,0:T(8,128)(2,1)S(1)}, u32[]{:S(2)}, u32[]{:S(2)}) async-start(bf16[16,48,128]{2,1,0:T(8,128)(2,1)} %get-tuple-element.30), calls=%async_computation.1 | async-start | bytes 393216 | tf_op jit(solution)/shard_map/all_to_all | solution.py:274
  33.3 4.0 %collective-permute-done.1.refs_2_ = bf16[16,2,48,128]{3,2,1,0:T(8,128)(2,1)S(1)} collective-permute-done((bf16[16,2,48,128]{3,2,1,0:T(8,128)(2,1)S(1)}, bf16[16,2,48,128]{3,2,1,0:T(8,128)(2,1)S(1)}, u32[]{:S(2)}, u32[]{:S(2)}) %collective-permute-start.1) | collective-permute-done | bytes 393248 | tf_op jit(solution)/shard_map/ppermute | solution.py:284
  37.3 0.0 collective-permute-done.refs_1_
  37.3 0.0 collective-permute-start.3
  37.3 0.5 collective-permute-start.5
  37.8 0.0 collective-permute-start.4
  37.8 1.4 %collective-permute-start.2 = (bf16[16,2,48,128]{3,2,1,0:T(8,128)(2,1)S(1)}, bf16[16,2,48,128]{3,2,1,0:T(8,128)(2,1)S(1)}, u32[]{:S(2)}, u32[]{:S(2)}) collective-permute-start(bf16[16,2,48,128]{3,2,1,0:T(8,128)(2,1)S(1)} %collective-permute-done.refs_1_), channel_id=1, source_target_pairs={{0,64},{2,194},{64,128},{66,2},{128,192},{130,66},{192,0},{194,130... | collective-permute-start | bytes 1179656 | tf_op jit(solution)/shard_map/ppermute | solution.py:284
  39.3 4.2 %all-to-all-done.1.q_ref = bf16[16,48,128]{2,1,0:T(8,128)(2,1)S(1)} async-done(((bf16[16,48,128]{2,1,0:T(8,128)(2,1)}), bf16[16,48,128]{2,1,0:T(8,128)(2,1)S(1)}, u32[]{:S(2)}, u32[]{:S(2)}) %all-to-all-start.1) | async-done | bytes 196640 | tf_op jit(solution)/shard_map/all_to_all | solution.py:274
  43.5 0.0 copy-start.1
  43.5 2.3 %shard_map.66 = (f32[768,128]{1,0:T(8,128)S(1)}, f32[768,128]{1,0:T(8,128)S(1)}, f32[768,128]{1,0:T(8,128)S(1)}) custom-call(bf16[16,48,128]{2,1,0:T(8,128)(2,1)S(1)} %all-to-all-done.1.q_ref, bf16[16,2,48,128]{3,2,1,0:T(8,128)(2,1)S(1)} %all-to-all-done.refs_0_, bf16[16,2,48,128]{3,2,1,0:T(8,128)(2,1)S(1)} %collective-permute-done.refs_1_, ...), custom_call_target="tpu_custom_call" | custom-call | flops 905969664 | bytes 2555904 | tf_op jit(solution)/shard_map/pallas_call | solution.py:232
  45.8 0.0 collective-permute-done.3.refs_0_
  45.8 0.0 collective-permute-done.5.refs_2_
  45.8 0.0 collective-permute-done.4.refs_1_
  45.8 2.4 %shard_map.67 = (f32[768,128]{1,0:T(8,128)S(1)}, f32[768,128]{1,0:T(8,128)S(1)}, f32[768,128]{1,0:T(8,128)S(1)}) custom-call(bf16[16,48,128]{2,1,0:T(8,128)(2,1)S(1)} %all-to-all-done.1.q_ref, bf16[16,2,48,128]{3,2,1,0:T(8,128)(2,1)S(1)} %collective-permute-done.3.refs_0_, bf16[16,2,48,128]{3,2,1,0:T(8,128)(2,1)S(1)} %collective-permute-done.4.refs_1_, ...), custom_call_target="tpu_custom_call" | custom-call | flops 905969664 | bytes 2555904 | tf_op jit(solution)/shard_map/pallas_call | solution.py:232
  48.2 0.0 collective-permute-done.2.refs_0_
  48.2 0.3 collective-permute-start.6
  48.5 1.0 %shard_map.68 = (f32[768,128]{1,0:T(8,128)S(1)}, f32[768,128]{1,0:T(8,128)S(1)}, f32[768,128]{1,0:T(8,128)S(1)}) custom-call(bf16[16,48,128]{2,1,0:T(8,128)(2,1)S(1)} %all-to-all-done.1.q_ref, bf16[16,2,48,128]{3,2,1,0:T(8,128)(2,1)S(1)} %collective-permute-done.2.refs_0_, f32[768,128]{1,0:T(8,128)S(1)} %get-tuple-element.42.refs_1_, ...), custom_call_target="tpu_custom_call" | custom-call | flops 301989888 | bytes 1769472 | tf_op jit(solution)/shard_map/pallas_call | solution.py:232
  49.5 0.7 collective-permute-done.6.refs_0_
  50.2 1.0 %shard_map.69 = bf16[768,128]{1,0:T(8,128)(2,1)S(1)} custom-call(bf16[16,48,128]{2,1,0:T(8,128)(2,1)S(1)} %all-to-all-done.1.q_ref, bf16[16,2,48,128]{3,2,1,0:T(8,128)(2,1)S(1)} %collective-permute-done.6.refs_0_, f32[768,128]{1,0:T(8,128)S(1)} %get-tuple-element.45.refs_1_, f32[768,128]{1,0:T(8,128)S(1)} %get-tuple-element.46.refs_2_, ...), custom_call_target="tpu_custom_call" | custom-call | flops 301989888 | bytes 1769472 | tf_op jit(solution)/shard_map/pallas_call | solution.py:232
  51.2 14.3 %all_to_all.15.x_ref = bf16[16,48,128]{2,1,0:T(8,128)(2,1)S(1)} all-to-all(bf16[16,48,128]{2,1,0:T(8,128)(2,1)S(1)} %bitcast.2), channel_id=1, replica_groups=mesh['x'=4,'zh'=4,'zl'=2,'yl'=2,'c'=2,'yh'=2] {'zh','zl','yl'}, dimensions={0} | all-to-all | bytes 393216 | tf_op jit(solution)/shard_map/all_to_all | solution.py:274
  65.5 0.0 copy-done.1
  65.5 1.9 %shard_map.72 = bf16[48,2560]{1,0:T(8,128)(2,1)S(1)} custom-call(bf16[16,48,128]{2,1,0:T(8,128)(2,1)S(1)} %all_to_all.15.x_ref, bf16[2048,2560]{1,0:T(8,128)(2,1)S(1)} %copy-done.1), custom_call_target="tpu_custom_call" | custom-call | flops 503316480 | bytes 10485760 | tf_op jit(solution)/shard_map/pallas_call | solution.py:252
  67.4 3.0 %collective-permute-start.7 = (bf16[48,2560]{1,0:T(8,128)(2,1)S(1)}, bf16[48,2560]{1,0:T(8,128)(2,1)S(1)}, u32[]{:S(2)}, u32[]{:S(2)}) collective-permute-start(bf16[48,2560]{1,0:T(8,128)(2,1)S(1)} %shard_map.72), channel_id=1, source_target_pairs={{0,1},{1,0},{2,3},{3,2},{4,5},{5,4},{6,7},{7,6},{8,9},{9,8},{10,11... | collective-permute-start | bytes 737288 | tf_op jit(solution)/shard_map/ppermute | solution.py:305
  70.4 4.8 %shard_map.70.w_ref = bf16[2048,2560]{1,0:T(8,128)(2,1)S(1)} custom-call(s32[1]{0:T(128)} %bitcast.half_ref, s32[2048,1280]{1,0:T(8,128)} %words_ref.3, bf16[16,5120]{1,0:T(8,128)(2,1)} %scales_ref.3), custom_call_target="tpu_custom_call" | custom-call | flops 39321600 | bytes 20971520 | tf_op jit(solution)/shard_map/pallas_call | solution.py:141
  75.2 0.0 copy-start.2
  75.2 0.0 copy-start.3
  75.2 1.9 %shard_map.71 = f32[48,2560]{1,0:T(8,128)S(1)} custom-call(bf16[16,48,128]{2,1,0:T(8,128)(2,1)S(1)} %all_to_all.15.x_ref, bf16[2048,2560]{1,0:T(8,128)(2,1)S(1)} %shard_map.70.w_ref), custom_call_target="tpu_custom_call" | custom-call | flops 503316480 | bytes 10485760 | tf_op jit(solution)/shard_map/pallas_call | solution.py:252
  77.1 0.0 collective-permute-done.7
  77.1 0.0 copy-done.2
  77.1 0.0 copy-done.3
  77.2 0.9 %add_multiply_fusion = f32[48,2560]{1,0:T(8,128)} fusion(f32[48,2560]{1,0:T(8,128)S(1)} %shard_map.71, bf16[48,2560]{1,0:T(8,128)(2,1)S(1)} %collective-permute-done.7, f32[2560]{0:T(1024)S(1)} %copy-done.2, f32[2560]{0:T(1024)S(1)} %copy-done.3), kind=kLoop, calls=%fused_computation | loop fusion | flops 491520 | bytes 1249280 | tf_op jit(solution)/shard_map/mul | solution.py:307
Async XLA Ops:
  2.4 24.1 %all-to-all-start = ((bf16[16,2,48,128]{3,2,1,0:T(8,128)(2,1)}), bf16[16,2,48,128]{3,2,1,0:T(8,128)(2,1)S(1)}, u32[]{:S(2)}, u32[]{:S(2)}) async-start(bf16[16,2,48,128]{3,2,1,0:T(8,128)(2,1)} %get-tuple-element.28), calls=%async_computation | async-start | bytes 786432 | tf_op jit(solution)/shard_map/all_to_all | solution.py:274
  16.8 4.0 %copy-start = (bf16[2048,2560]{1,0:T(8,128)(2,1)}, bf16[2048,2560]{1,0:T(8,128)(2,1)S(1)}, u32[]{:S(2)}) copy-start(bf16[2048,2560]{1,0:T(8,128)(2,1)S(1)} %shard_map.65.w_ref) | copy-start | bytes 31457284
  26.5 10.8 %collective-permute-start.1 = (bf16[16,2,48,128]{3,2,1,0:T(8,128)(2,1)S(1)}, bf16[16,2,48,128]{3,2,1,0:T(8,128)(2,1)S(1)}, u32[]{:S(2)}, u32[]{:S(2)}) collective-permute-start(bf16[16,2,48,128]{3,2,1,0:T(8,128)(2,1)S(1)} %all-to-all-done.refs_0_), channel_id=1, source_target_pairs={{0,192},{2,66},{64,0},{66,130},{128,64},{130,194},{192,128},{194,2... | collective-permute-start | bytes 1179656 | tf_op jit(solution)/shard_map/ppermute | solution.py:284
  27.4 10.0 %collective-permute-start = (bf16[16,2,48,128]{3,2,1,0:T(8,128)(2,1)S(1)}, bf16[16,2,48,128]{3,2,1,0:T(8,128)(2,1)S(1)}, u32[]{:S(2)}, u32[]{:S(2)}) collective-permute-start(bf16[16,2,48,128]{3,2,1,0:T(8,128)(2,1)S(1)} %all-to-all-done.refs_0_), channel_id=1, source_target_pairs={{0,64},{2,194},{64,128},{66,2},{128,192},{130,66},{192,0},{194,130... | collective-permute-start | bytes 1179656 | tf_op jit(solution)/shard_map/ppermute | solution.py:284
  29.8 13.7 %all-to-all-start.1 = ((bf16[16,48,128]{2,1,0:T(8,128)(2,1)}), bf16[16,48,128]{2,1,0:T(8,128)(2,1)S(1)}, u32[]{:S(2)}, u32[]{:S(2)}) async-start(bf16[16,48,128]{2,1,0:T(8,128)(2,1)} %get-tuple-element.30), calls=%async_computation.1 | async-start | bytes 393216 | tf_op jit(solution)/shard_map/all_to_all | solution.py:274
  37.3 8.5 %collective-permute-start.3 = (bf16[16,2,48,128]{3,2,1,0:T(8,128)(2,1)S(1)}, bf16[16,2,48,128]{3,2,1,0:T(8,128)(2,1)S(1)}, u32[]{:S(2)}, u32[]{:S(2)}) collective-permute-start(bf16[16,2,48,128]{3,2,1,0:T(8,128)(2,1)S(1)} %all-to-all-done.refs_0_), channel_id=1, source_target_pairs={{0,2},{2,0},{1,3},{3,1},{4,6},{6,4},{5,7},{7,5},{8,10},{10,8},{9,1... | collective-permute-start | bytes 1179656 | tf_op jit(solution)/shard_map/ppermute | solution.py:277
  37.3 8.5 %collective-permute-start.5 = (bf16[16,2,48,128]{3,2,1,0:T(8,128)(2,1)S(1)}, bf16[16,2,48,128]{3,2,1,0:T(8,128)(2,1)S(1)}, u32[]{:S(2)}, u32[]{:S(2)}) collective-permute-start(bf16[16,2,48,128]{3,2,1,0:T(8,128)(2,1)S(1)} %collective-permute-done.1.refs_2_), channel_id=1, source_target_pairs={{0,2},{2,0},{1,3},{3,1},{4,6},{6,4},{5,7},{7,5},{8,10},{10,8},{9,1... | collective-permute-start | bytes 1179656 | tf_op jit(solution)/shard_map/ppermute | solution.py:277
  37.8 8.0 %collective-permute-start.4 = (bf16[16,2,48,128]{3,2,1,0:T(8,128)(2,1)S(1)}, bf16[16,2,48,128]{3,2,1,0:T(8,128)(2,1)S(1)}, u32[]{:S(2)}, u32[]{:S(2)}) collective-permute-start(bf16[16,2,48,128]{3,2,1,0:T(8,128)(2,1)S(1)} %collective-permute-done.refs_1_), channel_id=1, source_target_pairs={{0,2},{2,0},{1,3},{3,1},{4,6},{6,4},{5,7},{7,5},{8,10},{10,8},{9,1... | collective-permute-start | bytes 1179656 | tf_op jit(solution)/shard_map/ppermute | solution.py:277
  37.8 10.3 %collective-permute-start.2 = (bf16[16,2,48,128]{3,2,1,0:T(8,128)(2,1)S(1)}, bf16[16,2,48,128]{3,2,1,0:T(8,128)(2,1)S(1)}, u32[]{:S(2)}, u32[]{:S(2)}) collective-permute-start(bf16[16,2,48,128]{3,2,1,0:T(8,128)(2,1)S(1)} %collective-permute-done.refs_1_), channel_id=1, source_target_pairs={{0,64},{2,194},{64,128},{66,2},{128,192},{130,66},{192,0},{194,130... | collective-permute-start | bytes 1179656 | tf_op jit(solution)/shard_map/ppermute | solution.py:284
  43.5 22.0 %copy-start.1 = (bf16[2048,2560]{1,0:T(8,128)(2,1)S(1)}, bf16[2048,2560]{1,0:T(8,128)(2,1)}, u32[]{:S(2)}) copy-start(bf16[2048,2560]{1,0:T(8,128)(2,1)} %copy-done) | copy-start | bytes 31457284
  48.2 2.0 %collective-permute-start.6 = (bf16[16,2,48,128]{3,2,1,0:T(8,128)(2,1)S(1)}, bf16[16,2,48,128]{3,2,1,0:T(8,128)(2,1)S(1)}, u32[]{:S(2)}, u32[]{:S(2)}) collective-permute-start(bf16[16,2,48,128]{3,2,1,0:T(8,128)(2,1)S(1)} %collective-permute-done.2.refs_0_), channel_id=1, source_target_pairs={{0,2},{2,0},{1,3},{3,1},{4,6},{6,4},{5,7},{7,5},{8,10},{10,8},{9,1... | collective-permute-start | bytes 1179656 | tf_op jit(solution)/shard_map/ppermute | solution.py:277
  67.4 9.7 %collective-permute-start.7 = (bf16[48,2560]{1,0:T(8,128)(2,1)S(1)}, bf16[48,2560]{1,0:T(8,128)(2,1)S(1)}, u32[]{:S(2)}, u32[]{:S(2)}) collective-permute-start(bf16[48,2560]{1,0:T(8,128)(2,1)S(1)} %shard_map.72), channel_id=1, source_target_pairs={{0,1},{1,0},{2,3},{3,2},{4,5},{5,4},{6,7},{7,6},{8,9},{9,8},{10,11... | collective-permute-start | bytes 737288 | tf_op jit(solution)/shard_map/ppermute | solution.py:305
  75.2 1.9 %copy-start.2 = (f32[2560]{0:T(1024)S(1)}, f32[2560]{0:T(1024)}, u32[]{:S(2)}) copy-start(f32[2560]{0:T(1024)} %param.11) | copy-start | bytes 30724
  75.2 1.9 %copy-start.3 = (f32[2560]{0:T(1024)S(1)}, f32[2560]{0:T(1024)}, u32[]{:S(2)}) copy-start(f32[2560]{0:T(1024)} %param.10) | copy-start | bytes 30724

commit v7 on v6

--- a/solution.py
+++ b/solution.py
@@ -105,6 +105,14 @@
     scales_copy.wait()
     wide[...] = narrow[...].astype(F32)
 
+    upper = half == 1
+    block = (chunk, across)
+    masks = [jnp.full(block, jnp.where(upper, 3840 << (4 * low), 15 << (4 * low)), jnp.int32) for low in range(2)]
+    middles = [
+        jnp.full(block, jnp.where(upper, 2048.0 * 16**low, 8.0 * 16**low), F32).astype(BF16) for low in range(2)
+    ]
+    shrink = [jnp.where(upper, 0.00390625 / 16**low, 1.0 / 16**low) for low in range(2)]
+
     def step(g, carry):
         fetch(g).wait()
         slot = lax.rem(g, ahead)
@@ -113,17 +121,16 @@
             scales = []
             for low in range(2):
                 at = pl.multiple_of((2 * half + low) * quarter + column, 128)
-                row = wide[pl.ds(g, 1), pl.ds(at, across)] * (0.0625 if low else 1.0)
+                row = wide[pl.ds(g, 1), pl.ds(at, across)] * shrink[low]
                 scales.append(jnp.broadcast_to(row, (chunk, across)).astype(BF16))
             for r in range(0, depth, chunk):
                 words = slots[slot, r : r + chunk, column : column + across]
-                shifted = lax.shift_right_logical(words, jnp.full(words.shape, 8 * half, jnp.int32))
                 for low in range(2):
-                    level = ((shifted & 240) if low else (shifted & 15)).astype(F32).astype(BF16)
+                    level = (words & masks[low]).astype(F32).astype(BF16)
                     out_ref[
                         pl.ds(start + r, chunk),
                         low * quarter + column : low * quarter + column + across,
-                    ] = (level - (128 if low else 8)) * scales[low]
+                    ] = (level - middles[low]) * scales[low]
 
         @pl.when(g + ahead < groups)
         def _():
@@ -290,7 +297,7 @@
     back = send(own, -1)
     queries = regroup(turned_queries)
     near, back, own = lax.optimization_barrier((near, back, own))
-    far = send(near, 1)
+    far = send(back, -1)
     beside, near_beside, back_beside = swap(own), swap(near), swap(back)
     state = attend(queries, [own, near, back], None)
     state = attend(queries, [beside, near_beside, back_beside], state)

time: 78.3 us -> 78.2 us (level)
  waiting for transfers between devices: 14.7 us -> 15.9 us
  starting transfers between devices: 21.5 us -> 20.5 us
    all_to_all x2, waiting for transfers between devices: 9.93 us -> 11.1 us  [regroup(): return lax.all_to_all(a, HEAD_AXES, split_axis=0, concat_axis=0, tiled=True)]
    ppermute x3, starting transfers between devices: 4.66 us -> 3.57 us  [send(): return lax.ppermute(a, (RING, 'c'), hops)]
where the time goes in v7:
time: 78.2 us; the launch traced here: 77.9 us
  Pallas kernels  22.2 us (28%)
  starting transfers between devices  20.5 us (26%)
  waiting for transfers between devices  15.9 us (20%)
  blocking collectives  14.3 us (18%)
  local copies, waits for them, and re-layouts  4.01 us (5%)
  other arithmetic  0.86 us (1%)
    all_to_all x1, blocking collectives, regroup(): return lax.all_to_all(a, HEAD_AXES, split_axis=0, concat_axis=0, tiled=True)  14.3 us
    all_to_all x2, starting transfers between devices, regroup(): return lax.all_to_all(a, HEAD_AXES, split_axis=0, concat_axis=0, tiled=True)  13.1 us
    all_to_all x2, waiting for transfers between devices, regroup(): return lax.all_to_all(a, HEAD_AXES, split_axis=0, concat_axis=0, tiled=True)  11.1 us
    pallas_call x2, Pallas kernels, dequantize(): pl.pallas_call(dequantize_kernel, in_specs=[pl.BlockSpec(memory_space=plt...  9.29 us
    pallas_call x4, Pallas kernels, attend(): pl.pallas_call(functools.partial(attend_kernel, first, last, blocks, len(...  6.68 us
    ppermute x3, waiting for transfers between devices, send(): return lax.ppermute(a, (RING, 'c'), hops)  4.04 us
    unnamed x8, local copies, waits for them, and re-layouts  4.01 us
    pallas_call x2, Pallas kernels, project(): pl.pallas_call(functools.partial(project_kernel, tile), in_specs=[pl.Bloc...  3.8 us
  transfers between devices with their start and end apart: 10, of which 4 were waited for; matrix products, arithmetic and copies ran while one was open for 0% of the time, Pallas kernels for 22%

profile of v7, /device:TPU:6, one launch (start us, length us, event | category | flops | bytes accessed | tf_op | source)
XLA Modules:
  0.0 77.9 jit_solution(9600518468544095570)
XLA Ops:
  0.0 2.4 %shard_map.64 = (bf16[16,48,128]{2,1,0:T(8,128)(2,1)}, bf16[16,2,48,128]{3,2,1,0:T(8,128)(2,1)}) custom-call(s32[3,48]{1,0:T(4,128)} %pos_hbm.1, bf16[48,3,16,128]{3,2,1,0:T(8,128)(2,1)} %x_hbm.1), custom_call_target="tpu_custom_call" | custom-call | tf_op jit(solution)/shard_map/pallas_call | solution.py:67
  2.4 9.6 %all-to-all-start = ((bf16[16,2,48,128]{3,2,1,0:T(8,128)(2,1)}), bf16[16,2,48,128]{3,2,1,0:T(8,128)(2,1)S(1)}, u32[]{:S(2)}, u32[]{:S(2)}) async-start(bf16[16,2,48,128]{3,2,1,0:T(8,128)(2,1)} %get-tuple-element.28), calls=%async_computation | async-start | bytes 786432 | tf_op jit(solution)/shard_map/all_to_all | solution.py:281
  12.0 4.6 %shard_map.65.w_ref = bf16[2048,2560]{1,0:T(8,128)(2,1)S(1)} custom-call(s32[1]{0:T(128)S(6)} %sub.3.half_ref, s32[2048,1280]{1,0:T(8,128)} %words_ref.3, bf16[16,5120]{1,0:T(8,128)(2,1)} %scales_ref.3), custom_call_target="tpu_custom_call" | custom-call | flops 39321600 | bytes 20971520 | tf_op jit(solution)/shard_map/pallas_call | solution.py:148
  16.7 0.0 copy-start
  16.7 4.0 %copy-done = bf16[2048,2560]{1,0:T(8,128)(2,1)} copy-done((bf16[2048,2560]{1,0:T(8,128)(2,1)}, bf16[2048,2560]{1,0:T(8,128)(2,1)S(1)}, u32[]{:S(2)}) %copy-start) | copy-done | bytes 10485784
  20.7 5.8 %all-to-all-done.refs_0_ = bf16[16,2,48,128]{3,2,1,0:T(8,128)(2,1)S(1)} async-done(((bf16[16,2,48,128]{3,2,1,0:T(8,128)(2,1)}), bf16[16,2,48,128]{3,2,1,0:T(8,128)(2,1)S(1)}, u32[]{:S(2)}, u32[]{:S(2)}) %all-to-all-start) | async-done | bytes 393248 | tf_op jit(solution)/shard_map/all_to_all | solution.py:281
  26.5 0.8 %collective-permute-start.1 = (bf16[16,2,48,128]{3,2,1,0:T(8,128)(2,1)S(1)}, bf16[16,2,48,128]{3,2,1,0:T(8,128)(2,1)S(1)}, u32[]{:S(2)}, u32[]{:S(2)}) collective-permute-start(bf16[16,2,48,128]{3,2,1,0:T(8,128)(2,1)S(1)} %all-to-all-done.refs_0_), channel_id=1, source_target_pairs={{0,192},{2,66},{64,0},{66,130},{128,64},{130,194},{192,128},{194,2... | collective-permute-start | bytes 1179656 | tf_op jit(solution)/shard_map/ppermute | solution.py:291
  27.4 2.4 %collective-permute-start = (bf16[16,2,48,128]{3,2,1,0:T(8,128)(2,1)S(1)}, bf16[16,2,48,128]{3,2,1,0:T(8,128)(2,1)S(1)}, u32[]{:S(2)}, u32[]{:S(2)}) collective-permute-start(bf16[16,2,48,128]{3,2,1,0:T(8,128)(2,1)S(1)} %all-to-all-done.refs_0_), channel_id=1, source_target_pairs={{0,64},{2,194},{64,128},{66,2},{128,192},{130,66},{192,0},{194,130... | collective-permute-start | bytes 1179656 | tf_op jit(solution)/shard_map/ppermute | solution.py:291
  29.8 3.5 %all-to-all-start.1 = ((bf16[16,48,128]{2,1,0:T(8,128)(2,1)}), bf16[16,48,128]{2,1,0:T(8,128)(2,1)S(1)}, u32[]{:S(2)}, u32[]{:S(2)}) async-start(bf16[16,48,128]{2,1,0:T(8,128)(2,1)} %get-tuple-element.30), calls=%async_computation.1 | async-start | bytes 393216 | tf_op jit(solution)/shard_map/all_to_all | solution.py:281
  33.3 4.0 %collective-permute-done.1.refs_2_ = bf16[16,2,48,128]{3,2,1,0:T(8,128)(2,1)S(1)} collective-permute-done((bf16[16,2,48,128]{3,2,1,0:T(8,128)(2,1)S(1)}, bf16[16,2,48,128]{3,2,1,0:T(8,128)(2,1)S(1)}, u32[]{:S(2)}, u32[]{:S(2)}) %collective-permute-start.1) | collective-permute-done | bytes 393248 | tf_op jit(solution)/shard_map/ppermute | solution.py:291
  37.3 0.0 collective-permute-done.refs_1_
  37.3 0.0 collective-permute-start.3
  37.3 0.5 collective-permute-start.4
  37.8 0.0 collective-permute-start.5
  37.8 0.3 collective-permute-start.2
  38.2 5.3 %all-to-all-done.1.q_ref = bf16[16,48,128]{2,1,0:T(8,128)(2,1)S(1)} async-done(((bf16[16,48,128]{2,1,0:T(8,128)(2,1)}), bf16[16,48,128]{2,1,0:T(8,128)(2,1)S(1)}, u32[]{:S(2)}, u32[]{:S(2)}) %all-to-all-start.1) | async-done | bytes 196640 | tf_op jit(solution)/shard_map/all_to_all | solution.py:281
  43.5 0.0 copy-start.1
  43.5 2.3 %shard_map.66 = (f32[768,128]{1,0:T(8,128)S(1)}, f32[768,128]{1,0:T(8,128)S(1)}, f32[768,128]{1,0:T(8,128)S(1)}) custom-call(bf16[16,48,128]{2,1,0:T(8,128)(2,1)S(1)} %all-to-all-done.1.q_ref, bf16[16,2,48,128]{3,2,1,0:T(8,128)(2,1)S(1)} %all-to-all-done.refs_0_, bf16[16,2,48,128]{3,2,1,0:T(8,128)(2,1)S(1)} %collective-permute-done.refs_1_, ...), custom_call_target="tpu_custom_call" | custom-call | flops 905969664 | bytes 2555904 | tf_op jit(solution)/shard_map/pallas_call | solution.py:239
  45.8 0.0 collective-permute-done.3.refs_0_
  45.8 0.0 collective-permute-done.4.refs_1_
  45.8 0.0 collective-permute-done.5.refs_2_
  45.8 2.4 %shard_map.67 = (f32[768,128]{1,0:T(8,128)S(1)}, f32[768,128]{1,0:T(8,128)S(1)}, f32[768,128]{1,0:T(8,128)S(1)}) custom-call(bf16[16,48,128]{2,1,0:T(8,128)(2,1)S(1)} %all-to-all-done.1.q_ref, bf16[16,2,48,128]{3,2,1,0:T(8,128)(2,1)S(1)} %collective-permute-done.3.refs_0_, bf16[16,2,48,128]{3,2,1,0:T(8,128)(2,1)S(1)} %collective-permute-done.4.refs_1_, ...), custom_call_target="tpu_custom_call" | custom-call | flops 905969664 | bytes 2555904 | tf_op jit(solution)/shard_map/pallas_call | solution.py:239
  48.2 0.0 collective-permute-done.2.refs_0_
  48.2 0.3 collective-permute-start.6
  48.5 1.0 %shard_map.68 = (f32[768,128]{1,0:T(8,128)S(1)}, f32[768,128]{1,0:T(8,128)S(1)}, f32[768,128]{1,0:T(8,128)S(1)}) custom-call(bf16[16,48,128]{2,1,0:T(8,128)(2,1)S(1)} %all-to-all-done.1.q_ref, bf16[16,2,48,128]{3,2,1,0:T(8,128)(2,1)S(1)} %collective-permute-done.2.refs_0_, f32[768,128]{1,0:T(8,128)S(1)} %get-tuple-element.42.refs_1_, ...), custom_call_target="tpu_custom_call" | custom-call | flops 301989888 | bytes 1769472 | tf_op jit(solution)/shard_map/pallas_call | solution.py:239
  49.5 0.7 collective-permute-done.6.refs_0_
  50.2 1.0 %shard_map.69 = bf16[768,128]{1,0:T(8,128)(2,1)S(1)} custom-call(bf16[16,48,128]{2,1,0:T(8,128)(2,1)S(1)} %all-to-all-done.1.q_ref, bf16[16,2,48,128]{3,2,1,0:T(8,128)(2,1)S(1)} %collective-permute-done.6.refs_0_, f32[768,128]{1,0:T(8,128)S(1)} %get-tuple-element.45.refs_1_, f32[768,128]{1,0:T(8,128)S(1)} %get-tuple-element.46.refs_2_, ...), custom_call_target="tpu_custom_call" | custom-call | flops 301989888 | bytes 1769472 | tf_op jit(solution)/shard_map/pallas_call | solution.py:239
  51.2 14.3 %all_to_all.15.x_ref = bf16[16,48,128]{2,1,0:T(8,128)(2,1)S(1)} all-to-all(bf16[16,48,128]{2,1,0:T(8,128)(2,1)S(1)} %bitcast.2), channel_id=1, replica_groups=mesh['x'=4,'zh'=4,'zl'=2,'yl'=2,'c'=2,'yh'=2] {'zh','zl','yl'}, dimensions={0} | all-to-all | bytes 393216 | tf_op jit(solution)/shard_map/all_to_all | solution.py:281
  65.5 0.0 copy-done.1
  65.5 1.9 %shard_map.72 = bf16[48,2560]{1,0:T(8,128)(2,1)S(1)} custom-call(bf16[16,48,128]{2,1,0:T(8,128)(2,1)S(1)} %all_to_all.15.x_ref, bf16[2048,2560]{1,0:T(8,128)(2,1)S(1)} %copy-done.1), custom_call_target="tpu_custom_call" | custom-call | flops 503316480 | bytes 10485760 | tf_op jit(solution)/shard_map/pallas_call | solution.py:259
  67.4 3.0 %collective-permute-start.7 = (bf16[48,2560]{1,0:T(8,128)(2,1)S(1)}, bf16[48,2560]{1,0:T(8,128)(2,1)S(1)}, u32[]{:S(2)}, u32[]{:S(2)}) collective-permute-start(bf16[48,2560]{1,0:T(8,128)(2,1)S(1)} %shard_map.72), channel_id=1, source_target_pairs={{0,1},{1,0},{2,3},{3,2},{4,5},{5,4},{6,7},{7,6},{8,9},{9,8},{10,11... | collective-permute-start | bytes 737288 | tf_op jit(solution)/shard_map/ppermute | solution.py:312
  70.4 4.6 %shard_map.70.w_ref = bf16[2048,2560]{1,0:T(8,128)(2,1)S(1)} custom-call(s32[1]{0:T(128)} %bitcast.half_ref, s32[2048,1280]{1,0:T(8,128)} %words_ref.3, bf16[16,5120]{1,0:T(8,128)(2,1)} %scales_ref.3), custom_call_target="tpu_custom_call" | custom-call | flops 39321600 | bytes 20971520 | tf_op jit(solution)/shard_map/pallas_call | solution.py:148
  75.1 0.0 copy-start.2
  75.1 0.0 copy-start.3
  75.1 1.9 %shard_map.71 = f32[48,2560]{1,0:T(8,128)S(1)} custom-call(bf16[16,48,128]{2,1,0:T(8,128)(2,1)S(1)} %all_to_all.15.x_ref, bf16[2048,2560]{1,0:T(8,128)(2,1)S(1)} %shard_map.70.w_ref), custom_call_target="tpu_custom_call" | custom-call | flops 503316480 | bytes 10485760 | tf_op jit(solution)/shard_map/pallas_call | solution.py:259
  77.0 0.0 collective-permute-done.7
  77.0 0.0 copy-done.2
  77.0 0.0 copy-done.3
  77.0 0.9 %add_multiply_fusion = f32[48,2560]{1,0:T(8,128)} fusion(f32[48,2560]{1,0:T(8,128)S(1)} %shard_map.71, bf16[48,2560]{1,0:T(8,128)(2,1)S(1)} %collective-permute-done.7, f32[2560]{0:T(1024)S(1)} %copy-done.2, f32[2560]{0:T(1024)S(1)} %copy-done.3), kind=kLoop, calls=%fused_computation | loop fusion | flops 491520 | bytes 1249280 | tf_op jit(solution)/shard_map/mul | solution.py:314
Async XLA Ops:
  2.4 24.1 %all-to-all-start = ((bf16[16,2,48,128]{3,2,1,0:T(8,128)(2,1)}), bf16[16,2,48,128]{3,2,1,0:T(8,128)(2,1)S(1)}, u32[]{:S(2)}, u32[]{:S(2)}) async-start(bf16[16,2,48,128]{3,2,1,0:T(8,128)(2,1)} %get-tuple-element.28), calls=%async_computation | async-start | bytes 786432 | tf_op jit(solution)/shard_map/all_to_all | solution.py:281
  16.7 4.0 %copy-start = (bf16[2048,2560]{1,0:T(8,128)(2,1)}, bf16[2048,2560]{1,0:T(8,128)(2,1)S(1)}, u32[]{:S(2)}) copy-start(bf16[2048,2560]{1,0:T(8,128)(2,1)S(1)} %shard_map.65.w_ref) | copy-start | bytes 31457284
  26.5 10.8 %collective-permute-start.1 = (bf16[16,2,48,128]{3,2,1,0:T(8,128)(2,1)S(1)}, bf16[16,2,48,128]{3,2,1,0:T(8,128)(2,1)S(1)}, u32[]{:S(2)}, u32[]{:S(2)}) collective-permute-start(bf16[16,2,48,128]{3,2,1,0:T(8,128)(2,1)S(1)} %all-to-all-done.refs_0_), channel_id=1, source_target_pairs={{0,192},{2,66},{64,0},{66,130},{128,64},{130,194},{192,128},{194,2... | collective-permute-start | bytes 1179656 | tf_op jit(solution)/shard_map/ppermute | solution.py:291
  27.4 10.0 %collective-permute-start = (bf16[16,2,48,128]{3,2,1,0:T(8,128)(2,1)S(1)}, bf16[16,2,48,128]{3,2,1,0:T(8,128)(2,1)S(1)}, u32[]{:S(2)}, u32[]{:S(2)}) collective-permute-start(bf16[16,2,48,128]{3,2,1,0:T(8,128)(2,1)S(1)} %all-to-all-done.refs_0_), channel_id=1, source_target_pairs={{0,64},{2,194},{64,128},{66,2},{128,192},{130,66},{192,0},{194,130... | collective-permute-start | bytes 1179656 | tf_op jit(solution)/shard_map/ppermute | solution.py:291
  29.8 13.7 %all-to-all-start.1 = ((bf16[16,48,128]{2,1,0:T(8,128)(2,1)}), bf16[16,48,128]{2,1,0:T(8,128)(2,1)S(1)}, u32[]{:S(2)}, u32[]{:S(2)}) async-start(bf16[16,48,128]{2,1,0:T(8,128)(2,1)} %get-tuple-element.30), calls=%async_computation.1 | async-start | bytes 393216 | tf_op jit(solution)/shard_map/all_to_all | solution.py:281
  37.3 8.5 %collective-permute-start.3 = (bf16[16,2,48,128]{3,2,1,0:T(8,128)(2,1)S(1)}, bf16[16,2,48,128]{3,2,1,0:T(8,128)(2,1)S(1)}, u32[]{:S(2)}, u32[]{:S(2)}) collective-permute-start(bf16[16,2,48,128]{3,2,1,0:T(8,128)(2,1)S(1)} %all-to-all-done.refs_0_), channel_id=1, source_target_pairs={{0,2},{2,0},{1,3},{3,1},{4,6},{6,4},{5,7},{7,5},{8,10},{10,8},{9,1... | collective-permute-start | bytes 1179656 | tf_op jit(solution)/shard_map/ppermute | solution.py:284
  37.3 8.5 %collective-permute-start.4 = (bf16[16,2,48,128]{3,2,1,0:T(8,128)(2,1)S(1)}, bf16[16,2,48,128]{3,2,1,0:T(8,128)(2,1)S(1)}, u32[]{:S(2)}, u32[]{:S(2)}) collective-permute-start(bf16[16,2,48,128]{3,2,1,0:T(8,128)(2,1)S(1)} %collective-permute-done.refs_1_), channel_id=1, source_target_pairs={{0,2},{2,0},{1,3},{3,1},{4,6},{6,4},{5,7},{7,5},{8,10},{10,8},{9,1... | collective-permute-start | bytes 1179656 | tf_op jit(solution)/shard_map/ppermute | solution.py:284
  37.8 8.0 %collective-permute-start.5 = (bf16[16,2,48,128]{3,2,1,0:T(8,128)(2,1)S(1)}, bf16[16,2,48,128]{3,2,1,0:T(8,128)(2,1)S(1)}, u32[]{:S(2)}, u32[]{:S(2)}) collective-permute-start(bf16[16,2,48,128]{3,2,1,0:T(8,128)(2,1)S(1)} %collective-permute-done.1.refs_2_), channel_id=1, source_target_pairs={{0,2},{2,0},{1,3},{3,1},{4,6},{6,4},{5,7},{7,5},{8,10},{10,8},{9,1... | collective-permute-start | bytes 1179656 | tf_op jit(solution)/shard_map/ppermute | solution.py:284
  37.8 10.3 %collective-permute-start.2 = (bf16[16,2,48,128]{3,2,1,0:T(8,128)(2,1)S(1)}, bf16[16,2,48,128]{3,2,1,0:T(8,128)(2,1)S(1)}, u32[]{:S(2)}, u32[]{:S(2)}) collective-permute-start(bf16[16,2,48,128]{3,2,1,0:T(8,128)(2,1)S(1)} %collective-permute-done.1.refs_2_), channel_id=1, source_target_pairs={{0,192},{2,66},{64,0},{66,130},{128,64},{130,194},{192,128},{194,2... | collective-permute-start | bytes 1179656 | tf_op jit(solution)/shard_map/ppermute | solution.py:291
  43.5 22.0 %copy-start.1 = (bf16[2048,2560]{1,0:T(8,128)(2,1)S(1)}, bf16[2048,2560]{1,0:T(8,128)(2,1)}, u32[]{:S(2)}) copy-start(bf16[2048,2560]{1,0:T(8,128)(2,1)} %copy-done) | copy-start | bytes 31457284
  48.2 2.0 %collective-permute-start.6 = (bf16[16,2,48,128]{3,2,1,0:T(8,128)(2,1)S(1)}, bf16[16,2,48,128]{3,2,1,0:T(8,128)(2,1)S(1)}, u32[]{:S(2)}, u32[]{:S(2)}) collective-permute-start(bf16[16,2,48,128]{3,2,1,0:T(8,128)(2,1)S(1)} %collective-permute-done.2.refs_0_), channel_id=1, source_target_pairs={{0,2},{2,0},{1,3},{3,1},{4,6},{6,4},{5,7},{7,5},{8,10},{10,8},{9,1... | collective-permute-start | bytes 1179656 | tf_op jit(solution)/shard_map/ppermute | solution.py:284
  67.4 9.6 %collective-permute-start.7 = (bf16[48,2560]{1,0:T(8,128)(2,1)S(1)}, bf16[48,2560]{1,0:T(8,128)(2,1)S(1)}, u32[]{:S(2)}, u32[]{:S(2)}) collective-permute-start(bf16[48,2560]{1,0:T(8,128)(2,1)S(1)} %shard_map.72), channel_id=1, source_target_pairs={{0,1},{1,0},{2,3},{3,2},{4,5},{5,4},{6,7},{7,6},{8,9},{9,8},{10,11... | collective-permute-start | bytes 737288 | tf_op jit(solution)/shard_map/ppermute | solution.py:312
  75.1 1.9 %copy-start.2 = (f32[2560]{0:T(1024)S(1)}, f32[2560]{0:T(1024)}, u32[]{:S(2)}) copy-start(f32[2560]{0:T(1024)} %param.11) | copy-start | bytes 30724
  75.1 1.9 %copy-start.3 = (f32[2560]{0:T(1024)S(1)}, f32[2560]{0:T(1024)}, u32[]{:S(2)}) copy-start(f32[2560]{0:T(1024)} %param.10) | copy-start | bytes 30724

commit v8 on v7

--- a/solution.py
+++ b/solution.py
@@ -48,7 +48,7 @@
     sine_even = jnp.where(is_even, -sine, 0.0)
     sine_odd = jnp.where(is_even, 0.0, sine)
     x_copy.wait()
-    wide[...] = x_ref[...].astype(F32).reshape(tokens * kinds * heads, width)
+    wide[: tokens * kinds * heads, :] = x_ref[...].astype(F32).reshape(tokens * kinds * heads, width)
     for kind in range(kinds):
         for head in range(heads):
             x = wide[pl.ds(kind * heads + head, tokens, stride=kinds * heads), :]
@@ -75,7 +75,7 @@
         scratch_shapes=[
             pltpu.VMEM(positions.shape, positions.dtype),
             pltpu.VMEM(head_inputs.shape, head_inputs.dtype),
-            pltpu.VMEM((tokens * kinds * heads, width), F32),
+            pltpu.VMEM(((tokens + 1) * kinds * heads, width), F32),
             pltpu.SemaphoreType.DMA((2,)),
         ],
         compiler_params=pltpu.CompilerParams(vmem_limit_bytes=16 * 1024 * 1024),

time: 78.2 us -> 78.2 us (level)
  no operation moved by 1% of the time
where the time goes in v8:
time: 78.2 us; the launch traced here: 77.9 us
  Pallas kernels  22.2 us (28%)
  starting transfers between devices  20.5 us (26%)
  waiting for transfers between devices  15.9 us (20%)
  blocking collectives  14.3 us (18%)
  local copies, waits for them, and re-layouts  4.01 us (5%)
  other arithmetic  0.86 us (1%)
    all_to_all x1, blocking collectives, regroup(): return lax.all_to_all(a, HEAD_AXES, split_axis=0, concat_axis=0, tiled=True)  14.3 us
    all_to_all x2, starting transfers between devices, regroup(): return lax.all_to_all(a, HEAD_AXES, split_axis=0, concat_axis=0, tiled=True)  13.1 us
    all_to_all x2, waiting for transfers between devices, regroup(): return lax.all_to_all(a, HEAD_AXES, split_axis=0, concat_axis=0, tiled=True)  11.1 us
    pallas_call x2, Pallas kernels, dequantize(): pl.pallas_call(dequantize_kernel, in_specs=[pl.BlockSpec(memory_space=plt...  9.29 us
    pallas_call x4, Pallas kernels, attend(): pl.pallas_call(functools.partial(attend_kernel, first, last, blocks, len(...  6.68 us
    ppermute x3, waiting for transfers between devices, send(): return lax.ppermute(a, (RING, 'c'), hops)  4.04 us
    unnamed x8, local copies, waits for them, and re-layouts  4.01 us
    pallas_call x2, Pallas kernels, project(): pl.pallas_call(functools.partial(project_kernel, tile), in_specs=[pl.Bloc...  3.8 us
  transfers between devices with their start and end apart: 10, of which 4 were waited for; matrix products, arithmetic and copies ran while one was open for 0% of the time, Pallas kernels for 22%

profile of v8, /device:TPU:6, one launch (start us, length us, event | category | flops | bytes accessed | tf_op | source)
XLA Modules:
  0.0 77.9 jit_solution(12596621806140679315)
XLA Ops:
  0.0 2.4 %shard_map.64 = (bf16[16,48,128]{2,1,0:T(8,128)(2,1)}, bf16[16,2,48,128]{3,2,1,0:T(8,128)(2,1)}) custom-call(s32[3,48]{1,0:T(4,128)} %pos_hbm.1, bf16[48,3,16,128]{3,2,1,0:T(8,128)(2,1)} %x_hbm.1), custom_call_target="tpu_custom_call" | custom-call | tf_op jit(solution)/shard_map/pallas_call | solution.py:67
  2.4 9.6 %all-to-all-start = ((bf16[16,2,48,128]{3,2,1,0:T(8,128)(2,1)}), bf16[16,2,48,128]{3,2,1,0:T(8,128)(2,1)S(1)}, u32[]{:S(2)}, u32[]{:S(2)}) async-start(bf16[16,2,48,128]{3,2,1,0:T(8,128)(2,1)} %get-tuple-element.28), calls=%async_computation | async-start | bytes 786432 | tf_op jit(solution)/shard_map/all_to_all | solution.py:281
  12.0 4.6 %shard_map.65.w_ref = bf16[2048,2560]{1,0:T(8,128)(2,1)S(1)} custom-call(s32[1]{0:T(128)S(6)} %sub.3.half_ref, s32[2048,1280]{1,0:T(8,128)} %words_ref.3, bf16[16,5120]{1,0:T(8,128)(2,1)} %scales_ref.3), custom_call_target="tpu_custom_call" | custom-call | flops 39321600 | bytes 20971520 | tf_op jit(solution)/shard_map/pallas_call | solution.py:148
  16.7 0.0 copy-start
  16.7 4.0 %copy-done = bf16[2048,2560]{1,0:T(8,128)(2,1)} copy-done((bf16[2048,2560]{1,0:T(8,128)(2,1)}, bf16[2048,2560]{1,0:T(8,128)(2,1)S(1)}, u32[]{:S(2)}) %copy-start) | copy-done | bytes 10485784
  20.7 5.8 %all-to-all-done.refs_0_ = bf16[16,2,48,128]{3,2,1,0:T(8,128)(2,1)S(1)} async-done(((bf16[16,2,48,128]{3,2,1,0:T(8,128)(2,1)}), bf16[16,2,48,128]{3,2,1,0:T(8,128)(2,1)S(1)}, u32[]{:S(2)}, u32[]{:S(2)}) %all-to-all-start) | async-done | bytes 393248 | tf_op jit(solution)/shard_map/all_to_all | solution.py:281
  26.5 0.8 %collective-permute-start.1 = (bf16[16,2,48,128]{3,2,1,0:T(8,128)(2,1)S(1)}, bf16[16,2,48,128]{3,2,1,0:T(8,128)(2,1)S(1)}, u32[]{:S(2)}, u32[]{:S(2)}) collective-permute-start(bf16[16,2,48,128]{3,2,1,0:T(8,128)(2,1)S(1)} %all-to-all-done.refs_0_), channel_id=1, source_target_pairs={{0,192},{2,66},{64,0},{66,130},{128,64},{130,194},{192,128},{194,2... | collective-permute-start | bytes 1179656 | tf_op jit(solution)/shard_map/ppermute | solution.py:291
  27.4 2.4 %collective-permute-start = (bf16[16,2,48,128]{3,2,1,0:T(8,128)(2,1)S(1)}, bf16[16,2,48,128]{3,2,1,0:T(8,128)(2,1)S(1)}, u32[]{:S(2)}, u32[]{:S(2)}) collective-permute-start(bf16[16,2,48,128]{3,2,1,0:T(8,128)(2,1)S(1)} %all-to-all-done.refs_0_), channel_id=1, source_target_pairs={{0,64},{2,194},{64,128},{66,2},{128,192},{130,66},{192,0},{194,130... | collective-permute-start | bytes 1179656 | tf_op jit(solution)/shard_map/ppermute | solution.py:291
  29.8 3.5 %all-to-all-start.1 = ((bf16[16,48,128]{2,1,0:T(8,128)(2,1)}), bf16[16,48,128]{2,1,0:T(8,128)(2,1)S(1)}, u32[]{:S(2)}, u32[]{:S(2)}) async-start(bf16[16,48,128]{2,1,0:T(8,128)(2,1)} %get-tuple-element.30), calls=%async_computation.1 | async-start | bytes 393216 | tf_op jit(solution)/shard_map/all_to_all | solution.py:281
  33.3 4.0 %collective-permute-done.1.refs_2_ = bf16[16,2,48,128]{3,2,1,0:T(8,128)(2,1)S(1)} collective-permute-done((bf16[16,2,48,128]{3,2,1,0:T(8,128)(2,1)S(1)}, bf16[16,2,48,128]{3,2,1,0:T(8,128)(2,1)S(1)}, u32[]{:S(2)}, u32[]{:S(2)}) %collective-permute-start.1) | collective-permute-done | bytes 393248 | tf_op jit(solution)/shard_map/ppermute | solution.py:291
  37.3 0.0 collective-permute-done.refs_1_
  37.3 0.0 collective-permute-start.3
  37.3 0.5 collective-permute-start.4
  37.8 0.0 collective-permute-start.5
  37.8 0.3 collective-permute-start.2
  38.2 5.3 %all-to-all-done.1.q_ref = bf16[16,48,128]{2,1,0:T(8,128)(2,1)S(1)} async-done(((bf16[16,48,128]{2,1,0:T(8,128)(2,1)}), bf16[16,48,128]{2,1,0:T(8,128)(2,1)S(1)}, u32[]{:S(2)}, u32[]{:S(2)}) %all-to-all-start.1) | async-done | bytes 196640 | tf_op jit(solution)/shard_map/all_to_all | solution.py:281
  43.5 0.0 copy-start.1
  43.5 2.3 %shard_map.66 = (f32[768,128]{1,0:T(8,128)S(1)}, f32[768,128]{1,0:T(8,128)S(1)}, f32[768,128]{1,0:T(8,128)S(1)}) custom-call(bf16[16,48,128]{2,1,0:T(8,128)(2,1)S(1)} %all-to-all-done.1.q_ref, bf16[16,2,48,128]{3,2,1,0:T(8,128)(2,1)S(1)} %all-to-all-done.refs_0_, bf16[16,2,48,128]{3,2,1,0:T(8,128)(2,1)S(1)} %collective-permute-done.refs_1_, ...), custom_call_target="tpu_custom_call" | custom-call | flops 905969664 | bytes 2555904 | tf_op jit(solution)/shard_map/pallas_call | solution.py:239
  45.8 0.0 collective-permute-done.3.refs_0_
  45.8 0.0 collective-permute-done.4.refs_1_
  45.8 0.0 collective-permute-done.5.refs_2_
  45.8 2.4 %shard_map.67 = (f32[768,128]{1,0:T(8,128)S(1)}, f32[768,128]{1,0:T(8,128)S(1)}, f32[768,128]{1,0:T(8,128)S(1)}) custom-call(bf16[16,48,128]{2,1,0:T(8,128)(2,1)S(1)} %all-to-all-done.1.q_ref, bf16[16,2,48,128]{3,2,1,0:T(8,128)(2,1)S(1)} %collective-permute-done.3.refs_0_, bf16[16,2,48,128]{3,2,1,0:T(8,128)(2,1)S(1)} %collective-permute-done.4.refs_1_, ...), custom_call_target="tpu_custom_call" | custom-call | flops 905969664 | bytes 2555904 | tf_op jit(solution)/shard_map/pallas_call | solution.py:239
  48.2 0.0 collective-permute-done.2.refs_0_
  48.2 0.3 collective-permute-start.6
  48.5 1.0 %shard_map.68 = (f32[768,128]{1,0:T(8,128)S(1)}, f32[768,128]{1,0:T(8,128)S(1)}, f32[768,128]{1,0:T(8,128)S(1)}) custom-call(bf16[16,48,128]{2,1,0:T(8,128)(2,1)S(1)} %all-to-all-done.1.q_ref, bf16[16,2,48,128]{3,2,1,0:T(8,128)(2,1)S(1)} %collective-permute-done.2.refs_0_, f32[768,128]{1,0:T(8,128)S(1)} %get-tuple-element.42.refs_1_, ...), custom_call_target="tpu_custom_call" | custom-call | flops 301989888 | bytes 1769472 | tf_op jit(solution)/shard_map/pallas_call | solution.py:239
  49.5 0.7 collective-permute-done.6.refs_0_
  50.2 1.0 %shard_map.69 = bf16[768,128]{1,0:T(8,128)(2,1)S(1)} custom-call(bf16[16,48,128]{2,1,0:T(8,128)(2,1)S(1)} %all-to-all-done.1.q_ref, bf16[16,2,48,128]{3,2,1,0:T(8,128)(2,1)S(1)} %collective-permute-done.6.refs_0_, f32[768,128]{1,0:T(8,128)S(1)} %get-tuple-element.45.refs_1_, f32[768,128]{1,0:T(8,128)S(1)} %get-tuple-element.46.refs_2_, ...), custom_call_target="tpu_custom_call" | custom-call | flops 301989888 | bytes 1769472 | tf_op jit(solution)/shard_map/pallas_call | solution.py:239
  51.2 14.3 %all_to_all.15.x_ref = bf16[16,48,128]{2,1,0:T(8,128)(2,1)S(1)} all-to-all(bf16[16,48,128]{2,1,0:T(8,128)(2,1)S(1)} %bitcast.2), channel_id=1, replica_groups=mesh['x'=4,'zh'=4,'zl'=2,'yl'=2,'c'=2,'yh'=2] {'zh','zl','yl'}, dimensions={0} | all-to-all | bytes 393216 | tf_op jit(solution)/shard_map/all_to_all | solution.py:281
  65.5 0.0 copy-done.1
  65.5 1.9 %shard_map.72 = bf16[48,2560]{1,0:T(8,128)(2,1)S(1)} custom-call(bf16[16,48,128]{2,1,0:T(8,128)(2,1)S(1)} %all_to_all.15.x_ref, bf16[2048,2560]{1,0:T(8,128)(2,1)S(1)} %copy-done.1), custom_call_target="tpu_custom_call" | custom-call | flops 503316480 | bytes 10485760 | tf_op jit(solution)/shard_map/pallas_call | solution.py:259
  67.4 3.0 %collective-permute-start.7 = (bf16[48,2560]{1,0:T(8,128)(2,1)S(1)}, bf16[48,2560]{1,0:T(8,128)(2,1)S(1)}, u32[]{:S(2)}, u32[]{:S(2)}) collective-permute-start(bf16[48,2560]{1,0:T(8,128)(2,1)S(1)} %shard_map.72), channel_id=1, source_target_pairs={{0,1},{1,0},{2,3},{3,2},{4,5},{5,4},{6,7},{7,6},{8,9},{9,8},{10,11... | collective-permute-start | bytes 737288 | tf_op jit(solution)/shard_map/ppermute | solution.py:312
  70.4 4.6 %shard_map.70.w_ref = bf16[2048,2560]{1,0:T(8,128)(2,1)S(1)} custom-call(s32[1]{0:T(128)} %bitcast.half_ref, s32[2048,1280]{1,0:T(8,128)} %words_ref.3, bf16[16,5120]{1,0:T(8,128)(2,1)} %scales_ref.3), custom_call_target="tpu_custom_call" | custom-call | flops 39321600 | bytes 20971520 | tf_op jit(solution)/shard_map/pallas_call | solution.py:148
  75.1 0.0 copy-start.2
  75.1 0.0 copy-start.3
  75.1 1.9 %shard_map.71 = f32[48,2560]{1,0:T(8,128)S(1)} custom-call(bf16[16,48,128]{2,1,0:T(8,128)(2,1)S(1)} %all_to_all.15.x_ref, bf16[2048,2560]{1,0:T(8,128)(2,1)S(1)} %shard_map.70.w_ref), custom_call_target="tpu_custom_call" | custom-call | flops 503316480 | bytes 10485760 | tf_op jit(solution)/shard_map/pallas_call | solution.py:259
  77.0 0.0 collective-permute-done.7
  77.0 0.0 copy-done.2
  77.0 0.0 copy-done.3
  77.0 0.9 %add_multiply_fusion = f32[48,2560]{1,0:T(8,128)} fusion(f32[48,2560]{1,0:T(8,128)S(1)} %shard_map.71, bf16[48,2560]{1,0:T(8,128)(2,1)S(1)} %collective-permute-done.7, f32[2560]{0:T(1024)S(1)} %copy-done.2, f32[2560]{0:T(1024)S(1)} %copy-done.3), kind=kLoop, calls=%fused_computation | loop fusion | flops 491520 | bytes 1249280 | tf_op jit(solution)/shard_map/mul | solution.py:314
Async XLA Ops:
  2.4 24.1 %all-to-all-start = ((bf16[16,2,48,128]{3,2,1,0:T(8,128)(2,1)}), bf16[16,2,48,128]{3,2,1,0:T(8,128)(2,1)S(1)}, u32[]{:S(2)}, u32[]{:S(2)}) async-start(bf16[16,2,48,128]{3,2,1,0:T(8,128)(2,1)} %get-tuple-element.28), calls=%async_computation | async-start | bytes 786432 | tf_op jit(solution)/shard_map/all_to_all | solution.py:281
  16.7 4.0 %copy-start = (bf16[2048,2560]{1,0:T(8,128)(2,1)}, bf16[2048,2560]{1,0:T(8,128)(2,1)S(1)}, u32[]{:S(2)}) copy-start(bf16[2048,2560]{1,0:T(8,128)(2,1)S(1)} %shard_map.65.w_ref) | copy-start | bytes 31457284
  26.5 10.8 %collective-permute-start.1 = (bf16[16,2,48,128]{3,2,1,0:T(8,128)(2,1)S(1)}, bf16[16,2,48,128]{3,2,1,0:T(8,128)(2,1)S(1)}, u32[]{:S(2)}, u32[]{:S(2)}) collective-permute-start(bf16[16,2,48,128]{3,2,1,0:T(8,128)(2,1)S(1)} %all-to-all-done.refs_0_), channel_id=1, source_target_pairs={{0,192},{2,66},{64,0},{66,130},{128,64},{130,194},{192,128},{194,2... | collective-permute-start | bytes 1179656 | tf_op jit(solution)/shard_map/ppermute | solution.py:291
  27.4 10.0 %collective-permute-start = (bf16[16,2,48,128]{3,2,1,0:T(8,128)(2,1)S(1)}, bf16[16,2,48,128]{3,2,1,0:T(8,128)(2,1)S(1)}, u32[]{:S(2)}, u32[]{:S(2)}) collective-permute-start(bf16[16,2,48,128]{3,2,1,0:T(8,128)(2,1)S(1)} %all-to-all-done.refs_0_), channel_id=1, source_target_pairs={{0,64},{2,194},{64,128},{66,2},{128,192},{130,66},{192,0},{194,130... | collective-permute-start | bytes 1179656 | tf_op jit(solution)/shard_map/ppermute | solution.py:291
  29.8 13.7 %all-to-all-start.1 = ((bf16[16,48,128]{2,1,0:T(8,128)(2,1)}), bf16[16,48,128]{2,1,0:T(8,128)(2,1)S(1)}, u32[]{:S(2)}, u32[]{:S(2)}) async-start(bf16[16,48,128]{2,1,0:T(8,128)(2,1)} %get-tuple-element.30), calls=%async_computation.1 | async-start | bytes 393216 | tf_op jit(solution)/shard_map/all_to_all | solution.py:281
  37.3 8.5 %collective-permute-start.3 = (bf16[16,2,48,128]{3,2,1,0:T(8,128)(2,1)S(1)}, bf16[16,2,48,128]{3,2,1,0:T(8,128)(2,1)S(1)}, u32[]{:S(2)}, u32[]{:S(2)}) collective-permute-start(bf16[16,2,48,128]{3,2,1,0:T(8,128)(2,1)S(1)} %all-to-all-done.refs_0_), channel_id=1, source_target_pairs={{0,2},{2,0},{1,3},{3,1},{4,6},{6,4},{5,7},{7,5},{8,10},{10,8},{9,1... | collective-permute-start | bytes 1179656 | tf_op jit(solution)/shard_map/ppermute | solution.py:284
  37.3 8.5 %collective-permute-start.4 = (bf16[16,2,48,128]{3,2,1,0:T(8,128)(2,1)S(1)}, bf16[16,2,48,128]{3,2,1,0:T(8,128)(2,1)S(1)}, u32[]{:S(2)}, u32[]{:S(2)}) collective-permute-start(bf16[16,2,48,128]{3,2,1,0:T(8,128)(2,1)S(1)} %collective-permute-done.refs_1_), channel_id=1, source_target_pairs={{0,2},{2,0},{1,3},{3,1},{4,6},{6,4},{5,7},{7,5},{8,10},{10,8},{9,1... | collective-permute-start | bytes 1179656 | tf_op jit(solution)/shard_map/ppermute | solution.py:284
  37.8 8.0 %collective-permute-start.5 = (bf16[16,2,48,128]{3,2,1,0:T(8,128)(2,1)S(1)}, bf16[16,2,48,128]{3,2,1,0:T(8,128)(2,1)S(1)}, u32[]{:S(2)}, u32[]{:S(2)}) collective-permute-start(bf16[16,2,48,128]{3,2,1,0:T(8,128)(2,1)S(1)} %collective-permute-done.1.refs_2_), channel_id=1, source_target_pairs={{0,2},{2,0},{1,3},{3,1},{4,6},{6,4},{5,7},{7,5},{8,10},{10,8},{9,1... | collective-permute-start | bytes 1179656 | tf_op jit(solution)/shard_map/ppermute | solution.py:284
  37.8 10.3 %collective-permute-start.2 = (bf16[16,2,48,128]{3,2,1,0:T(8,128)(2,1)S(1)}, bf16[16,2,48,128]{3,2,1,0:T(8,128)(2,1)S(1)}, u32[]{:S(2)}, u32[]{:S(2)}) collective-permute-start(bf16[16,2,48,128]{3,2,1,0:T(8,128)(2,1)S(1)} %collective-permute-done.1.refs_2_), channel_id=1, source_target_pairs={{0,192},{2,66},{64,0},{66,130},{128,64},{130,194},{192,128},{194,2... | collective-permute-start | bytes 1179656 | tf_op jit(solution)/shard_map/ppermute | solution.py:291
  43.5 22.0 %copy-start.1 = (bf16[2048,2560]{1,0:T(8,128)(2,1)S(1)}, bf16[2048,2560]{1,0:T(8,128)(2,1)}, u32[]{:S(2)}) copy-start(bf16[2048,2560]{1,0:T(8,128)(2,1)} %copy-done) | copy-start | bytes 31457284
  48.2 2.0 %collective-permute-start.6 = (bf16[16,2,48,128]{3,2,1,0:T(8,128)(2,1)S(1)}, bf16[16,2,48,128]{3,2,1,0:T(8,128)(2,1)S(1)}, u32[]{:S(2)}, u32[]{:S(2)}) collective-permute-start(bf16[16,2,48,128]{3,2,1,0:T(8,128)(2,1)S(1)} %collective-permute-done.2.refs_0_), channel_id=1, source_target_pairs={{0,2},{2,0},{1,3},{3,1},{4,6},{6,4},{5,7},{7,5},{8,10},{10,8},{9,1... | collective-permute-start | bytes 1179656 | tf_op jit(solution)/shard_map/ppermute | solution.py:284
  67.4 9.6 %collective-permute-start.7 = (bf16[48,2560]{1,0:T(8,128)(2,1)S(1)}, bf16[48,2560]{1,0:T(8,128)(2,1)S(1)}, u32[]{:S(2)}, u32[]{:S(2)}) collective-permute-start(bf16[48,2560]{1,0:T(8,128)(2,1)S(1)} %shard_map.72), channel_id=1, source_target_pairs={{0,1},{1,0},{2,3},{3,2},{4,5},{5,4},{6,7},{7,6},{8,9},{9,8},{10,11... | collective-permute-start | bytes 737288 | tf_op jit(solution)/shard_map/ppermute | solution.py:312
  75.1 1.9 %copy-start.2 = (f32[2560]{0:T(1024)S(1)}, f32[2560]{0:T(1024)}, u32[]{:S(2)}) copy-start(f32[2560]{0:T(1024)} %param.11) | copy-start | bytes 30724
  75.1 1.9 %copy-start.3 = (f32[2560]{0:T(1024)S(1)}, f32[2560]{0:T(1024)}, u32[]{:S(2)}) copy-start(f32[2560]{0:T(1024)} %param.10) | copy-start | bytes 30724

commit v9 on v8

--- a/solution.py
+++ b/solution.py
@@ -163,6 +163,102 @@
         compiler_params=pltpu.CompilerParams(vmem_limit_bytes=12 * 1024 * 1024),
         cost_estimate=pl.CostEstimate(flops=rows * quarter * 15, bytes_accessed=rows * quarter * 8, transcendentals=0),
     )(half, in_hbm(code_words), in_hbm(group_scales))
+
+
+def keep_kernel(half_ref, words_ref, scales_ref, x_ref, out_ref, slots, narrow, wide, even, odd, x_pairs, sems):
+    rows, quarter = words_ref.shape
+    groups, depth = scales_ref.shape[0], rows // scales_ref.shape[0]
+    half = half_ref[0]
+    chunk, across, tile = 16, 256, 512
+    scales_copy = pltpu.make_async_copy(scales_ref, narrow, sems.at[groups])
+    scales_copy.start()
+
+    def fetch(g):
+        start = pl.multiple_of(g * depth, depth)
+        return pltpu.make_async_copy(words_ref.at[pl.ds(start, depth)], slots.at[g], sems.at[g])
+
+    for g in range(groups):
+        fetch(g).start()
+    for pair in range(groups // 2):
+        x_pairs[pair] = jnp.concatenate([x_ref[2 * pair], x_ref[2 * pair + 1]], axis=1)
+    out_ref[...] = jnp.zeros_like(out_ref)
+    upper = half == 1
+    block = (chunk, across)
+    masks = [jnp.full(block, jnp.where(upper, 3840 << (4 * low), 15 << (4 * low)), jnp.int32) for low in range(2)]
+    middles = [
+        jnp.full(block, jnp.where(upper, 2048.0 * 16**low, 8.0 * 16**low), F32).astype(BF16) for low in range(2)
+    ]
+    shrink = [jnp.where(upper, 0.00390625 / 16**low, 1.0 / 16**low) for low in range(2)]
+    scales_copy.wait()
+    wide[...] = narrow[...].astype(F32)
+
+    def unpack(pair, target):
+        for member in range(2):
+            g = 2 * pair + member
+            fetch(g).wait()
+            for column in range(0, quarter, across):
+                scales = []
+                for low in range(2):
+                    at = pl.multiple_of((2 * half + low) * quarter + column, 128)
+                    row = wide[pl.ds(g, 1), pl.ds(at, across)] * shrink[low]
+                    scales.append(jnp.broadcast_to(row, block).astype(BF16))
+                for r in range(0, depth, chunk):
+                    words = slots[g, r : r + chunk, column : column + across]
+                    for low in range(2):
+                        level = (words & masks[low]).astype(F32).astype(BF16)
+                        target[
+                            member * depth + r : member * depth + r + chunk,
+                            low * quarter + column : low * quarter + column + across,
+                        ] = (level - middles[low]) * scales[low]
+
+    def add(pair, source):
+        x = x_pairs[pair]
+        for c in range(0, out_ref.shape[1], tile):
+            out_ref[:, c : c + tile] += jnp.dot(x, source[:, c : c + tile], preferred_element_type=F32)
+
+    unpack(0, even)
+
+    def step(i, carry):
+        add(2 * i, even)
+        unpack(2 * i + 1, odd)
+        add(2 * i + 1, odd)
+        unpack(2 * i + 2, even)
+        return carry
+
+    lax.fori_loop(0, groups // 4 - 1, step, 0)
+    add(groups // 2 - 2, even)
+    unpack(groups // 2 - 1, odd)
+    add(groups // 2 - 1, odd)
+
+
+def keep(half, code_words, group_scales, returned):
+    rows, quarter = code_words.shape
+    groups = group_scales.shape[0]
+    heads, tokens, width = returned.shape
+    return pl.pallas_call(
+        keep_kernel,
+        in_specs=[
+            pl.BlockSpec(memory_space=pltpu.SMEM),
+            pl.BlockSpec(memory_space=pltpu.HBM),
+            pl.BlockSpec(memory_space=pltpu.HBM),
+            pl.BlockSpec(memory_space=pltpu.VMEM),
+        ],
+        out_specs=pl.BlockSpec(memory_space=pltpu.VMEM),
+        out_shape=jax.ShapeDtypeStruct((tokens, 2 * quarter), F32),
+        scratch_shapes=[
+            pltpu.VMEM((groups, rows // groups, quarter), jnp.int32),
+            pltpu.VMEM(group_scales.shape, group_scales.dtype),
+            pltpu.VMEM(group_scales.shape, F32),
+            pltpu.VMEM((2 * width, 2 * quarter), BF16),
+            pltpu.VMEM((2 * width, 2 * quarter), BF16),
+            pltpu.VMEM((heads // 2, tokens, 2 * width), BF16),
+            pltpu.SemaphoreType.DMA((groups + 1,)),
+        ],
+        compiler_params=pltpu.CompilerParams(vmem_limit_bytes=20 * 1024 * 1024),
+        cost_estimate=pl.CostEstimate(
+            flops=4 * tokens * rows * quarter, bytes_accessed=rows * quarter * 8, transcendentals=0
+        ),
+    )(half, in_hbm(code_words), in_hbm(group_scales), returned)
 
 
 def attend_kernel(first, last, blocks, after, tile, q_ref, *refs):
@@ -307,10 +403,9 @@
     attended = attend(queries, [far_beside], state, True)
     returned = regroup(attended.reshape(queries.shape))
     returned, half = lax.optimization_barrier((returned, half))
-    mine = dequantize(half, code_words, group_scales)
     outgoing = project(returned, theirs, BF16)
     incoming = lax.ppermute(outgoing, "yh", [(0, 1), (1, 0)])
-    kept = project(returned, mine, F32)
+    kept = keep(half, code_words, group_scales, returned)
     return out_gate[None, :] * (kept + incoming.astype(F32) + out_bias[None, :])
 
 

time: 78.2 us -> 77.5 us (level)
    pallas_call x0 -> x1, Pallas kernels: none -> 5.91 us  [keep(): pl.pallas_call(keep_kernel, in_specs=[pl.BlockSpec(memory_space=pltpu.SME...]
    pallas_call x2 -> x1, Pallas kernels: 9.29 us -> 4.65 us  [dequantize(): pl.pallas_call(dequantize_kernel, in_specs=[pl.BlockSpec(memory_space=plt...]
    pallas_call x2 -> x1, Pallas kernels: 3.8 us -> 1.88 us  [project(): pl.pallas_call(functools.partial(project_kernel, tile), in_specs=[pl.Bloc...]
  transfers between devices with their start and end apart: 10 -> 10, of which waited for: 4 -> 4; matrix products, arithmetic and copies ran while one was open for 0% -> 0% of each run, Pallas kernels for 22% -> 21%
where the time goes in v9:
time: 77.5 us; the launch traced here: 77.2 us
  Pallas kernels  21.6 us (28%)
  starting transfers between devices  20.5 us (26%)
  waiting for transfers between devices  15.9 us (21%)
  blocking collectives  14.3 us (18%)
  local copies, waits for them, and re-layouts  4 us (5%)
  other arithmetic  0.85 us (1%)
    all_to_all x1, blocking collectives, regroup(): return lax.all_to_all(a, HEAD_AXES, split_axis=0, concat_axis=0, tiled=True)  14.3 us
    all_to_all x2, starting transfers between devices, regroup(): return lax.all_to_all(a, HEAD_AXES, split_axis=0, concat_axis=0, tiled=True)  13.1 us
    all_to_all x2, waiting for transfers between devices, regroup(): return lax.all_to_all(a, HEAD_AXES, split_axis=0, concat_axis=0, tiled=True)  11.1 us
    pallas_call x4, Pallas kernels, attend(): pl.pallas_call(functools.partial(attend_kernel, first, last, blocks, len(...  6.68 us
    pallas_call x1, Pallas kernels, keep(): pl.pallas_call(keep_kernel, in_specs=[pl.BlockSpec(memory_space=pltpu.SME...  5.91 us
    pallas_call x1, Pallas kernels, dequantize(): pl.pallas_call(dequantize_kernel, in_specs=[pl.BlockSpec(memory_space=plt...  4.65 us
    ppermute x3, waiting for transfers between devices, send(): return lax.ppermute(a, (RING, 'c'), hops)  4.04 us
    unnamed x8, local copies, waits for them, and re-layouts  4 us
  transfers between devices with their start and end apart: 10, of which 4 were waited for; matrix products, arithmetic and copies ran while one was open for 0% of the time, Pallas kernels for 21%

profile of v9, /device:TPU:6, one launch (start us, length us, event | category | flops | bytes accessed | tf_op | source)
XLA Modules:
  0.0 77.2 jit_solution(12139870620950248934)
XLA Ops:
  0.0 2.4 %shard_map.64 = (bf16[16,48,128]{2,1,0:T(8,128)(2,1)}, bf16[16,2,48,128]{3,2,1,0:T(8,128)(2,1)}) custom-call(s32[3,48]{1,0:T(4,128)} %pos_hbm.1, bf16[48,3,16,128]{3,2,1,0:T(8,128)(2,1)} %x_hbm.1), custom_call_target="tpu_custom_call" | custom-call | tf_op jit(solution)/shard_map/pallas_call | solution.py:67
  2.4 9.6 %all-to-all-start = ((bf16[16,2,48,128]{3,2,1,0:T(8,128)(2,1)}), bf16[16,2,48,128]{3,2,1,0:T(8,128)(2,1)S(1)}, u32[]{:S(2)}, u32[]{:S(2)}) async-start(bf16[16,2,48,128]{3,2,1,0:T(8,128)(2,1)} %get-tuple-element.28), calls=%async_computation | async-start | bytes 786432 | tf_op jit(solution)/shard_map/all_to_all | solution.py:377
  12.0 4.6 %shard_map.65.w_ref = bf16[2048,2560]{1,0:T(8,128)(2,1)S(1)} custom-call(s32[1]{0:T(128)S(6)} %sub.3.half_ref, s32[2048,1280]{1,0:T(8,128)} %words_ref.3, bf16[16,5120]{1,0:T(8,128)(2,1)} %scales_ref.3), custom_call_target="tpu_custom_call" | custom-call | flops 39321600 | bytes 20971520 | tf_op jit(solution)/shard_map/pallas_call | solution.py:148
  16.7 0.0 copy-start
  16.7 4.0 %copy-done = bf16[2048,2560]{1,0:T(8,128)(2,1)} copy-done((bf16[2048,2560]{1,0:T(8,128)(2,1)}, bf16[2048,2560]{1,0:T(8,128)(2,1)S(1)}, u32[]{:S(2)}) %copy-start) | copy-done | bytes 10485784
  20.7 5.8 %all-to-all-done.refs_0_ = bf16[16,2,48,128]{3,2,1,0:T(8,128)(2,1)S(1)} async-done(((bf16[16,2,48,128]{3,2,1,0:T(8,128)(2,1)}), bf16[16,2,48,128]{3,2,1,0:T(8,128)(2,1)S(1)}, u32[]{:S(2)}, u32[]{:S(2)}) %all-to-all-start) | async-done | bytes 393248 | tf_op jit(solution)/shard_map/all_to_all | solution.py:377
  26.5 0.8 %collective-permute-start.1 = (bf16[16,2,48,128]{3,2,1,0:T(8,128)(2,1)S(1)}, bf16[16,2,48,128]{3,2,1,0:T(8,128)(2,1)S(1)}, u32[]{:S(2)}, u32[]{:S(2)}) collective-permute-start(bf16[16,2,48,128]{3,2,1,0:T(8,128)(2,1)S(1)} %all-to-all-done.refs_0_), channel_id=1, source_target_pairs={{0,192},{2,66},{64,0},{66,130},{128,64},{130,194},{192,128},{194,2... | collective-permute-start | bytes 1179656 | tf_op jit(solution)/shard_map/ppermute | solution.py:387
  27.4 2.4 %collective-permute-start = (bf16[16,2,48,128]{3,2,1,0:T(8,128)(2,1)S(1)}, bf16[16,2,48,128]{3,2,1,0:T(8,128)(2,1)S(1)}, u32[]{:S(2)}, u32[]{:S(2)}) collective-permute-start(bf16[16,2,48,128]{3,2,1,0:T(8,128)(2,1)S(1)} %all-to-all-done.refs_0_), channel_id=1, source_target_pairs={{0,64},{2,194},{64,128},{66,2},{128,192},{130,66},{192,0},{194,130... | collective-permute-start | bytes 1179656 | tf_op jit(solution)/shard_map/ppermute | solution.py:387
  29.8 3.5 %all-to-all-start.1 = ((bf16[16,48,128]{2,1,0:T(8,128)(2,1)}), bf16[16,48,128]{2,1,0:T(8,128)(2,1)S(1)}, u32[]{:S(2)}, u32[]{:S(2)}) async-start(bf16[16,48,128]{2,1,0:T(8,128)(2,1)} %get-tuple-element.30), calls=%async_computation.1 | async-start | bytes 393216 | tf_op jit(solution)/shard_map/all_to_all | solution.py:377
  33.3 4.0 %collective-permute-done.1.refs_2_ = bf16[16,2,48,128]{3,2,1,0:T(8,128)(2,1)S(1)} collective-permute-done((bf16[16,2,48,128]{3,2,1,0:T(8,128)(2,1)S(1)}, bf16[16,2,48,128]{3,2,1,0:T(8,128)(2,1)S(1)}, u32[]{:S(2)}, u32[]{:S(2)}) %collective-permute-start.1) | collective-permute-done | bytes 393248 | tf_op jit(solution)/shard_map/ppermute | solution.py:387
  37.3 0.0 collective-permute-done.refs_1_
  37.3 0.0 collective-permute-start.3
  37.3 0.5 collective-permute-start.4
  37.8 0.0 collective-permute-start.5
  37.8 0.3 collective-permute-start.2
  38.2 5.3 %all-to-all-done.1.q_ref = bf16[16,48,128]{2,1,0:T(8,128)(2,1)S(1)} async-done(((bf16[16,48,128]{2,1,0:T(8,128)(2,1)}), bf16[16,48,128]{2,1,0:T(8,128)(2,1)S(1)}, u32[]{:S(2)}, u32[]{:S(2)}) %all-to-all-start.1) | async-done | bytes 196640 | tf_op jit(solution)/shard_map/all_to_all | solution.py:377
  43.5 0.0 copy-start.1
  43.5 2.3 %shard_map.66 = (f32[768,128]{1,0:T(8,128)S(1)}, f32[768,128]{1,0:T(8,128)S(1)}, f32[768,128]{1,0:T(8,128)S(1)}) custom-call(bf16[16,48,128]{2,1,0:T(8,128)(2,1)S(1)} %all-to-all-done.1.q_ref, bf16[16,2,48,128]{3,2,1,0:T(8,128)(2,1)S(1)} %all-to-all-done.refs_0_, bf16[16,2,48,128]{3,2,1,0:T(8,128)(2,1)S(1)} %collective-permute-done.refs_1_, ...), custom_call_target="tpu_custom_call" | custom-call | flops 905969664 | bytes 2555904 | tf_op jit(solution)/shard_map/pallas_call | solution.py:335
  45.8 0.0 collective-permute-done.3.refs_0_
  45.8 0.0 collective-permute-done.4.refs_1_
  45.8 0.0 collective-permute-done.5.refs_2_
  45.8 2.4 %shard_map.67 = (f32[768,128]{1,0:T(8,128)S(1)}, f32[768,128]{1,0:T(8,128)S(1)}, f32[768,128]{1,0:T(8,128)S(1)}) custom-call(bf16[16,48,128]{2,1,0:T(8,128)(2,1)S(1)} %all-to-all-done.1.q_ref, bf16[16,2,48,128]{3,2,1,0:T(8,128)(2,1)S(1)} %collective-permute-done.3.refs_0_, bf16[16,2,48,128]{3,2,1,0:T(8,128)(2,1)S(1)} %collective-permute-done.4.refs_1_, ...), custom_call_target="tpu_custom_call" | custom-call | flops 905969664 | bytes 2555904 | tf_op jit(solution)/shard_map/pallas_call | solution.py:335
  48.2 0.0 collective-permute-done.2.refs_0_
  48.2 0.3 collective-permute-start.6
  48.5 1.0 %shard_map.68 = (f32[768,128]{1,0:T(8,128)S(1)}, f32[768,128]{1,0:T(8,128)S(1)}, f32[768,128]{1,0:T(8,128)S(1)}) custom-call(bf16[16,48,128]{2,1,0:T(8,128)(2,1)S(1)} %all-to-all-done.1.q_ref, bf16[16,2,48,128]{3,2,1,0:T(8,128)(2,1)S(1)} %collective-permute-done.2.refs_0_, f32[768,128]{1,0:T(8,128)S(1)} %get-tuple-element.42.refs_1_, ...), custom_call_target="tpu_custom_call" | custom-call | flops 301989888 | bytes 1769472 | tf_op jit(solution)/shard_map/pallas_call | solution.py:335
  49.5 0.7 collective-permute-done.6.refs_0_
  50.2 1.0 %shard_map.69 = bf16[768,128]{1,0:T(8,128)(2,1)S(1)} custom-call(bf16[16,48,128]{2,1,0:T(8,128)(2,1)S(1)} %all-to-all-done.1.q_ref, bf16[16,2,48,128]{3,2,1,0:T(8,128)(2,1)S(1)} %collective-permute-done.6.refs_0_, f32[768,128]{1,0:T(8,128)S(1)} %get-tuple-element.45.refs_1_, f32[768,128]{1,0:T(8,128)S(1)} %get-tuple-element.46.refs_2_, ...), custom_call_target="tpu_custom_call" | custom-call | flops 301989888 | bytes 1769472 | tf_op jit(solution)/shard_map/pallas_call | solution.py:335
  51.2 14.3 %all_to_all.15.x_ref = bf16[16,48,128]{2,1,0:T(8,128)(2,1)S(1)} all-to-all(bf16[16,48,128]{2,1,0:T(8,128)(2,1)S(1)} %bitcast.2), channel_id=1, replica_groups=mesh['x'=4,'zh'=4,'zl'=2,'yl'=2,'c'=2,'yh'=2] {'zh','zl','yl'}, dimensions={0} | all-to-all | bytes 393216 | tf_op jit(solution)/shard_map/all_to_all | solution.py:377
  65.5 0.0 copy-done.1
  65.5 0.0 copy-start.2
  65.5 0.0 copy-start.3
  65.5 1.9 %shard_map.71 = bf16[48,2560]{1,0:T(8,128)(2,1)S(1)} custom-call(bf16[16,48,128]{2,1,0:T(8,128)(2,1)S(1)} %all_to_all.15.x_ref, bf16[2048,2560]{1,0:T(8,128)(2,1)S(1)} %copy-done.1), custom_call_target="tpu_custom_call" | custom-call | flops 503316480 | bytes 10485760 | tf_op jit(solution)/shard_map/pallas_call | solution.py:355
  67.4 3.0 %collective-permute-start.7 = (bf16[48,2560]{1,0:T(8,128)(2,1)S(1)}, bf16[48,2560]{1,0:T(8,128)(2,1)S(1)}, u32[]{:S(2)}, u32[]{:S(2)}) collective-permute-start(bf16[48,2560]{1,0:T(8,128)(2,1)S(1)} %shard_map.71), channel_id=1, source_target_pairs={{0,1},{1,0},{2,3},{3,2},{4,5},{5,4},{6,7},{7,6},{8,9},{9,8},{10,11... | collective-permute-start | bytes 737288 | tf_op jit(solution)/shard_map/ppermute | solution.py:407
  70.4 5.9 %shard_map.70 = f32[48,2560]{1,0:T(8,128)S(1)} custom-call(s32[1]{0:T(128)} %bitcast.half_ref, s32[2048,1280]{1,0:T(8,128)} %words_ref.3, bf16[16,5120]{1,0:T(8,128)(2,1)} %scales_ref.3, bf16[16,48,128]{2,1,0:T(8,128)(2,1)S(1)} %all_to_all.15.x_ref), custom_call_target="tpu_custom_call" | custom-call | flops 503316480 | bytes 20971520 | tf_op jit(solution)/shard_map/pallas_call | solution.py:238
  76.3 0.0 collective-permute-done.7
  76.3 0.0 copy-done.2
  76.4 0.0 copy-done.3
  76.4 0.9 %add_multiply_fusion = f32[48,2560]{1,0:T(8,128)} fusion(f32[48,2560]{1,0:T(8,128)S(1)} %shard_map.70, bf16[48,2560]{1,0:T(8,128)(2,1)S(1)} %collective-permute-done.7, f32[2560]{0:T(1024)S(1)} %copy-done.2, f32[2560]{0:T(1024)S(1)} %copy-done.3), kind=kLoop, calls=%fused_computation | loop fusion | flops 491520 | bytes 1249280 | tf_op jit(solution)/shard_map/mul | solution.py:409
Async XLA Ops:
  2.4 24.1 %all-to-all-start = ((bf16[16,2,48,128]{3,2,1,0:T(8,128)(2,1)}), bf16[16,2,48,128]{3,2,1,0:T(8,128)(2,1)S(1)}, u32[]{:S(2)}, u32[]{:S(2)}) async-start(bf16[16,2,48,128]{3,2,1,0:T(8,128)(2,1)} %get-tuple-element.28), calls=%async_computation | async-start | bytes 786432 | tf_op jit(solution)/shard_map/all_to_all | solution.py:377
  16.7 4.0 %copy-start = (bf16[2048,2560]{1,0:T(8,128)(2,1)}, bf16[2048,2560]{1,0:T(8,128)(2,1)S(1)}, u32[]{:S(2)}) copy-start(bf16[2048,2560]{1,0:T(8,128)(2,1)S(1)} %shard_map.65.w_ref) | copy-start | bytes 31457284
  26.5 10.8 %collective-permute-start.1 = (bf16[16,2,48,128]{3,2,1,0:T(8,128)(2,1)S(1)}, bf16[16,2,48,128]{3,2,1,0:T(8,128)(2,1)S(1)}, u32[]{:S(2)}, u32[]{:S(2)}) collective-permute-start(bf16[16,2,48,128]{3,2,1,0:T(8,128)(2,1)S(1)} %all-to-all-done.refs_0_), channel_id=1, source_target_pairs={{0,192},{2,66},{64,0},{66,130},{128,64},{130,194},{192,128},{194,2... | collective-permute-start | bytes 1179656 | tf_op jit(solution)/shard_map/ppermute | solution.py:387
  27.4 10.0 %collective-permute-start = (bf16[16,2,48,128]{3,2,1,0:T(8,128)(2,1)S(1)}, bf16[16,2,48,128]{3,2,1,0:T(8,128)(2,1)S(1)}, u32[]{:S(2)}, u32[]{:S(2)}) collective-permute-start(bf16[16,2,48,128]{3,2,1,0:T(8,128)(2,1)S(1)} %all-to-all-done.refs_0_), channel_id=1, source_target_pairs={{0,64},{2,194},{64,128},{66,2},{128,192},{130,66},{192,0},{194,130... | collective-permute-start | bytes 1179656 | tf_op jit(solution)/shard_map/ppermute | solution.py:387
  29.8 13.7 %all-to-all-start.1 = ((bf16[16,48,128]{2,1,0:T(8,128)(2,1)}), bf16[16,48,128]{2,1,0:T(8,128)(2,1)S(1)}, u32[]{:S(2)}, u32[]{:S(2)}) async-start(bf16[16,48,128]{2,1,0:T(8,128)(2,1)} %get-tuple-element.30), calls=%async_computation.1 | async-start | bytes 393216 | tf_op jit(solution)/shard_map/all_to_all | solution.py:377
  37.3 8.5 %collective-permute-start.3 = (bf16[16,2,48,128]{3,2,1,0:T(8,128)(2,1)S(1)}, bf16[16,2,48,128]{3,2,1,0:T(8,128)(2,1)S(1)}, u32[]{:S(2)}, u32[]{:S(2)}) collective-permute-start(bf16[16,2,48,128]{3,2,1,0:T(8,128)(2,1)S(1)} %all-to-all-done.refs_0_), channel_id=1, source_target_pairs={{0,2},{2,0},{1,3},{3,1},{4,6},{6,4},{5,7},{7,5},{8,10},{10,8},{9,1... | collective-permute-start | bytes 1179656 | tf_op jit(solution)/shard_map/ppermute | solution.py:380
  37.3 8.5 %collective-permute-start.4 = (bf16[16,2,48,128]{3,2,1,0:T(8,128)(2,1)S(1)}, bf16[16,2,48,128]{3,2,1,0:T(8,128)(2,1)S(1)}, u32[]{:S(2)}, u32[]{:S(2)}) collective-permute-start(bf16[16,2,48,128]{3,2,1,0:T(8,128)(2,1)S(1)} %collective-permute-done.refs_1_), channel_id=1, source_target_pairs={{0,2},{2,0},{1,3},{3,1},{4,6},{6,4},{5,7},{7,5},{8,10},{10,8},{9,1... | collective-permute-start | bytes 1179656 | tf_op jit(solution)/shard_map/ppermute | solution.py:380
  37.8 8.0 %collective-permute-start.5 = (bf16[16,2,48,128]{3,2,1,0:T(8,128)(2,1)S(1)}, bf16[16,2,48,128]{3,2,1,0:T(8,128)(2,1)S(1)}, u32[]{:S(2)}, u32[]{:S(2)}) collective-permute-start(bf16[16,2,48,128]{3,2,1,0:T(8,128)(2,1)S(1)} %collective-permute-done.1.refs_2_), channel_id=1, source_target_pairs={{0,2},{2,0},{1,3},{3,1},{4,6},{6,4},{5,7},{7,5},{8,10},{10,8},{9,1... | collective-permute-start | bytes 1179656 | tf_op jit(solution)/shard_map/ppermute | solution.py:380
  37.8 10.3 %collective-permute-start.2 = (bf16[16,2,48,128]{3,2,1,0:T(8,128)(2,1)S(1)}, bf16[16,2,48,128]{3,2,1,0:T(8,128)(2,1)S(1)}, u32[]{:S(2)}, u32[]{:S(2)}) collective-permute-start(bf16[16,2,48,128]{3,2,1,0:T(8,128)(2,1)S(1)} %collective-permute-done.1.refs_2_), channel_id=1, source_target_pairs={{0,192},{2,66},{64,0},{66,130},{128,64},{130,194},{192,128},{194,2... | collective-permute-start | bytes 1179656 | tf_op jit(solution)/shard_map/ppermute | solution.py:387
  43.5 22.0 %copy-start.1 = (bf16[2048,2560]{1,0:T(8,128)(2,1)S(1)}, bf16[2048,2560]{1,0:T(8,128)(2,1)}, u32[]{:S(2)}) copy-start(bf16[2048,2560]{1,0:T(8,128)(2,1)} %copy-done) | copy-start | bytes 31457284
  48.2 2.0 %collective-permute-start.6 = (bf16[16,2,48,128]{3,2,1,0:T(8,128)(2,1)S(1)}, bf16[16,2,48,128]{3,2,1,0:T(8,128)(2,1)S(1)}, u32[]{:S(2)}, u32[]{:S(2)}) collective-permute-start(bf16[16,2,48,128]{3,2,1,0:T(8,128)(2,1)S(1)} %collective-permute-done.2.refs_0_), channel_id=1, source_target_pairs={{0,2},{2,0},{1,3},{3,1},{4,6},{6,4},{5,7},{7,5},{8,10},{10,8},{9,1... | collective-permute-start | bytes 1179656 | tf_op jit(solution)/shard_map/ppermute | solution.py:380
  65.5 10.8 %copy-start.2 = (f32[2560]{0:T(1024)S(1)}, f32[2560]{0:T(1024)}, u32[]{:S(2)}) copy-start(f32[2560]{0:T(1024)} %param.11) | copy-start | bytes 30724
  65.5 10.8 %copy-start.3 = (f32[2560]{0:T(1024)S(1)}, f32[2560]{0:T(1024)}, u32[]{:S(2)}) copy-start(f32[2560]{0:T(1024)} %param.10) | copy-start | bytes 30724
  67.4 8.9 %collective-permute-start.7 = (bf16[48,2560]{1,0:T(8,128)(2,1)S(1)}, bf16[48,2560]{1,0:T(8,128)(2,1)S(1)}, u32[]{:S(2)}, u32[]{:S(2)}) collective-permute-start(bf16[48,2560]{1,0:T(8,128)(2,1)S(1)} %shard_map.71), channel_id=1, source_target_pairs={{0,1},{1,0},{2,3},{3,2},{4,5},{5,4},{6,7},{7,6},{8,9},{9,8},{10,11... | collective-permute-start | bytes 737288 | tf_op jit(solution)/shard_map/ppermute | solution.py:407

commit v10 on v9

--- a/solution.py
+++ b/solution.py
@@ -165,7 +165,7 @@
     )(half, in_hbm(code_words), in_hbm(group_scales))
 
 
-def keep_kernel(half_ref, words_ref, scales_ref, x_ref, out_ref, slots, narrow, wide, even, odd, x_pairs, sems):
+def keep_kernel(half_ref, words_ref, scales_ref, x_ref, gate_ref, bias_ref, out_ref, slots, narrow, wide, even, odd, x_pairs, sems):
     rows, quarter = words_ref.shape
     groups, depth = scales_ref.shape[0], rows // scales_ref.shape[0]
     half = half_ref[0]
@@ -229,9 +229,10 @@
     add(groups // 2 - 2, even)
     unpack(groups // 2 - 1, odd)
     add(groups // 2 - 1, odd)
-
-
-def keep(half, code_words, group_scales, returned):
+    out_ref[...] = gate_ref[...] * (out_ref[...] + bias_ref[...])
+
+
+def keep(half, code_words, group_scales, returned, out_gate, out_bias):
     rows, quarter = code_words.shape
     groups = group_scales.shape[0]
     heads, tokens, width = returned.shape
@@ -242,6 +243,8 @@
             pl.BlockSpec(memory_space=pltpu.HBM),
             pl.BlockSpec(memory_space=pltpu.HBM),
             pl.BlockSpec(memory_space=pltpu.VMEM),
+            pl.BlockSpec(memory_space=pltpu.VMEM),
+            pl.BlockSpec(memory_space=pltpu.VMEM),
         ],
         out_specs=pl.BlockSpec(memory_space=pltpu.VMEM),
         out_shape=jax.ShapeDtypeStruct((tokens, 2 * quarter), F32),
@@ -258,7 +261,7 @@
         cost_estimate=pl.CostEstimate(
             flops=4 * tokens * rows * quarter, bytes_accessed=rows * quarter * 8, transcendentals=0
         ),
-    )(half, in_hbm(code_words), in_hbm(group_scales), returned)
+    )(half, in_hbm(code_words), in_hbm(group_scales), returned, out_gate[None, :], out_bias[None, :])
 
 
 def attend_kernel(first, last, blocks, after, tile, q_ref, *refs):
@@ -405,8 +408,8 @@
     returned, half = lax.optimization_barrier((returned, half))
     outgoing = project(returned, theirs, BF16)
     incoming = lax.ppermute(outgoing, "yh", [(0, 1), (1, 0)])
-    kept = keep(half, code_words, group_scales, returned)
-    return out_gate[None, :] * (kept + incoming.astype(F32) + out_bias[None, :])
+    kept = keep(half, code_words, group_scales, returned, out_gate, out_bias)
+    return kept + out_gate[None, :] * incoming.astype(F32)
 
 
 def solution(mesh):

time: 77.5 us -> 76.9 us (level)
  starting transfers between devices: 20.5 us -> 18.9 us
  waiting for transfers between devices: 15.9 us -> 17 us
    ppermute x3, starting transfers between devices: 3.57 us -> 2.03 us  [send(): return lax.ppermute(a, (RING, 'c'), hops)]
    ppermute x3, waiting for transfers between devices: 4.04 us -> 5.02 us  [send(): return lax.ppermute(a, (RING, 'c'), hops)]
    mul x1 -> x0, other arithmetic: 0.85 us -> none  [body(): return out_gate[None, :] * (kept + incoming.astype(F32) + out_bias[None, :])]
    add x0 -> x1, other arithmetic: none -> 0.83 us  [body(): return kept + out_gate[None, :] * incoming.astype(F32)]
  transfers between devices with their start and end apart: 10 -> 10, of which waited for: 4 -> 5; matrix products, arithmetic and copies ran while one was open for 0% -> 0% of each run, Pallas kernels for 21% -> 21%
where the time goes in v10:
time: 76.9 us; the launch traced here: 76.6 us
  Pallas kernels  21.6 us (28%)
  starting transfers between devices  18.9 us (25%)
  waiting for transfers between devices  17 us (22%)
  blocking collectives  14 us (18%)
  local copies, waits for them, and re-layouts  4.02 us (5%)
  other arithmetic  0.83 us (1%)
    all_to_all x1, blocking collectives, regroup(): return lax.all_to_all(a, HEAD_AXES, split_axis=0, concat_axis=0, tiled=True)  14 us
    all_to_all x2, starting transfers between devices, regroup(): return lax.all_to_all(a, HEAD_AXES, split_axis=0, concat_axis=0, tiled=True)  13.1 us
    all_to_all x2, waiting for transfers between devices, regroup(): return lax.all_to_all(a, HEAD_AXES, split_axis=0, concat_axis=0, tiled=True)  11.3 us
    pallas_call x4, Pallas kernels, attend(): pl.pallas_call(functools.partial(attend_kernel, first, last, blocks, len(...  6.68 us
    pallas_call x1, Pallas kernels, keep(): pl.pallas_call(keep_kernel, in_specs=[pl.BlockSpec(memory_space=pltpu.SME...  5.93 us
    ppermute x3, waiting for transfers between devices, send(): return lax.ppermute(a, (RING, 'c'), hops)  5.02 us
    pallas_call x1, Pallas kernels, dequantize(): pl.pallas_call(dequantize_kernel, in_specs=[pl.BlockSpec(memory_space=plt...  4.65 us
    unnamed x8, local copies, waits for them, and re-layouts  4.01 us
  transfers between devices with their start and end apart: 10, of which 5 were waited for; matrix products, arithmetic and copies ran while one was open for 0% of the time, Pallas kernels for 21%

profile of v10, /device:TPU:6, one launch (start us, length us, event | category | flops | bytes accessed | tf_op | source)
XLA Modules:
  0.0 76.6 jit_solution(16489979733486964099)
XLA Ops:
  0.0 2.4 %shard_map.64 = (bf16[16,48,128]{2,1,0:T(8,128)(2,1)}, bf16[16,2,48,128]{3,2,1,0:T(8,128)(2,1)}) custom-call(s32[3,48]{1,0:T(4,128)} %pos_hbm.1, bf16[48,3,16,128]{3,2,1,0:T(8,128)(2,1)} %x_hbm.1), custom_call_target="tpu_custom_call" | custom-call | tf_op jit(solution)/shard_map/pallas_call | solution.py:67
  2.4 9.6 %all-to-all-start = ((bf16[16,2,48,128]{3,2,1,0:T(8,128)(2,1)}), bf16[16,2,48,128]{3,2,1,0:T(8,128)(2,1)S(1)}, u32[]{:S(2)}, u32[]{:S(2)}) async-start(bf16[16,2,48,128]{3,2,1,0:T(8,128)(2,1)} %get-tuple-element.28), calls=%async_computation | async-start | bytes 786432 | tf_op jit(solution)/shard_map/all_to_all | solution.py:380
  12.0 4.6 %shard_map.65.w_ref = bf16[2048,2560]{1,0:T(8,128)(2,1)S(1)} custom-call(s32[1]{0:T(128)S(6)} %sub.3.half_ref, s32[2048,1280]{1,0:T(8,128)} %words_ref.3, bf16[16,5120]{1,0:T(8,128)(2,1)} %scales_ref.3), custom_call_target="tpu_custom_call" | custom-call | flops 39321600 | bytes 20971520 | tf_op jit(solution)/shard_map/pallas_call | solution.py:148
  16.7 0.0 copy-start
  16.7 4.0 %copy-done = bf16[2048,2560]{1,0:T(8,128)(2,1)} copy-done((bf16[2048,2560]{1,0:T(8,128)(2,1)}, bf16[2048,2560]{1,0:T(8,128)(2,1)S(1)}, u32[]{:S(2)}) %copy-start) | copy-done | bytes 10485784
  20.7 5.8 %all-to-all-done.refs_0_ = bf16[16,2,48,128]{3,2,1,0:T(8,128)(2,1)S(1)} async-done(((bf16[16,2,48,128]{3,2,1,0:T(8,128)(2,1)}), bf16[16,2,48,128]{3,2,1,0:T(8,128)(2,1)S(1)}, u32[]{:S(2)}, u32[]{:S(2)}) %all-to-all-start) | async-done | bytes 393248 | tf_op jit(solution)/shard_map/all_to_all | solution.py:380
  26.5 0.5 collective-permute-start
  27.0 1.5 %collective-permute-start.1 = (bf16[16,2,48,128]{3,2,1,0:T(8,128)(2,1)S(1)}, bf16[16,2,48,128]{3,2,1,0:T(8,128)(2,1)S(1)}, u32[]{:S(2)}, u32[]{:S(2)}) collective-permute-start(bf16[16,2,48,128]{3,2,1,0:T(8,128)(2,1)S(1)} %all-to-all-done.refs_0_), channel_id=1, source_target_pairs={{0,192},{2,66},{64,0},{66,130},{128,64},{130,194},{192,128},{194,2... | collective-permute-start | bytes 1179656 | tf_op jit(solution)/shard_map/ppermute | solution.py:390
  28.6 3.5 %all-to-all-start.1 = ((bf16[16,48,128]{2,1,0:T(8,128)(2,1)}), bf16[16,48,128]{2,1,0:T(8,128)(2,1)S(1)}, u32[]{:S(2)}, u32[]{:S(2)}) async-start(bf16[16,48,128]{2,1,0:T(8,128)(2,1)} %get-tuple-element.30), calls=%async_computation.1 | async-start | bytes 393216 | tf_op jit(solution)/shard_map/all_to_all | solution.py:380
  32.1 0.0 copy-start.2
  32.1 0.0 copy-start.3
  32.1 4.4 %collective-permute-done.refs_1_ = bf16[16,2,48,128]{3,2,1,0:T(8,128)(2,1)S(1)} collective-permute-done((bf16[16,2,48,128]{3,2,1,0:T(8,128)(2,1)S(1)}, bf16[16,2,48,128]{3,2,1,0:T(8,128)(2,1)S(1)}, u32[]{:S(2)}, u32[]{:S(2)}) %collective-permute-start) | collective-permute-done | bytes 393248 | tf_op jit(solution)/shard_map/ppermute | solution.py:390
  36.5 0.7 collective-permute-done.1.refs_2_
  37.1 0.0 collective-permute-start.5
  37.1 0.5 collective-permute-start.3
  37.6 0.0 collective-permute-start.4
  37.6 0.0 collective-permute-start.2
  37.6 5.5 %all-to-all-done.1.q_ref = bf16[16,48,128]{2,1,0:T(8,128)(2,1)S(1)} async-done(((bf16[16,48,128]{2,1,0:T(8,128)(2,1)}), bf16[16,48,128]{2,1,0:T(8,128)(2,1)S(1)}, u32[]{:S(2)}, u32[]{:S(2)}) %all-to-all-start.1) | async-done | bytes 196640 | tf_op jit(solution)/shard_map/all_to_all | solution.py:380
  43.1 0.0 copy-start.1
  43.1 2.3 %shard_map.66 = (f32[768,128]{1,0:T(8,128)S(1)}, f32[768,128]{1,0:T(8,128)S(1)}, f32[768,128]{1,0:T(8,128)S(1)}) custom-call(bf16[16,48,128]{2,1,0:T(8,128)(2,1)S(1)} %all-to-all-done.1.q_ref, bf16[16,2,48,128]{3,2,1,0:T(8,128)(2,1)S(1)} %all-to-all-done.refs_0_, bf16[16,2,48,128]{3,2,1,0:T(8,128)(2,1)S(1)} %collective-permute-done.refs_1_, ...), custom_call_target="tpu_custom_call" | custom-call | flops 905969664 | bytes 2555904 | tf_op jit(solution)/shard_map/pallas_call | solution.py:338
  45.4 0.0 collective-permute-done.5.refs_2_
  45.4 0.0 collective-permute-done.3.refs_0_
  45.4 0.0 collective-permute-done.4.refs_1_
  45.4 2.4 %shard_map.67 = (f32[768,128]{1,0:T(8,128)S(1)}, f32[768,128]{1,0:T(8,128)S(1)}, f32[768,128]{1,0:T(8,128)S(1)}) custom-call(bf16[16,48,128]{2,1,0:T(8,128)(2,1)S(1)} %all-to-all-done.1.q_ref, bf16[16,2,48,128]{3,2,1,0:T(8,128)(2,1)S(1)} %collective-permute-done.3.refs_0_, bf16[16,2,48,128]{3,2,1,0:T(8,128)(2,1)S(1)} %collective-permute-done.4.refs_1_, ...), custom_call_target="tpu_custom_call" | custom-call | flops 905969664 | bytes 2555904 | tf_op jit(solution)/shard_map/pallas_call | solution.py:338
  47.8 0.0 collective-permute-done.2.refs_0_
  47.8 0.3 collective-permute-start.6
  48.1 1.0 %shard_map.68 = (f32[768,128]{1,0:T(8,128)S(1)}, f32[768,128]{1,0:T(8,128)S(1)}, f32[768,128]{1,0:T(8,128)S(1)}) custom-call(bf16[16,48,128]{2,1,0:T(8,128)(2,1)S(1)} %all-to-all-done.1.q_ref, bf16[16,2,48,128]{3,2,1,0:T(8,128)(2,1)S(1)} %collective-permute-done.2.refs_0_, f32[768,128]{1,0:T(8,128)S(1)} %get-tuple-element.42.refs_1_, ...), custom_call_target="tpu_custom_call" | custom-call | flops 301989888 | bytes 1769472 | tf_op jit(solution)/shard_map/pallas_call | solution.py:338
  49.1 0.7 collective-permute-done.6.refs_0_
  49.8 1.0 %shard_map.69 = bf16[768,128]{1,0:T(8,128)(2,1)S(1)} custom-call(bf16[16,48,128]{2,1,0:T(8,128)(2,1)S(1)} %all-to-all-done.1.q_ref, bf16[16,2,48,128]{3,2,1,0:T(8,128)(2,1)S(1)} %collective-permute-done.6.refs_0_, f32[768,128]{1,0:T(8,128)S(1)} %get-tuple-element.45.refs_1_, f32[768,128]{1,0:T(8,128)S(1)} %get-tuple-element.46.refs_2_, ...), custom_call_target="tpu_custom_call" | custom-call | flops 301989888 | bytes 1769472 | tf_op jit(solution)/shard_map/pallas_call | solution.py:338
  50.9 14.0 %all_to_all.15.x_ref = bf16[16,48,128]{2,1,0:T(8,128)(2,1)S(1)} all-to-all(bf16[16,48,128]{2,1,0:T(8,128)(2,1)S(1)} %bitcast.2), channel_id=1, replica_groups=mesh['x'=4,'zh'=4,'zl'=2,'yl'=2,'c'=2,'yh'=2] {'zh','zl','yl'}, dimensions={0} | all-to-all | bytes 393216 | tf_op jit(solution)/shard_map/all_to_all | solution.py:380
  64.9 0.0 copy-done.1
  64.9 1.9 %shard_map.71 = bf16[48,2560]{1,0:T(8,128)(2,1)S(1)} custom-call(bf16[16,48,128]{2,1,0:T(8,128)(2,1)S(1)} %all_to_all.15.x_ref, bf16[2048,2560]{1,0:T(8,128)(2,1)S(1)} %copy-done.1), custom_call_target="tpu_custom_call" | custom-call | flops 503316480 | bytes 10485760 | tf_op jit(solution)/shard_map/pallas_call | solution.py:358
  66.8 3.0 %collective-permute-start.7 = (bf16[48,2560]{1,0:T(8,128)(2,1)S(1)}, bf16[48,2560]{1,0:T(8,128)(2,1)S(1)}, u32[]{:S(2)}, u32[]{:S(2)}) collective-permute-start(bf16[48,2560]{1,0:T(8,128)(2,1)S(1)} %shard_map.71), channel_id=1, source_target_pairs={{0,1},{1,0},{2,3},{3,2},{4,5},{5,4},{6,7},{7,6},{8,9},{9,8},{10,11... | collective-permute-start | bytes 737288 | tf_op jit(solution)/shard_map/ppermute | solution.py:410
  69.8 0.0 copy-done.2
  69.8 0.0 copy-done.3
  69.8 5.9 %shard_map.70 = f32[48,2560]{1,0:T(8,128)S(1)} custom-call(s32[1]{0:T(128)} %bitcast.half_ref, s32[2048,1280]{1,0:T(8,128)} %words_ref.3, bf16[16,5120]{1,0:T(8,128)(2,1)} %scales_ref.3, bf16[16,48,128]{2,1,0:T(8,128)(2,1)S(1)} %all_to_all.15.x_ref, f32[1,2560]{1,0:T(1,128)S(1)} %broadcast_in_dim.7.gate_ref, f32[1,2560]{1,0:T(1,128)S(1)} %broadcast_in_dim.8.bias_ref), custom_call_target="tpu_custom_call" | custom-call | flops 503316480 | bytes 20971520 | tf_op jit(solution)/shard_map/pallas_call | solution.py:239
  75.8 0.0 collective-permute-done.7
  75.8 0.8 %multiply_add_fusion = f32[48,2560]{1,0:T(8,128)} fusion(f32[48,2560]{1,0:T(8,128)S(1)} %shard_map.70, bf16[48,2560]{1,0:T(8,128)(2,1)S(1)} %collective-permute-done.7, f32[2560]{0:T(1024)S(1)} %copy-done.2), kind=kLoop, calls=%fused_computation | loop fusion | flops 368640 | bytes 1239040 | tf_op jit(solution)/shard_map/add | solution.py:412
  (2 shorter events, 0.0 us)
Async XLA Ops:
  2.4 24.1 %all-to-all-start = ((bf16[16,2,48,128]{3,2,1,0:T(8,128)(2,1)}), bf16[16,2,48,128]{3,2,1,0:T(8,128)(2,1)S(1)}, u32[]{:S(2)}, u32[]{:S(2)}) async-start(bf16[16,2,48,128]{3,2,1,0:T(8,128)(2,1)} %get-tuple-element.28), calls=%async_computation | async-start | bytes 786432 | tf_op jit(solution)/shard_map/all_to_all | solution.py:380
  16.7 4.0 %copy-start = (bf16[2048,2560]{1,0:T(8,128)(2,1)}, bf16[2048,2560]{1,0:T(8,128)(2,1)S(1)}, u32[]{:S(2)}) copy-start(bf16[2048,2560]{1,0:T(8,128)(2,1)S(1)} %shard_map.65.w_ref) | copy-start | bytes 31457284
  26.5 9.9 %collective-permute-start = (bf16[16,2,48,128]{3,2,1,0:T(8,128)(2,1)S(1)}, bf16[16,2,48,128]{3,2,1,0:T(8,128)(2,1)S(1)}, u32[]{:S(2)}, u32[]{:S(2)}) collective-permute-start(bf16[16,2,48,128]{3,2,1,0:T(8,128)(2,1)S(1)} %all-to-all-done.refs_0_), channel_id=1, source_target_pairs={{0,64},{2,194},{64,128},{66,2},{128,192},{130,66},{192,0},{194,130... | collective-permute-start | bytes 1179656 | tf_op jit(solution)/shard_map/ppermute | solution.py:390
  27.0 10.1 %collective-permute-start.1 = (bf16[16,2,48,128]{3,2,1,0:T(8,128)(2,1)S(1)}, bf16[16,2,48,128]{3,2,1,0:T(8,128)(2,1)S(1)}, u32[]{:S(2)}, u32[]{:S(2)}) collective-permute-start(bf16[16,2,48,128]{3,2,1,0:T(8,128)(2,1)S(1)} %all-to-all-done.refs_0_), channel_id=1, source_target_pairs={{0,192},{2,66},{64,0},{66,130},{128,64},{130,194},{192,128},{194,2... | collective-permute-start | bytes 1179656 | tf_op jit(solution)/shard_map/ppermute | solution.py:390
  28.6 14.5 %all-to-all-start.1 = ((bf16[16,48,128]{2,1,0:T(8,128)(2,1)}), bf16[16,48,128]{2,1,0:T(8,128)(2,1)S(1)}, u32[]{:S(2)}, u32[]{:S(2)}) async-start(bf16[16,48,128]{2,1,0:T(8,128)(2,1)} %get-tuple-element.30), calls=%async_computation.1 | async-start | bytes 393216 | tf_op jit(solution)/shard_map/all_to_all | solution.py:380
  32.1 37.7 %copy-start.2 = (f32[2560]{0:T(1024)S(1)}, f32[2560]{0:T(1024)}, u32[]{:S(2)}) copy-start(f32[2560]{0:T(1024)} %param.10) | copy-start | bytes 30724
  32.1 37.7 %copy-start.3 = (f32[2560]{0:T(1024)S(1)}, f32[2560]{0:T(1024)}, u32[]{:S(2)}) copy-start(f32[2560]{0:T(1024)} %param.11) | copy-start | bytes 30724
  37.1 8.3 %collective-permute-start.5 = (bf16[16,2,48,128]{3,2,1,0:T(8,128)(2,1)S(1)}, bf16[16,2,48,128]{3,2,1,0:T(8,128)(2,1)S(1)}, u32[]{:S(2)}, u32[]{:S(2)}) collective-permute-start(bf16[16,2,48,128]{3,2,1,0:T(8,128)(2,1)S(1)} %collective-permute-done.1.refs_2_), channel_id=1, source_target_pairs={{0,2},{2,0},{1,3},{3,1},{4,6},{6,4},{5,7},{7,5},{8,10},{10,8},{9,1... | collective-permute-start | bytes 1179656 | tf_op jit(solution)/shard_map/ppermute | solution.py:383
  37.1 8.3 %collective-permute-start.3 = (bf16[16,2,48,128]{3,2,1,0:T(8,128)(2,1)S(1)}, bf16[16,2,48,128]{3,2,1,0:T(8,128)(2,1)S(1)}, u32[]{:S(2)}, u32[]{:S(2)}) collective-permute-start(bf16[16,2,48,128]{3,2,1,0:T(8,128)(2,1)S(1)} %all-to-all-done.refs_0_), channel_id=1, source_target_pairs={{0,2},{2,0},{1,3},{3,1},{4,6},{6,4},{5,7},{7,5},{8,10},{10,8},{9,1... | collective-permute-start | bytes 1179656 | tf_op jit(solution)/shard_map/ppermute | solution.py:383
  37.6 7.8 %collective-permute-start.4 = (bf16[16,2,48,128]{3,2,1,0:T(8,128)(2,1)S(1)}, bf16[16,2,48,128]{3,2,1,0:T(8,128)(2,1)S(1)}, u32[]{:S(2)}, u32[]{:S(2)}) collective-permute-start(bf16[16,2,48,128]{3,2,1,0:T(8,128)(2,1)S(1)} %collective-permute-done.refs_1_), channel_id=1, source_target_pairs={{0,2},{2,0},{1,3},{3,1},{4,6},{6,4},{5,7},{7,5},{8,10},{10,8},{9,1... | collective-permute-start | bytes 1179656 | tf_op jit(solution)/shard_map/ppermute | solution.py:383
  37.6 10.2 %collective-permute-start.2 = (bf16[16,2,48,128]{3,2,1,0:T(8,128)(2,1)S(1)}, bf16[16,2,48,128]{3,2,1,0:T(8,128)(2,1)S(1)}, u32[]{:S(2)}, u32[]{:S(2)}) collective-permute-start(bf16[16,2,48,128]{3,2,1,0:T(8,128)(2,1)S(1)} %collective-permute-done.1.refs_2_), channel_id=1, source_target_pairs={{0,192},{2,66},{64,0},{66,130},{128,64},{130,194},{192,128},{194,2... | collective-permute-start | bytes 1179656 | tf_op jit(solution)/shard_map/ppermute | solution.py:390
  43.1 21.8 %copy-start.1 = (bf16[2048,2560]{1,0:T(8,128)(2,1)S(1)}, bf16[2048,2560]{1,0:T(8,128)(2,1)}, u32[]{:S(2)}) copy-start(bf16[2048,2560]{1,0:T(8,128)(2,1)} %copy-done) | copy-start | bytes 31457284
  47.8 2.0 %collective-permute-start.6 = (bf16[16,2,48,128]{3,2,1,0:T(8,128)(2,1)S(1)}, bf16[16,2,48,128]{3,2,1,0:T(8,128)(2,1)S(1)}, u32[]{:S(2)}, u32[]{:S(2)}) collective-permute-start(bf16[16,2,48,128]{3,2,1,0:T(8,128)(2,1)S(1)} %collective-permute-done.2.refs_0_), channel_id=1, source_target_pairs={{0,2},{2,0},{1,3},{3,1},{4,6},{6,4},{5,7},{7,5},{8,10},{10,8},{9,1... | collective-permute-start | bytes 1179656 | tf_op jit(solution)/shard_map/ppermute | solution.py:383
  66.8 9.0 %collective-permute-start.7 = (bf16[48,2560]{1,0:T(8,128)(2,1)S(1)}, bf16[48,2560]{1,0:T(8,128)(2,1)S(1)}, u32[]{:S(2)}, u32[]{:S(2)}) collective-permute-start(bf16[48,2560]{1,0:T(8,128)(2,1)S(1)} %shard_map.71), channel_id=1, source_target_pairs={{0,1},{1,0},{2,3},{3,2},{4,5},{5,4},{6,7},{7,6},{8,9},{9,8},{10,11... | collective-permute-start | bytes 737288 | tf_op jit(solution)/shard_map/ppermute | solution.py:410
